TPU v7x, 32 devices: a whole 2x2x4 slice. The times are simulated.
32 devices in a mesh: mem: 8 (over z, core), lat: 4 (over y, x).
Axes of the slice: x: 2, y: 2, z: 4, core: 2. Of those that a mesh axis runs over, the one named last changes fastest.
Arguments:
- equivalents: float32 [384, 24576], P('mem', 'lat'), may hold values from -12 to 12
- innovations: float32 [384, 24576], P('mem', 'lat'), may hold values from -6 to 6
- obs_var: float32 [24576], P('lat'), may hold values from 0.5 to 2
- taper_tiles: bfloat16 [2, 512, 512], replicated, may hold values from 0 to 1
- region_blocks: int32 [4, 8], replicated, may hold values from 1 to 2, 12 in all within a row
- pair_mask: int32 [4, 12], replicated, may hold values 0 or 1
- taper_index: int32 [4, 12, 3], replicated, may hold values from 0 to 1
- eig_low: float32 [1], replicated, may hold values from 0.3 to 0.6
- eig_high: float32 [1], replicated, may hold values from 6 to 10
Outputs:
- solution: float32 [384, 24576], P('mem', 'lat')
Inputs may be any that keep to these rules, and one draw needn't show every extreme that they name: `region_blocks`: in every band the counts sum to 12 and some region holds exactly 2 blocks.
All inputs are finite; a program needn't handle non-finite values.
Results may differ from a plain program's by a relative error of at most 0.0044.
Values may be sent and summed in bfloat16 or wider, within the bound.
No kernel may reach another device: no remote copies, remote signals or barrier semaphores. Data moves between devices by JAX's collectives and lax.ppermute only.
A program may use at most 64 MiB of HBM per device.

v0:
```python
import jax
import jax.numpy as jnp
from jax import lax
from jax.sharding import PartitionSpec as P

M = 384
BLOCK = 512
MAXB = 2
ITERS = 3


def extended(shard, sides, width):
    for axis, dim in sides:
        count, length = (lax.axis_size(axis), shard.shape[dim])
        up = [(i, (i + 1) % count) for i in range(count - 1)]
        down = [(j, i) for i, j in up]
        last = lax.slice_in_dim(shard, length - width, length, axis=dim)
        initial = lax.slice_in_dim(shard, 0, width, axis=dim)
        before = lax.ppermute(last, axis, up)
        after = lax.ppermute(initial, axis, down)
        shard = jnp.concatenate([before, shard, after], axis=dim)
    return shard


def block_prod(left_op, right_op, einsum_form):
    return jnp.einsum(einsum_form, left_op, right_op, preferred_element_type=jnp.float32)


def on_device(
    equivalents,
    innovations,
    obs_var,
    taper_tiles,
    region_blocks,
    pair_mask,
    taper_index,
    eig_low,
    eig_high,
):
    groups = lax.axis_size("mem")
    my_group = lax.axis_index("mem")
    my_band = lax.axis_index("lat")
    group_rows, band_cols = equivalents.shape
    band_count = band_cols // BLOCK
    inv_scale = (M - 1) ** (-0.5)
    starts_all = jnp.cumsum(region_blocks, axis=1) - region_blocks
    counts_band = lax.dynamic_index_in_dim(region_blocks, my_band, 0, keepdims=False)
    starts_band = lax.dynamic_index_in_dim(starts_all, my_band, 0, keepdims=False)
    slot_offsets = jnp.arange(MAXB, dtype=jnp.int32)
    slot_blocks = starts_band[:, None] + slot_offsets[None, :]
    slot_valid = (slot_offsets[None, :] < counts_band[:, None]).astype(jnp.float32)

    def pack_regions(values):
        blocks = jnp.swapaxes(values.reshape(group_rows, band_count, BLOCK), 0, 1)
        padded = jnp.concatenate(
            [blocks, jnp.zeros((MAXB, group_rows, BLOCK), values.dtype)], axis=0
        )
        picked = padded[slot_blocks] * slot_valid[:, :, None, None]
        return picked.reshape(groups * MAXB, group_rows, BLOCK)

    rhs_packed = pack_regions(innovations)
    raw_region, rhs_region = (
        lax.all_to_all(pack_regions(equivalents), "mem", split_axis=0, concat_axis=1, tiled=True),
        lax.all_to_all(rhs_packed, "mem", split_axis=0, concat_axis=1, tiled=True),
    )
    mean_rows = jnp.mean(raw_region, axis=1, keepdims=True)
    perturb = ((raw_region - mean_rows) * inv_scale).astype(jnp.bfloat16)
    region_start = starts_band[my_group]
    region_count = counts_band[my_group]
    own_valid = (slot_offsets < region_count).astype(jnp.float32)
    own_blocks = jnp.minimum(region_start + slot_offsets, band_count - 1)
    var_blocks = jnp.concatenate(
        [obs_var.reshape(band_count, BLOCK), jnp.zeros((MAXB, BLOCK), jnp.float32)], axis=0
    )
    variance = var_blocks[region_start + slot_offsets] * own_valid[:, None]
    index_band = lax.dynamic_index_in_dim(taper_index, my_band, 0, keepdims=False)
    mask_band = lax.dynamic_index_in_dim(pair_mask, my_band, 0, keepdims=False)
    taper_table = taper_tiles.astype(jnp.float32)
    own_index = index_band[own_blocks]
    tile_self = taper_table[own_index[:, 0]]
    tile_self = 0.5 * (tile_self + jnp.swapaxes(tile_self, 1, 2))
    cov_self = (tile_self * block_prod(perturb, perturb, "jmi,jmk->jik")).astype(jnp.bfloat16)
    east_active = (
        (slot_offsets[:-1] + 1 < region_count) & (mask_band[own_blocks[:-1]] == 1)
    ).astype(jnp.float32)
    tile_east = taper_table[own_index[:-1, 1]]
    cov_east = (
        tile_east
        * block_prod(perturb[:-1], perturb[1:], "jmi,jmk->jik")
        * east_active[:, None, None]
    ).astype(jnp.bfloat16)
    tile_north = taper_table[index_band[region_start, 2]]
    own_first = perturb[0]
    edge_rows = extended(perturb[0:1], (("lat", 0),), 1)
    cov_north = (tile_north * block_prod(own_first, edge_rows[2], "mi,mk->ik")).astype(jnp.bfloat16)
    lower_band = jnp.maximum(my_band - 1, 0)
    lower_start = starts_all[lower_band, my_group]
    tile_south = taper_table[taper_index[lower_band, lower_start, 2]]
    cov_south = (tile_south.T * block_prod(own_first, edge_rows[0], "mi,mk->ik")).astype(
        jnp.bfloat16
    )
    low_bound = eig_low[0]
    high_bound = eig_high[0]
    centre = 0.5 * (high_bound + low_bound)
    half_width = 0.5 * (high_bound - low_bound)
    ratio_scale = centre / half_width
    ratio_prev = 1.0 / ratio_scale
    residual = rhs_region
    solution = jnp.zeros_like(residual)
    direction = residual / centre
    for iteration in range(ITERS):
        solution = solution + direction
        if iteration + 1 < ITERS:
            dir_bf = direction.astype(jnp.bfloat16)
            edge_dirs = extended(dir_bf[0:1], (("lat", 0),), 1)
            result = variance[:, None, :] * direction + block_prod(cov_self, dir_bf, "jik,jmk->jmi")
            east_term = block_prod(cov_east, dir_bf[1:], "jik,jmk->jmi")
            west_term = block_prod(cov_east, dir_bf[:-1], "jki,jmk->jmi")
            zero_block = jnp.zeros((1, M, BLOCK), jnp.float32)
            edge_term = block_prod(cov_north, edge_dirs[2], "ik,mk->mi") + block_prod(
                cov_south, edge_dirs[0], "ik,mk->mi"
            )
            result = (
                result
                + jnp.concatenate([east_term, zero_block], axis=0)
                + jnp.concatenate([zero_block, west_term], axis=0)
            )
            residual = residual - (
                result
                + jnp.concatenate(
                    [edge_term[None], jnp.zeros((MAXB - 1, M, BLOCK), jnp.float32)], axis=0
                )
            )
            ratio_next = 1.0 / (2.0 * ratio_scale - ratio_prev)
            direction = (
                ratio_next * ratio_prev * direction + 2.0 * ratio_next / half_width * residual
            )
            ratio_prev = ratio_next
    returned = lax.all_to_all(solution, "mem", split_axis=1, concat_axis=0, tiled=True)
    block_ids = jnp.arange(band_count, dtype=jnp.int32)
    owners = jnp.sum((starts_band[None, :] <= block_ids[:, None]).astype(jnp.int32), axis=1) - 1
    source_slots = owners * MAXB + block_ids - starts_band[owners]
    picked = returned[source_slots]
    return jnp.swapaxes(picked, 0, 1).reshape(group_rows, band_cols)


def solution(mesh):
    return jax.shard_map(
        on_device,
        mesh=mesh,
        in_specs=(P("mem", "lat"), P("mem", "lat"), P("lat"), P(), P(), P(), P(), P(), P()),
        out_specs=P("mem", "lat"),
        check_vma=False,
    )
```

profile of v0, /device:TPU:0, one launch (start us, length us, event | category | flops | bytes accessed | tf_op | source)
XLA Modules:
  0.0 204.2 jit_solution(3621518125521709635)
XLA Ops:
  0.0 1.0 reduce_window_sum.11
  1.0 0.7 sub.45
  1.6 0.7 fusion.30
  2.6 1.4 copy.67
  4.2 0.2 concatenate.29
  4.5 1.8 gather_fusion.4
  6.3 1.9 gather_fusion
  8.2 3.1 %broadcast_multiply_fusion = (f32[16,48,512]{2,1,0:T(8,128)S(1)}, f32[16,48,512]{2,1,0:T(8,128)}) fusion(f32[16,48,512]{2,1,0:T(8,128)S(1)} %copy-done.3, f32[16]{0:T(128)S(1)} %reshape.292, f32[16,48,512]{2,1,0:T(8,128)} %gather_fusion), kind=kLoop, calls=%fused_computation.37 | loop fusion | flops 786432 | bytes 6291520 | tf_op jit(solution)/shard_map/mul | solution.py:58
  11.3 44.0 %all_to_all.54 = f32[16,48,512]{2,1,0:T(8,128)} all-to-all(f32[16,48,512]{2,1,0:T(8,128)S(1)} %get-tuple-element.33), channel_id=1, replica_groups=mesh['mem'=8,'lat'=4] {'mem'}, dimensions={0} | all-to-all | bytes 3145728 | tf_op jit(solution)/shard_map/all_to_all | solution.py:63
  55.4 4.4 %all-to-all-start = ((f32[16,48,512]{2,1,0:T(8,128)}), f32[16,48,512]{2,1,0:T(8,128)}, u32[]{:S(2)}, u32[]{:S(2)}) async-start(f32[16,48,512]{2,1,0:T(8,128)} %get-tuple-element.34), calls=%async_computation | async-start | bytes 3145728 | tf_op jit(solution)/shard_map/all_to_all | solution.py:64
  61.3 1.3 dynamic_slice.41
  62.5 0.6 fusion.42
  66.8 1.4 constant_dynamic-slice_fusion.5
  70.7 0.7 add_minimum_fusion
  72.1 1.3 dynamic-slice.10
  74.0 0.7 constant_dynamic-slice_fusion.1
  74.8 0.8 fusion.27
  75.6 0.6 gather_fusion.2
  76.1 0.7 slice.36
  78.2 0.3 convert_element_type.50
  79.3 2.0 gather_fusion.3
  81.4 1.3 copy.54
  82.7 2.9 %copy.50 = f32[2,512,512]{1,2,0:T(8,128)} copy(f32[2,512,512]{2,1,0:T(8,128)} %gather_fusion.3) | data formatting | bytes 4194304 | tf_op jit(solution)/shard_map/gather | solution.py:80
  86.9 0.6 gather_fusion.1
  87.5 0.6 compare_convert_fusion
  88.1 1.7 copy.52
  89.9 0.2 copy-done.1
  90.1 0.2 fusion.4
  90.4 0.8 slice.73
  91.1 1.3 collective-permute-start.1
  92.4 5.3 %collective-permute-start.3 = (bf16[1,384,512]{2,1,0:T(8,128)(2,1)}, bf16[1,384,512]{2,1,0:T(8,128)(2,1)}, u32[]{:S(2)}, u32[]{:S(2)}) collective-permute-start(bf16[1,384,512]{2,1,0:T(8,128)(2,1)} %slice.73), channel_id=1, source_target_pairs={{0,1},{1,2},{2,3},{4,5},{5,6},{6,7},{8,9},{9,10},{10,11},{12,13},{... | collective-permute-start | bytes 1179656 | tf_op jit(solution)/shard_map/ppermute | solution.py:19
  97.8 1.6 copy.48
  99.4 0.2 fusion.41
  99.6 1.6 collective-permute-start
  101.1 4.6 %collective-permute-start.2 = (bf16[1,384,512]{2,1,0:T(8,128)(2,1)S(1)}, bf16[1,384,512]{2,1,0:T(8,128)(2,1)S(1)}, u32[]{:S(2)}, u32[]{:S(2)}) collective-permute-start(bf16[1,384,512]{2,1,0:T(8,128)(2,1)S(1)} %slice.75), channel_id=1, source_target_pairs={{0,1},{1,2},{2,3},{4,5},{5,6},{6,7},{8,9},{9,10},{10,11},{12,13},{... | collective-permute-start | bytes 1179656 | tf_op jit(solution)/shard_map/ppermute | solution.py:19
  105.7 0.9 fusion.2
  106.6 0.5 fusion.7
  107.1 0.4 convolution_bitcast_fusion.3
  107.5 0.4 convolution_bitcast_fusion.2
  107.9 0.4 copy-done.12
  108.3 1.5 fusion.11
  109.8 1.7 fusion.10
  111.5 2.8 %collective-permute-done.2 = bf16[1,384,512]{2,1,0:T(8,128)(2,1)S(1)} collective-permute-done((bf16[1,384,512]{2,1,0:T(8,128)(2,1)S(1)}, bf16[1,384,512]{2,1,0:T(8,128)(2,1)S(1)}, u32[]{:S(2)}, u32[]{:S(2)}) %collective-permute-start.2) | collective-permute-done | bytes 393248 | tf_op jit(solution)/shard_map/ppermute | solution.py:19
  114.2 0.4 fusion.17
  114.7 7.4 %collective-permute-done = bf16[1,384,512]{2,1,0:T(8,128)(2,1)S(1)} collective-permute-done((bf16[1,384,512]{2,1,0:T(8,128)(2,1)S(1)}, bf16[1,384,512]{2,1,0:T(8,128)(2,1)S(1)}, u32[]{:S(2)}, u32[]{:S(2)}) %collective-permute-start) | collective-permute-done | bytes 393248 | tf_op jit(solution)/shard_map/ppermute | solution.py:20
  122.0 0.4 fusion.9
  122.5 2.1 %fusion.5 = (bf16[2,384,512]{2,1,0:T(8,128)(2,1)S(1)}, f32[2,384,512]{2,1,0:T(8,128)}) fusion(f32[2,384,512]{2,1,0:T(8,128)S(1)} %get-tuple-element.28, f32[]{:T(128)S(6)} %div.35, f32[]{:T(128)S(6)} %mul.148, f32[1,384,512]{2,1,0:T(8,128)S(1)} %fusion.9, f32[1,384,512]{2,1,0:T(8,128)S(1)} %convolution_bitcast_fusion.2, ...), kind=kOutput, calls=%fused_computation.19 | convolution fusion | flops 406978560 | bytes 8917000 | tf_op jit(solution)/shard_map/jik,jmk->jmi/dot_general | solution.py:26
  124.6 0.8 slice.77
  125.3 10.5 %collective-permute-start.5 = (bf16[1,384,512]{2,1,0:T(8,128)(2,1)}, bf16[1,384,512]{2,1,0:T(8,128)(2,1)}, u32[]{:S(2)}, u32[]{:S(2)}) collective-permute-start(bf16[1,384,512]{2,1,0:T(8,128)(2,1)} %slice.77), channel_id=1, source_target_pairs={{0,1},{1,2},{2,3},{4,5},{5,6},{6,7},{8,9},{9,10},{10,11},{12,13},{... | collective-permute-start | bytes 1179656 | tf_op jit(solution)/shard_map/ppermute | solution.py:19
  136.0 1.4 collective-permute-start.4
  137.4 0.4 convolution_bitcast_fusion
  137.8 0.4 convolution_bitcast_fusion.1
  138.2 5.3 %collective-permute-done.5 = bf16[1,384,512]{2,1,0:T(8,128)(2,1)} collective-permute-done((bf16[1,384,512]{2,1,0:T(8,128)(2,1)}, bf16[1,384,512]{2,1,0:T(8,128)(2,1)}, u32[]{:S(2)}, u32[]{:S(2)}) %collective-permute-start.5) | collective-permute-done | bytes 393248 | tf_op jit(solution)/shard_map/ppermute | solution.py:19
  143.5 1.5 fusion.12
  145.1 10.6 %collective-permute-done.4 = bf16[1,384,512]{2,1,0:T(8,128)(2,1)S(1)} collective-permute-done((bf16[1,384,512]{2,1,0:T(8,128)(2,1)}, bf16[1,384,512]{2,1,0:T(8,128)(2,1)S(1)}, u32[]{:S(2)}, u32[]{:S(2)}) %collective-permute-start.4) | collective-permute-done | bytes 393248 | tf_op jit(solution)/shard_map/ppermute | solution.py:20
  155.6 0.4 fusion.8
  156.1 1.1 add_add_fusion
  157.2 2.4 %copy.55 = f32[2,384,512]{2,0,1:T(2,128)} copy(f32[2,384,512]{2,1,0:T(8,128)S(1)} %add_add_fusion) | data formatting | bytes 3145728 | tf_op jit(solution)/shard_map/add | solution.py:112
  159.6 4.5 %all-to-all-start.2 = ((f32[2,384,512]{2,0,1:T(2,128)}), f32[2,384,512]{2,0,1:T(2,128)S(1)}, u32[]{:S(2)}, u32[]{:S(2)}) async-start(f32[2,384,512]{2,0,1:T(2,128)} %copy.55), calls=%async_computation.2 | async-start | bytes 3145728 | tf_op jit(solution)/shard_map/all_to_all | solution.py:139
  164.2 0.7 gather_fusion.5
  164.9 37.0 %all-to-all-done.2 = f32[2,384,512]{2,0,1:T(2,128)S(1)} async-done(((f32[2,384,512]{2,0,1:T(2,128)}), f32[2,384,512]{2,0,1:T(2,128)S(1)}, u32[]{:S(2)}, u32[]{:S(2)}) %all-to-all-start.2) | async-done | bytes 1572896 | tf_op jit(solution)/shard_map/all_to_all | solution.py:139
  202.0 0.3 copy.56
  202.4 0.6 gather_fusion.6
  203.1 1.1 copy.63
  (61 shorter events, 1.5 us)
Async XLA Ops:
  0.0 4.0 %copy-start.14 = (f32[48,6144]{1,0:T(8,128)S(1)}, f32[48,6144]{1,0:T(8,128)}, u32[]{:S(2)}) copy-start(f32[48,6144]{1,0:T(8,128)} %param.10) | copy-start | bytes 3538948
  6.3 1.9 copy-start.3
  55.4 22.8 %copy-start.16 = (f32[6144]{0:T(1024)S(1)}, f32[6144]{0:T(1024)}, u32[]{:S(2)}) copy-start(f32[6144]{0:T(1024)} %param.11) | copy-start | bytes 73732
  55.4 22.8 %copy-start.15 = (bf16[2,512,512]{2,1,0:T(8,128)(2,1)S(1)}, bf16[2,512,512]{2,1,0:T(8,128)(2,1)}, u32[]{:S(2)}) copy-start(bf16[2,512,512]{2,1,0:T(8,128)(2,1)} %param.12) | copy-start | bytes 3145732
  55.4 42.4 %all-to-all-start = ((f32[16,48,512]{2,1,0:T(8,128)}), f32[16,48,512]{2,1,0:T(8,128)}, u32[]{:S(2)}, u32[]{:S(2)}) async-start(f32[16,48,512]{2,1,0:T(8,128)} %get-tuple-element.34), calls=%async_computation | async-start | bytes 3145728 | tf_op jit(solution)/shard_map/all_to_all | solution.py:64
  88.1 1.9 copy-start.1
  91.1 18.7 %collective-permute-start.1 = (bf16[1,384,512]{2,1,0:T(8,128)(2,1)}, bf16[1,384,512]{2,1,0:T(8,128)(2,1)}, u32[]{:S(2)}, u32[]{:S(2)}) collective-permute-start(bf16[1,384,512]{2,1,0:T(8,128)(2,1)} %slice.73), channel_id=1, source_target_pairs={{1,0},{2,1},{3,2},{5,4},{6,5},{7,6},{9,8},{10,9},{11,10},{13,12},{... | collective-permute-start | bytes 1179656 | tf_op jit(solution)/shard_map/ppermute | solution.py:20
  92.4 15.4 %collective-permute-start.3 = (bf16[1,384,512]{2,1,0:T(8,128)(2,1)}, bf16[1,384,512]{2,1,0:T(8,128)(2,1)}, u32[]{:S(2)}, u32[]{:S(2)}) collective-permute-start(bf16[1,384,512]{2,1,0:T(8,128)(2,1)} %slice.73), channel_id=1, source_target_pairs={{0,1},{1,2},{2,3},{4,5},{5,6},{6,7},{8,9},{9,10},{10,11},{12,13},{... | collective-permute-start | bytes 1179656 | tf_op jit(solution)/shard_map/ppermute | solution.py:19
  99.3 6.4 %copy-start = (f32[2,512,512]{2,1,0:T(8,128)S(1)}, f32[2,512,512]{2,1,0:T(8,128)}, u32[]{:S(2)}) copy-start(f32[2,512,512]{2,1,0:T(8,128)} %gather_fusion.3) | copy-start | bytes 6291460
  99.3 6.4 %copy-start.2 = (f32[2,512,512]{1,2,0:T(8,128)S(1)}, f32[2,512,512]{1,2,0:T(8,128)}, u32[]{:S(2)}) copy-start(f32[2,512,512]{1,2,0:T(8,128)} %copy.50) | copy-start | bytes 6291460
  99.5 22.9 %copy-start.4 = (f32[2,384,512]{2,1,0:T(8,128)}, f32[2,384,512]{2,1,0:T(8,128)S(1)}, u32[]{:S(2)}) copy-start(f32[2,384,512]{2,1,0:T(8,128)S(1)} %get-tuple-element.28) | copy-start | bytes 4718596
  99.6 22.5 %collective-permute-start = (bf16[1,384,512]{2,1,0:T(8,128)(2,1)S(1)}, bf16[1,384,512]{2,1,0:T(8,128)(2,1)S(1)}, u32[]{:S(2)}, u32[]{:S(2)}) collective-permute-start(bf16[1,384,512]{2,1,0:T(8,128)(2,1)S(1)} %slice.75), channel_id=1, source_target_pairs={{1,0},{2,1},{3,2},{5,4},{6,5},{7,6},{9,8},{10,9},{11,10},{13,12},{... | collective-permute-start | bytes 1179656 | tf_op jit(solution)/shard_map/ppermute | solution.py:20
  101.1 13.1 %collective-permute-start.2 = (bf16[1,384,512]{2,1,0:T(8,128)(2,1)S(1)}, bf16[1,384,512]{2,1,0:T(8,128)(2,1)S(1)}, u32[]{:S(2)}, u32[]{:S(2)}) collective-permute-start(bf16[1,384,512]{2,1,0:T(8,128)(2,1)S(1)} %slice.75), channel_id=1, source_target_pairs={{0,1},{1,2},{2,3},{4,5},{5,6},{6,7},{8,9},{9,10},{10,11},{12,13},{... | collective-permute-start | bytes 1179656 | tf_op jit(solution)/shard_map/ppermute | solution.py:19
  106.6 15.9 %copy-start.10 = (bf16[2,512,512]{2,1,0:T(8,128)(2,1)}, bf16[2,512,512]{2,1,0:T(8,128)(2,1)S(1)}, u32[]{:S(2)}) copy-start(bf16[2,512,512]{2,1,0:T(8,128)(2,1)S(1)} %fusion.2) | copy-start | bytes 3145732
  107.1 1.2 copy-start.12
  109.8 4.9 %copy-start.8 = (bf16[512,512]{1,0:T(8,128)(2,1)}, bf16[512,512]{1,0:T(8,128)(2,1)S(1)}, u32[]{:S(2)}) copy-start(bf16[512,512]{1,0:T(8,128)(2,1)S(1)} %fusion.11) | copy-start | bytes 1572868
  111.5 11.0 %copy-start.6 = (bf16[512,512]{1,0:T(8,128)(2,1)}, bf16[512,512]{1,0:T(8,128)(2,1)S(1)}, u32[]{:S(2)}) copy-start(bf16[512,512]{1,0:T(8,128)(2,1)S(1)} %fusion.10) | copy-start | bytes 1572868
  125.3 18.1 %collective-permute-start.5 = (bf16[1,384,512]{2,1,0:T(8,128)(2,1)}, bf16[1,384,512]{2,1,0:T(8,128)(2,1)}, u32[]{:S(2)}, u32[]{:S(2)}) collective-permute-start(bf16[1,384,512]{2,1,0:T(8,128)(2,1)} %slice.77), channel_id=1, source_target_pairs={{0,1},{1,2},{2,3},{4,5},{5,6},{6,7},{8,9},{9,10},{10,11},{12,13},{... | collective-permute-start | bytes 1179656 | tf_op jit(solution)/shard_map/ppermute | solution.py:19
  135.9 7.6 %copy-start.9 = (bf16[512,512]{1,0:T(8,128)(2,1)S(1)}, bf16[512,512]{1,0:T(8,128)(2,1)}, u32[]{:S(2)}) copy-start(bf16[512,512]{1,0:T(8,128)(2,1)} %copy-done.8) | copy-start | bytes 1572868
  136.0 19.7 %collective-permute-start.4 = (bf16[1,384,512]{2,1,0:T(8,128)(2,1)}, bf16[1,384,512]{2,1,0:T(8,128)(2,1)S(1)}, u32[]{:S(2)}, u32[]{:S(2)}) collective-permute-start(bf16[1,384,512]{2,1,0:T(8,128)(2,1)} %slice.77), channel_id=1, source_target_pairs={{1,0},{2,1},{3,2},{5,4},{6,5},{7,6},{9,8},{10,9},{11,10},{13,12},{... | collective-permute-start | bytes 1179656 | tf_op jit(solution)/shard_map/ppermute | solution.py:20
  137.8 17.9 %copy-start.7 = (bf16[512,512]{1,0:T(8,128)(2,1)S(1)}, bf16[512,512]{1,0:T(8,128)(2,1)}, u32[]{:S(2)}) copy-start(bf16[512,512]{1,0:T(8,128)(2,1)} %copy-done.6) | copy-start | bytes 1572868
  143.5 12.6 %copy-start.11 = (bf16[2,512,512]{2,1,0:T(8,128)(2,1)S(1)}, bf16[2,512,512]{2,1,0:T(8,128)(2,1)}, u32[]{:S(2)}) copy-start(bf16[2,512,512]{2,1,0:T(8,128)(2,1)} %copy-done.10) | copy-start | bytes 3145732
  143.5 12.6 %copy-start.13 = (f32[2,384,512]{2,1,0:T(8,128)S(1)}, f32[2,384,512]{2,1,0:T(8,128)}, u32[]{:S(2)}) copy-start(f32[2,384,512]{2,1,0:T(8,128)} %get-tuple-element.36) | copy-start | bytes 4718596
  145.0 11.0 %copy-start.5 = (f32[2,384,512]{2,1,0:T(8,128)S(1)}, f32[2,384,512]{2,1,0:T(8,128)}, u32[]{:S(2)}) copy-start(f32[2,384,512]{2,1,0:T(8,128)} %copy-done.4) | copy-start | bytes 4718596
  159.6 42.4 %all-to-all-start.2 = ((f32[2,384,512]{2,0,1:T(2,128)}), f32[2,384,512]{2,0,1:T(2,128)S(1)}, u32[]{:S(2)}, u32[]{:S(2)}) async-start(f32[2,384,512]{2,0,1:T(2,128)} %copy.55), calls=%async_computation.2 | async-start | bytes 3145728 | tf_op jit(solution)/shard_map/all_to_all | solution.py:139
where the time goes:
time: 205 us; the launch traced here: 204 us
  waiting for transfers between devices  63.1 us (31%)
  blocking collectives  44 us (21%)
  starting transfers between devices  33.6 us (16%)
  local copies, waits for them, and re-layouts  30.5 us (15%)
  between operations  12.9 us (6%)
  matrix products  11.9 us (6%)
  other arithmetic  8.02 us (4%)
    all_to_all x1, blocking collectives, on_device(): lax.all_to_all(pack_regions(equivalents), 'mem', split_axis=0, concat_axi...  44 us
    all_to_all x1, waiting for transfers between devices, on_device(): lax.all_to_all(solution, 'mem', split_axis=1, concat_axis=0, tiled=True)  37 us
    ppermute x3, starting transfers between devices, extended(): before = lax.ppermute(last, axis, up)  20.4 us
    ppermute x3, waiting for transfers between devices, extended(): after = lax.ppermute(initial, axis, down)  18 us
    dot_general x14, matrix products, block_prod(): jnp.einsum(einsum_form, left_op, right_op, preferred_element_type=jnp.flo...  11.9 us
    ppermute x3, waiting for transfers between devices, extended(): before = lax.ppermute(last, axis, up)  8.11 us
    gather x2, local copies, waits for them, and re-layouts, on_device(): tile_self = taper_table[own_index[:, 0]]  4.93 us
    all_to_all x1, starting transfers between devices, on_device(): lax.all_to_all(solution, 'mem', split_axis=1, concat_axis=0, tiled=True)  4.53 us
  transfers between devices with their start and end apart: 8, of which 5 were waited for; matrix products, arithmetic and copies ran while one was open for 14% of the time, Pallas kernels for 0%

commit v1 on v0

v1 whole, which is shorter than its diff:
```python
import functools

import jax
import jax.numpy as jnp
from jax import lax
from jax.experimental import pallas as pl
from jax.experimental.pallas import tpu as pltpu
from jax.sharding import PartitionSpec as P

BF = jnp.bfloat16
F32 = jnp.float32
VMEM_LIMIT = 48 * 1024 * 1024

SMEM_SPEC = pl.BlockSpec(memory_space=pltpu.SMEM)
VMEM_SPEC = pl.BlockSpec(memory_space=pltpu.VMEM)


def kernel_call(body, outs, scalars, arrays, scratch=(), name=None):
    return pl.pallas_call(
        body,
        out_shape=tuple(jax.ShapeDtypeStruct(s, d) for s, d in outs),
        in_specs=[SMEM_SPEC] * len(scalars) + [VMEM_SPEC] * len(arrays),
        out_specs=tuple(VMEM_SPEC for _ in outs),
        scratch_shapes=list(scratch),
        compiler_params=pltpu.CompilerParams(vmem_limit_bytes=VMEM_LIMIT),
        name=name,
    )(*scalars, *arrays)


def dot_nn(a, b):
    return lax.dot_general(a, b, (((1,), (0,)), ((), ())), preferred_element_type=F32)


def dot_nt(a, b):
    return lax.dot_general(a, b, (((1,), (1,)), ((), ())), preferred_element_type=F32)


def dot_tn(a, b):
    return lax.dot_general(a, b, (((0,), (0,)), ((), ())), preferred_element_type=F32)


def region_start(rb, band, m):
    return lax.fori_loop(0, m, lambda i, acc: acc + rb[band, i], jnp.int32(0))


def block_cols(block, width):
    return pl.ds(pl.multiple_of(block * width, width), width)


def chebyshev(low, high, width):
    low = jnp.full((1, width), low, F32)
    high = jnp.full((1, width), high, F32)
    centre = 0.5 * (high + low)
    half = 0.5 * (high - low)
    s = centre / half
    q0 = 1.0 / s
    q1 = 1.0 / (2.0 * s - q0)
    q2 = 1.0 / (2.0 * s - q1)
    inv_c = 1.0 / centre
    keep1, gain1 = q1 * q0, 2.0 * q1 / half
    keep2, gain2 = q2 * q1, 2.0 * q2 / half
    return inv_c, keep1, gain1, keep2, gain2


def on_device(
    equivalents,
    innovations,
    obs_var,
    taper_tiles,
    region_blocks,
    pair_mask,
    taper_index,
    eig_low,
    eig_high,
):
    n = lax.axis_size("mem")
    n_lat = lax.axis_size("lat")
    chips = n // 2
    rows, cols = equivalents.shape
    B = taper_tiles.shape[1]
    nb = cols // B
    members = rows * n
    inv_scale = (members - 1) ** (-0.5)
    rp = -(-rows // 16) * 16
    mp = rp * n
    half = mp // 2

    def put_rows(ref_set, lo, value):
        ref_set(slice(lo, lo + rows), value)
        if rp > rows:
            ref_set(slice(lo + rows, lo + rp), jnp.zeros((rp - rows, B), value.dtype))

    def pack_body(rb, eq, inn, lsum, r1own, r1oth, r2own, r2oth, xoth):
        me, band = lax.axis_index("mem"), lax.axis_index("lat")
        lsum[...] = jnp.sum(eq[...], axis=0, keepdims=True)
        for k in range(chips):
            first = region_start(rb, band, me ^ (2 * k))
            second = jnp.minimum(first + 1, nb - 1)
            put_rows(lambda s, v: r1own.__setitem__((k, s), v), 0, inn[:, block_cols(first, B)].astype(BF))
            put_rows(lambda s, v: r2own.__setitem__((k, s), v), 0, inn[:, block_cols(second, B)].astype(BF))
            first = region_start(rb, band, me ^ (2 * k + 1))
            second = jnp.minimum(first + 1, nb - 1)
            put_rows(lambda s, v: r1oth.__setitem__((k, s), v), 0, inn[:, block_cols(first, B)].astype(BF))
            put_rows(lambda s, v: r2oth.__setitem__((k, s), v), 0, inn[:, block_cols(second, B)].astype(BF))
            put_rows(lambda s, v: xoth.__setitem__((k, s), v), 0, eq[:, block_cols(first, B)])
            put_rows(lambda s, v: xoth.__setitem__((chips + k, s), v), 0, eq[:, block_cols(second, B)])

    slots = (chips, rp, B)
    lsum, r1own, r1oth, r2own, r2oth, xoth = kernel_call(
        pack_body,
        [((1, cols), F32), (slots, BF), (slots, BF), (slots, BF), (slots, BF), ((2 * chips, rp, B), F32)],
        [region_blocks],
        [equivalents, innovations],
        name="pack",
    )
    core_pairs = [(i, i ^ 1) for i in range(n)]

    def swap_core(x):
        return lax.ppermute(x, "mem", core_pairs)

    def z_exchange(parts):
        got = [parts[0]] + [None] * (chips - 1)
        for k in reversed(range(1, chips)):
            got[k] = lax.ppermute(parts[k], "mem", [(i, i ^ (2 * k)) for i in range(n)])
        return got

    r1oth = swap_core(r1oth)
    sums = lax.all_gather(lsum, "mem", axis=0, tiled=True)
    xoth = swap_core(xoth)
    r2oth = swap_core(r2oth)

    def join_body(own, oth, *outs):
        for k in range(chips):
            outs[k][0:rp, :] = own[k]
            outs[k][rp : 2 * rp, :] = oth[k]

    r1_parts = kernel_call(
        join_body, [((2 * rp, B), BF)] * chips, [], [r1own, r1oth], name="join_r1"
    )
    r1_got = z_exchange(r1_parts)

    def perturb(x, sums_ref, block):
        mean = jnp.sum(sums_ref[:, block_cols(block, B)], axis=0, keepdims=True) * (1.0 / members)
        return ((x - mean) * inv_scale).astype(BF)

    def perturb1_body(rb, eq, sums_ref, xo, *outs):
        me, band = lax.axis_index("mem"), lax.axis_index("lat")
        for k in range(chips):
            first = region_start(rb, band, me ^ (2 * k))
            own = perturb(eq[:, block_cols(first, B)], sums_ref, first)
            oth = perturb(xo[k, 0:rows, :], sums_ref, first)
            put = lambda s, v: outs[k].__setitem__((s,), v)
            put_rows(put, 0, own)
            put_rows(put, rp, oth)

    def perturb2_body(rb, eq, sums_ref, xo, r2w, r2o, *outs):
        me, band = lax.axis_index("mem"), lax.axis_index("lat")
        for k in range(chips):
            second = jnp.minimum(region_start(rb, band, me ^ (2 * k)) + 1, nb - 1)
            own = perturb(eq[:, block_cols(second, B)], sums_ref, second)
            oth = perturb(xo[chips + k, 0:rows, :], sums_ref, second)
            put = lambda s, v: outs[k].__setitem__((s,), v)
            put_rows(put, 0, own)
            put_rows(put, rp, oth)
            outs[k][2 * rp : 3 * rp, :] = r2w[k]
            outs[k][3 * rp : 4 * rp, :] = r2o[k]

    p1_parts = kernel_call(
        perturb1_body,
        [((2 * rp, B), BF)] * chips,
        [region_blocks],
        [equivalents, sums, xoth],
        name="perturb_first",
    )
    p1_got = z_exchange(p1_parts)
    p2_parts = kernel_call(
        perturb2_body,
        [((4 * rp, B), BF)] * chips,
        [region_blocks],
        [equivalents, sums, xoth, r2own, r2oth],
        name="perturb_second",
    )
    p2_got = z_exchange(p2_parts)

    pair_list = [(i, i ^ 1) for i in range(n_lat)]
    skew_list = [(i, i + 1) for i in range(1, n_lat - 1, 2)] + [(i + 1, i) for i in range(1, n_lat - 1, 2)]
    hop1_list = [(i, i + 2) for i in range(1, n_lat - 1, 2)] + [(i, i - 2) for i in range(2, n_lat, 2)]
    hop2_list = [(i + 2, i + 1) for i in range(1, n_lat - 1, 2)] + [(i - 2, i - 1) for i in range(2, n_lat, 2)]

    def lat_exchange(whole, low, high):
        relay = lax.ppermute(high, "lat", hop1_list)
        skew_low = lax.ppermute(low, "lat", skew_list)
        pair = lax.ppermute(whole, "lat", pair_list)
        skew_high = lax.ppermute(relay, "lat", hop2_list)
        return pair, skew_low, skew_high

    def gather_body(*refs):
        parts, (whole, low, high) = refs[:chips], refs[chips:]
        step = 2 * rp
        for k in range(chips):
            value = parts[k][...]
            whole[k * step : (k + 1) * step, :] = value
            if k < chips // 2:
                low[k * step : (k + 1) * step, :] = value
            else:
                high[(k - chips // 2) * step : (k + 1 - chips // 2) * step, :] = value

    block_outs = [((mp, B), BF), ((half, B), BF), ((half, B), BF)]
    r1, r1_low, r1_high = kernel_call(gather_body, block_outs, [], r1_got, name="gather_r1")
    r1_pair, r1_skew_low, r1_skew_high = lat_exchange(r1, r1_low, r1_high)
    p1, p1_low, p1_high = kernel_call(gather_body, block_outs, [], p1_got, name="gather_p1")
    p1_pair, p1_skew_low, p1_skew_high = lat_exchange(p1, p1_low, p1_high)

    var_row = obs_var.reshape(1, cols)
    step = 2 * rp

    def region_body(rb, pm, ti, el, eh, tt, var, p1_ref, r1_ref, *refs):
        parts = refs[:chips]
        s1, s2, ce, z1, d2b, t2, p2s, r2s = refs[chips:]
        me, band = lax.axis_index("mem"), lax.axis_index("lat")
        first = region_start(rb, band, me)
        second = jnp.minimum(first + 1, nb - 1)
        count = rb[band, me]
        inv_c, keep1, gain1, keep2, gain2 = chebyshev(el[0], eh[0], B)
        for k in range(chips):
            p2s[k * step : (k + 1) * step, :] = parts[k][0:step, :]
            r2s[k * step : (k + 1) * step, :] = parts[k][step : 2 * step, :]
        p1v, p2v, r1v, r2v = p1_ref[...], p2s[...], r1_ref[...], r2s[...]

        def self_cov(pv, block):
            tile = tt[ti[band, block, 0]].astype(F32)
            tile = 0.5 * (tile + tile.T)
            return (tile * dot_tn(pv, pv)).astype(BF)

        s1[...] = self_cov(p1v, first)
        s2[...] = self_cov(p2v, second)
        active = ((count > 1) & (pm[band, first] == 1)).astype(F32)
        tile_east = tt[ti[band, first, 1]].astype(F32) * active
        ce[...] = (tile_east * dot_tn(p1v, p2v)).astype(BF)
        z1[...] = dot_nn(r1v, s1[...]) + dot_nt(r2v, ce[...])
        prod = dot_nn(r2v, s2[...]) + dot_nn(r1v, ce[...])
        var2 = var[:, block_cols(second, B)]
        r2f = r2v.astype(F32)
        d0 = r2f * inv_c
        res = r2f - (var2 * d0 + prod * inv_c)
        d1 = keep1 * d0 + gain1 * res
        d2b[...] = d1.astype(BF)
        t2[...] = (1.0 + keep2) * d1 + gain2 * (res - var2 * d1)

    mat = ((B, B), BF)
    field = ((mp, B), F32)
    s1, s2, ce, z1, d1b_2, t2 = kernel_call(
        region_body,
        [mat, mat, mat, field, ((mp, B), BF), field],
        [region_blocks, pair_mask, taper_index, eig_low, eig_high],
        [taper_tiles, var_row, p1, r1, *p2_got],
        scratch=[pltpu.VMEM((mp, B), BF), pltpu.VMEM((mp, B), BF)],
        name="region_cov",
    )

    def edge_body(
        rb, ti, el, eh, tt, var, p1_ref, pp, pl_lo, pl_hi, r1_ref, rpair, rl_lo, rl_hi, z1_ref,
        qp, qs, d1w, d1l, d1h, t1, pskew, rskew,
    ):
        me, band = lax.axis_index("mem"), lax.axis_index("lat")
        first = region_start(rb, band, me)
        below = jnp.maximum(band - 1, 0)
        first_below = region_start(rb, below, me)
        even = lax.rem(band, 2) == 0
        tile_up = tt[ti[band, first, 2]].astype(F32).T
        tile_down = tt[ti[below, first_below, 2]].astype(F32)
        pskew[0:half, :] = pl_lo[...]
        pskew[half:mp, :] = pl_hi[...]
        rskew[0:half, :] = rl_lo[...]
        rskew[half:mp, :] = rl_hi[...]
        p1v = p1_ref[...]
        qp[...] = (jnp.where(even, tile_up, tile_down) * dot_tn(pp[...], p1v)).astype(BF)
        qs[...] = (jnp.where(even, tile_down, tile_up) * dot_tn(pskew[...], p1v)).astype(BF)
        prod = z1_ref[...] + dot_nn(rpair[...], qp[...]) + dot_nn(rskew[...], qs[...])
        inv_c, keep1, gain1, keep2, gain2 = chebyshev(el[0], eh[0], B)
        var1 = var[:, block_cols(first, B)]
        r1f = r1_ref[...].astype(F32)
        d0 = r1f * inv_c
        res = r1f - (var1 * d0 + prod * inv_c)
        d1 = keep1 * d0 + gain1 * res
        d1b = d1.astype(BF)
        d1w[...] = d1b
        d1l[...] = d1b[0:half, :]
        d1h[...] = d1b[half:mp, :]
        t1[...] = (1.0 + keep2) * d1 + gain2 * (res - var1 * d1)

    qp, qs, d1b_1, d1_low, d1_high, t1 = kernel_call(
        edge_body,
        [mat, mat, *block_outs, field],
        [region_blocks, taper_index, eig_low, eig_high],
        [
            taper_tiles, var_row, p1, p1_pair, p1_skew_low, p1_skew_high,
            r1, r1_pair, r1_skew_low, r1_skew_high, z1,
        ],
        scratch=[pltpu.VMEM((mp, B), BF), pltpu.VMEM((mp, B), BF)],
        name="edge_cov",
    )
    d1_pair, d1_skew_low, d1_skew_high = lat_exchange(d1b_1, d1_low, d1_high)

    def by_member(out, value):
        me = lax.axis_index("mem")
        for j in range(n):
            out[me ^ j] = value[j * rp : (j + 1) * rp, :].astype(BF)

    def inner_body(el, eh, s1_ref, s2_ref, ce_ref, d1_ref, d2_ref, t1_ref, t2_ref, out, w1):
        gain2 = chebyshev(el[0], eh[0], B)[4]
        d1v, d2v, cev = d1_ref[...], d2_ref[...], ce_ref[...]
        by_member(out, t2_ref[...] - gain2 * (dot_nn(d2v, s2_ref[...]) + dot_nn(d1v, cev)))
        w1[...] = t1_ref[...] - gain2 * (dot_nn(d1v, s1_ref[...]) + dot_nt(d2v, cev))

    back = ((n, rp, B), BF)
    sol_2, w1 = kernel_call(
        inner_body,
        [back, field],
        [eig_low, eig_high],
        [s1, s2, ce, d1b_1, d1b_2, t1, t2],
        name="inner_step",
    )

    def outer_body(el, eh, qp_ref, qs_ref, dp, dl, dh, w1_ref, out, dskew):
        gain2 = chebyshev(el[0], eh[0], B)[4]
        dskew[0:half, :] = dl[...]
        dskew[half:mp, :] = dh[...]
        prod = dot_nn(dp[...], qp_ref[...]) + dot_nn(dskew[...], qs_ref[...])
        by_member(out, w1_ref[...] - gain2 * prod)

    (sol_1,) = kernel_call(
        outer_body,
        [back],
        [eig_low, eig_high],
        [qp, qs, d1_pair, d1_skew_low, d1_skew_high, w1],
        scratch=[pltpu.VMEM((mp, B), BF)],
        name="outer_step",
    )
    sol_2 = lax.all_to_all(sol_2, "mem", split_axis=0, concat_axis=0, tiled=True)
    sol_1 = lax.all_to_all(sol_1, "mem", split_axis=0, concat_axis=0, tiled=True)

    def unpack_body(rb, el, eh, inn, a1, a2, out):
        band = lax.axis_index("lat")
        inv_c = chebyshev(el[0], eh[0], B)[0]
        block = jnp.int32(0)
        for m in range(n):
            at = block_cols(block, B)
            out[:, at] = inn[:, at] * inv_c + a1[m, 0:rows, :].astype(F32)
            count = rb[band, m]
            after = block + 1

            @pl.when(count > 1)
            def _():
                at2 = block_cols(jnp.minimum(after, nb - 1), B)
                out[:, at2] = inn[:, at2] * inv_c + a2[m, 0:rows, :].astype(F32)

            block = block + count

    (out,) = kernel_call(
        unpack_body,
        [((rows, cols), F32)],
        [region_blocks, eig_low, eig_high],
        [innovations, sol_1, sol_2],
        name="unpack",
    )
    return out


def solution(mesh):
    return jax.shard_map(
        on_device,
        mesh=mesh,
        in_specs=(P("mem", "lat"), P("mem", "lat"), P("lat"), P(), P(), P(), P(), P(), P()),
        out_specs=P("mem", "lat"),
        check_vma=False,
    )
```

time: 205 us -> 135 us (0.66)
  waiting for transfers between devices: 63.1 us -> 26.1 us
  local copies, waits for them, and re-layouts: 30.5 us -> 16 us
  Pallas kernels: 0 us -> 13.2 us
  matrix products: 11.9 us -> 0 us
  between operations: 12.9 us -> 1.67 us
  blocking collectives: 44 us -> 34.1 us
  starting transfers between devices: 33.6 us -> 42.9 us
  other arithmetic: 8.02 us -> 0 us
    all_to_all x2 -> x1, waiting for transfers between devices: 37.1 us -> 0.01 us  [on_device(): lax.all_to_all(sol_2, 'mem', split_axis=0, concat_axis=0, tiled=True)]
    all_to_all x1, blocking collectives: 44 us -> 17.1 us  [on_device(): lax.all_to_all(sol_1, 'mem', split_axis=0, concat_axis=0, tiled=True)]
    all_gather x0 -> x1, blocking collectives: none -> 17 us  [on_device(): sums = lax.all_gather(lsum, 'mem', axis=0, tiled=True)]
    unnamed x34 -> x54, local copies, waits for them, and re-layouts: 0.67 us -> 16 us
    ppermute x6 -> x24, starting transfers between devices: 24.7 us -> 38.9 us  [the longest x9 12 us: z_exchange(): got[k] = lax.ppermute(parts[k], 'mem', [(i, i ^ 2 * k) for i in range(n)])]
    pallas_call x0 -> x11, Pallas kernels: none -> 13.2 us  [kernel_call(): pl.pallas_call(body, out_shape=tuple((jax.ShapeDtypeStruct(s, d) for s, d...]
    gather x9 -> x0, local copies, waits for them, and re-layouts: 12.3 us -> none  [the longest x2 4.93 us: on_device(): tile_self = taper_table[own_index[:, 0]]]
    dot_general x14 -> x0, matrix products: 11.9 us -> none  [block_prod(): jnp.einsum(einsum_form, left_op, right_op, preferred_element_type=jnp.flo...]
  transfers between devices with their start and end apart: 8 -> 25, of which waited for: 5 -> 5; matrix products, arithmetic and copies ran while one was open for 14% -> 0% of each run, Pallas kernels for 0% -> 5%
where the time goes in v1:
time: 135 us; the launch traced here: 134 us
  starting transfers between devices  42.9 us (32%)
  blocking collectives  34.1 us (25%)
  waiting for transfers between devices  26.1 us (19%)
  local copies, waits for them, and re-layouts  16 us (12%)
  Pallas kernels  13.2 us (10%)
  between operations  1.67 us (1%)
    all_to_all x1, blocking collectives, on_device(): lax.all_to_all(sol_1, 'mem', split_axis=0, concat_axis=0, tiled=True)  17.1 us
    all_gather x1, blocking collectives, on_device(): sums = lax.all_gather(lsum, 'mem', axis=0, tiled=True)  17 us
    unnamed x54, local copies, waits for them, and re-layouts  16 us
    ppermute x9, waiting for transfers between devices, z_exchange(): got[k] = lax.ppermute(parts[k], 'mem', [(i, i ^ 2 * k) for i in range(n)])  13.6 us
    pallas_call x11, Pallas kernels, kernel_call(): pl.pallas_call(body, out_shape=tuple((jax.ShapeDtypeStruct(s, d) for s, d...  13.2 us
    ppermute x9, starting transfers between devices, z_exchange(): got[k] = lax.ppermute(parts[k], 'mem', [(i, i ^ 2 * k) for i in range(n)])  12 us
    ppermute x3, starting transfers between devices, lat_exchange(): pair = lax.ppermute(whole, 'lat', pair_list)  10.6 us
    ppermute x3, starting transfers between devices, lat_exchange(): skew_high = lax.ppermute(relay, 'lat', hop2_list)  9.45 us
  transfers between devices with their start and end apart: 25, of which 5 were waited for; matrix products, arithmetic and copies ran while one was open for 0% of the time, Pallas kernels for 5%

profile of v1, /device:TPU:0, one launch (start us, length us, event | category | flops | bytes accessed | tf_op | source)
XLA Modules:
  0.0 134.0 jit_solution(5940340053336589524)
XLA Ops:
  0.0 1.3 copy-done
  1.3 1.3 copy-done.2
  2.5 0.7 copy-done.22
  3.2 1.0 pack.1
  4.2 0.5 collective-permute-start
  4.7 0.1 collective-permute-start.8
  4.8 0.4 collective-permute-start.16
  5.3 1.7 %collective-permute-done.8.oth = bf16[4,48,512]{2,1,0:T(8,128)(2,1)S(1)} collective-permute-done((bf16[4,48,512]{2,1,0:T(8,128)(2,1)S(1)}, bf16[4,48,512]{2,1,0:T(8,128)(2,1)S(1)}, u32[]{:S(2)}, u32[]{:S(2)}) %collective-permute-start.8) | collective-permute-done | bytes 196640 | tf_op jit(solution)/shard_map/ppermute | solution.py:119
  7.0 3.0 %collective-permute-start.9 = (bf16[96,512]{1,0:T(8,128)(2,1)S(1)}, bf16[96,512]{1,0:T(8,128)(2,1)S(1)}, u32[]{:S(2)}, u32[]{:S(2)}) collective-permute-start(bf16[96,512]{1,0:T(8,128)(2,1)S(1)} %get-tuple-element.55), channel_id=1, source_target_pairs={{0,8},{4,12},{8,0},{12,4},{16,24},{20,28},{24,16},{28,20},{1,9},{5... | collective-permute-start | bytes 294920 | tf_op jit(solution)/shard_map/ppermute | solution.py:124
  10.0 2.6 %collective-permute-start.10 = (bf16[96,512]{1,0:T(8,128)(2,1)S(1)}, bf16[96,512]{1,0:T(8,128)(2,1)S(1)}, u32[]{:S(2)}, u32[]{:S(2)}) collective-permute-start(bf16[96,512]{1,0:T(8,128)(2,1)S(1)} %get-tuple-element.56), channel_id=1, source_target_pairs={{0,16},{4,20},{8,24},{12,28},{16,0},{20,4},{24,8},{28,12},{1,17},{... | collective-permute-start | bytes 294920 | tf_op jit(solution)/shard_map/ppermute | solution.py:124
  12.6 17.0 %all-gather = f32[8,1,6144]{2,1,0:T(1,128)S(1)} all-gather(f32[1,1,6144]{2,1,0:T(1,128)S(1)} %bitcast.9), channel_id=1, replica_groups=mesh['mem'=8,'lat'=4] {'mem'}, dimensions={0}, use_global_device_ids=true | all-gather | bytes 221184 | tf_op jit(solution)/shard_map/all_gather | solution.py:128
  29.6 0.1 copy.16
  29.7 0.8 perturb_first.1
  30.4 0.1 collective-permute-start.1
  30.6 0.1 gather_r1.1
  30.6 0.7 collective-permute-start.13
  31.3 1.3 collective-permute-start.14
  32.6 0.0 copy-start.25
  32.6 0.0 copy-start.4
  32.7 0.8 perturb_second.1
  33.5 2.1 %collective-permute-start.17 = (bf16[192,512]{1,0:T(8,128)(2,1)S(1)}, bf16[192,512]{1,0:T(8,128)(2,1)S(1)}, u32[]{:S(2)}, u32[]{:S(2)}) collective-permute-start(bf16[192,512]{1,0:T(8,128)(2,1)S(1)} %get-tuple-element.64), channel_id=1, source_target_pairs={{0,8},{4,12},{8,0},{12,4},{16,24},{20,28},{24,16},{28,20},{1,9},{5... | collective-permute-start | bytes 589832 | tf_op jit(solution)/shard_map/ppermute | solution.py:124
  35.5 0.6 collective-permute-start.2
  36.1 1.8 %collective-permute-start.3 = (bf16[96,512]{1,0:T(8,128)(2,1)S(1)}, bf16[96,512]{1,0:T(8,128)(2,1)S(1)}, u32[]{:S(2)}, u32[]{:S(2)}) collective-permute-start(bf16[96,512]{1,0:T(8,128)(2,1)S(1)} %get-tuple-element.48), channel_id=1, source_target_pairs={{0,24},{4,28},{8,16},{12,20},{16,8},{20,12},{24,0},{28,4},{1,25},{... | collective-permute-start | bytes 294920 | tf_op jit(solution)/shard_map/ppermute | solution.py:124
  38.0 8.3 %collective-permute-done.2.refs_2_ = bf16[96,512]{1,0:T(8,128)(2,1)S(1)} collective-permute-done((bf16[96,512]{1,0:T(8,128)(2,1)S(1)}, bf16[96,512]{1,0:T(8,128)(2,1)S(1)}, u32[]{:S(2)}, u32[]{:S(2)}) %collective-permute-start.2) | collective-permute-done | bytes 98336 | tf_op jit(solution)/shard_map/ppermute | solution.py:124
  46.3 4.6 %collective-permute-start.12 = (bf16[384,512]{1,0:T(8,128)(2,1)S(1)}, bf16[384,512]{1,0:T(8,128)(2,1)S(1)}, u32[]{:S(2)}, u32[]{:S(2)}) collective-permute-start(bf16[384,512]{1,0:T(8,128)(2,1)S(1)} %get-tuple-element.58.r1_ref), channel_id=1, source_target_pairs={{0,1},{1,0},{2,3},{3,2},{4,5},{5,4},{6,7},{7,6},{8,9},{9,8},{10,11... | collective-permute-start | bytes 1179656 | tf_op jit(solution)/shard_map/ppermute | solution.py:193
  50.9 0.3 collective-permute-start.18
  51.2 0.7 gather_p1.1
  51.9 1.4 %collective-permute-start.19 = (bf16[192,512]{1,0:T(8,128)(2,1)S(1)}, bf16[192,512]{1,0:T(8,128)(2,1)S(1)}, u32[]{:S(2)}, u32[]{:S(2)}) collective-permute-start(bf16[192,512]{1,0:T(8,128)(2,1)S(1)} %get-tuple-element.66), channel_id=1, source_target_pairs={{0,24},{4,28},{8,16},{12,20},{16,8},{20,12},{24,0},{28,4},{1,25},{... | collective-permute-start | bytes 589832 | tf_op jit(solution)/shard_map/ppermute | solution.py:124
  53.4 1.3 collective-permute-start.6
  54.7 0.7 copy-done.15
  55.3 3.3 %collective-permute-start.4 = (bf16[384,512]{1,0:T(8,128)(2,1)S(1)}, bf16[384,512]{1,0:T(8,128)(2,1)S(1)}, u32[]{:S(2)}, u32[]{:S(2)}) collective-permute-start(bf16[384,512]{1,0:T(8,128)(2,1)S(1)} %get-tuple-element.49.p1_ref), channel_id=1, source_target_pairs={{0,1},{1,0},{2,3},{3,2},{4,5},{5,4},{6,7},{7,6},{8,9},{9,8},{10,11... | collective-permute-start | bytes 1179656 | tf_op jit(solution)/shard_map/ppermute | solution.py:193
  58.6 5.3 %collective-permute-done.18.refs_2_ = bf16[192,512]{1,0:T(8,128)(2,1)S(1)} collective-permute-done((bf16[192,512]{1,0:T(8,128)(2,1)S(1)}, bf16[192,512]{1,0:T(8,128)(2,1)S(1)}, u32[]{:S(2)}, u32[]{:S(2)}) %collective-permute-start.18) | collective-permute-done | bytes 196640 | tf_op jit(solution)/shard_map/ppermute | solution.py:124
  63.9 0.7 copy-done.17
  64.6 3.3 %collective-permute-start.15 = (bf16[192,512]{1,0:T(8,128)(2,1)}, bf16[192,512]{1,0:T(8,128)(2,1)S(1)}, u32[]{:S(2)}, u32[]{:S(2)}) collective-permute-start(bf16[192,512]{1,0:T(8,128)(2,1)} %collective-permute-done.14), channel_id=1, source_target_pairs={{3,2},{0,1},{7,6},{4,5},{11,10},{8,9},{15,14},{12,13},{19,18},{16,... | collective-permute-start | bytes 589832 | tf_op jit(solution)/shard_map/ppermute | solution.py:194
  68.0 0.7 copy-done.19
  68.7 0.7 collective-permute-start.5
  69.3 4.6 %collective-permute-start.7 = (bf16[192,512]{1,0:T(8,128)(2,1)}, bf16[192,512]{1,0:T(8,128)(2,1)}, u32[]{:S(2)}, u32[]{:S(2)}) collective-permute-start(bf16[192,512]{1,0:T(8,128)(2,1)} %collective-permute-done.6), channel_id=1, source_target_pairs={{3,2},{0,1},{7,6},{4,5},{11,10},{8,9},{15,14},{12,13},{19,18},{16,... | collective-permute-start | bytes 589832 | tf_op jit(solution)/shard_map/ppermute | solution.py:194
  75.3 0.1 copy.13.ti
  75.4 0.9 copy-done.14
  76.4 0.9 copy-done.16
  77.3 0.9 copy-done.18
  78.2 0.9 copy-done.20
  79.1 3.3 %region_cov.1 = (bf16[512,512]{1,0:T(8,128)(2,1)S(1)}, bf16[512,512]{1,0:T(8,128)(2,1)S(1)}, bf16[512,512]{1,0:T(8,128)(2,1)S(1)}, f32[384,512]{1,0:T(8,128)S(1)...) custom-call(s32[4,8]{1,0:T(4,128)S(1)} %copy-done.23, s32[4,12]{1,0:T(4,128)S(1)} %copy-done.24, ...), custom_call_target="tpu_custom_call" | custom-call | tf_op jit(solution)/shard_map/region_cov/pallas_call | solution.py:19
  82.5 0.7 copy-done.9
  83.2 0.7 copy-done.11
  83.9 0.7 copy-done.7
  84.6 1.0 copy-done.8
  85.6 0.9 copy-done.10
  86.6 0.9 copy-done.12
  87.5 2.9 %edge_cov.1 = (bf16[512,512]{1,0:T(8,128)(2,1)S(1)}, bf16[512,512]{1,0:T(8,128)(2,1)S(1)}, bf16[384,512]{1,0:T(8,128)(2,1)S(1)}, bf16[192,512]{1,0:T(8,128)(2,1)...) custom-call(s32[4,8]{1,0:T(4,128)S(1)} %copy-done.23, s32[4,12,3]{2,1,0:T(8,128)S(1)} %copy.13.ti, ...), custom_call_target="tpu_custom_call" | custom-call | tf_op jit(solution)/shard_map/edge_cov/pallas_call | solution.py:19
  90.3 0.0 copy-start.5
  90.4 0.8 copy-done.5
  91.1 1.4 %inner_step.1 = (bf16[8,48,512]{2,1,0:T(8,128)(2,1)}, f32[384,512]{1,0:T(8,128)S(1)}) custom-call(f32[1]{0:T(128)S(6)} %copy.17.el, f32[1]{0:T(128)S(6)} %copy.18.eh, bf16[512,512]{1,0:T(8,128)(2,1)S(1)} %get-tuple-element.73.s1_ref, bf16[512,512]{1,0:T(8,128)(2,1)S(1)} %get-tuple-element.74.s2_ref, bf16[512,512]{1,0:T(8,128)(2,1)S(1)} %get-tuple-element.75.ce_ref, ...), custom_call_target="tpu_custom_call" | custom-call | tf_op jit(solution)/shard_map/inner_step/pallas_call | solution.py:19
  92.5 4.0 %all-to-all-start.1 = ((bf16[8,48,512]{2,1,0:T(8,128)(2,1)}), bf16[8,48,512]{2,1,0:T(8,128)(2,1)S(1)}, u32[]{:S(2)}, u32[]{:S(2)}) async-start(bf16[8,48,512]{2,1,0:T(8,128)(2,1)} %get-tuple-element.80), calls=%async_computation.1 | async-start | bytes 786432 | tf_op jit(solution)/shard_map/all_to_all | solution.py:340
  96.5 1.3 collective-permute-start.22
  97.8 2.8 %collective-permute-start.20 = (bf16[384,512]{1,0:T(8,128)(2,1)S(1)}, bf16[384,512]{1,0:T(8,128)(2,1)S(1)}, u32[]{:S(2)}, u32[]{:S(2)}) collective-permute-start(bf16[384,512]{1,0:T(8,128)(2,1)S(1)} %get-tuple-element.70.d1_ref), channel_id=1, source_target_pairs={{0,1},{1,0},{2,3},{3,2},{4,5},{5,4},{6,7},{7,6},{8,9},{9,8},{10,11... | collective-permute-start | bytes 1179656 | tf_op jit(solution)/shard_map/ppermute | solution.py:193
  100.6 0.7 collective-permute-start.21
  101.3 4.5 %collective-permute-done.22 = bf16[192,512]{1,0:T(8,128)(2,1)S(1)} collective-permute-done((bf16[192,512]{1,0:T(8,128)(2,1)S(1)}, bf16[192,512]{1,0:T(8,128)(2,1)S(1)}, u32[]{:S(2)}, u32[]{:S(2)}) %collective-permute-start.22) | collective-permute-done | bytes 196640 | tf_op jit(solution)/shard_map/ppermute | solution.py:191
  105.7 1.5 %collective-permute-start.23 = (bf16[192,512]{1,0:T(8,128)(2,1)S(1)}, bf16[192,512]{1,0:T(8,128)(2,1)S(1)}, u32[]{:S(2)}, u32[]{:S(2)}) collective-permute-start(bf16[192,512]{1,0:T(8,128)(2,1)S(1)} %collective-permute-done.22), channel_id=1, source_target_pairs={{3,2},{0,1},{7,6},{4,5},{11,10},{8,9},{15,14},{12,13},{19,18},{16,... | collective-permute-start | bytes 589832 | tf_op jit(solution)/shard_map/ppermute | solution.py:194
  107.2 6.3 %collective-permute-done.23.dh = bf16[192,512]{1,0:T(8,128)(2,1)S(1)} collective-permute-done((bf16[192,512]{1,0:T(8,128)(2,1)S(1)}, bf16[192,512]{1,0:T(8,128)(2,1)S(1)}, u32[]{:S(2)}, u32[]{:S(2)}) %collective-permute-start.23) | collective-permute-done | bytes 196640 | tf_op jit(solution)/shard_map/ppermute | solution.py:194
  113.6 1.0 copy-done.6
  114.6 0.6 outer_step.1
  115.2 17.1 %all_to_all.10.a1 = bf16[8,48,512]{2,1,0:T(8,128)(2,1)S(1)} all-to-all(bf16[8,48,512]{2,1,0:T(8,128)(2,1)S(1)} %outer_step.1), channel_id=1, replica_groups=mesh['mem'=8,'lat'=4] {'mem'}, dimensions={0} | all-to-all | bytes 786432 | tf_op jit(solution)/shard_map/all_to_all | solution.py:341
  132.3 1.7 %unpack.1 = f32[48,6144]{1,0:T(8,128)} custom-call(s32[4,8]{1,0:T(4,128)S(1)} %copy-done.23, f32[1]{0:T(128)S(6)} %copy.17.el, f32[1]{0:T(128)S(6)} %copy.18.eh, f32[48,6144]{1,0:T(8,128)S(1)} %copy-done.3, bf16[8,48,512]{2,1,0:T(8,128)(2,1)S(1)} %all_to_all.10.a1, bf16[8,48,512]{2,1,0:T(8,128)(2,1)S(1)} %all-to-all-done.1.a2), custom_call_target="tpu_custom_call" | custom-call | tf_op jit(solution)/shard_map/unpack/pallas_call | solution.py:19
  (53 shorter events, 0.1 us)
Async XLA Ops:
  0.0 1.3 copy-start
  1.3 1.3 copy-start.2
  2.5 0.7 copy-start.22
  3.2 26.4 %copy-start.1 = (f32[48,6144]{1,0:T(8,128)S(1)}, f32[48,6144]{1,0:T(8,128)}, u32[]{:S(2)}) copy-start(f32[48,6144]{1,0:T(8,128)} %eq.5) | copy-start | bytes 3538948
  3.2 26.4 %copy-start.23 = (s32[4,8]{1,0:T(4,128)S(1)}, s32[4,8]{1,0:T(4,128)}, u32[]{:S(2)}) copy-start(s32[4,8]{1,0:T(4,128)} %rb.11) | copy-start | bytes 388
  4.2 25.4 %collective-permute-start = (f32[8,48,512]{2,1,0:T(8,128)S(1)}, f32[8,48,512]{2,1,0:T(8,128)S(1)}, u32[]{:S(2)}, u32[]{:S(2)}) collective-permute-start(f32[8,48,512]{2,1,0:T(8,128)S(1)} %get-tuple-element.44), channel_id=1, source_target_pairs={{0,4},{4,0},{8,12},{12,8},{16,20},{20,16},{24,28},{28,24},{1,5},{5... | collective-permute-start | bytes 2359304 | tf_op jit(solution)/shard_map/ppermute | solution.py:119
  4.7 2.2 %collective-permute-start.8 = (bf16[4,48,512]{2,1,0:T(8,128)(2,1)S(1)}, bf16[4,48,512]{2,1,0:T(8,128)(2,1)S(1)}, u32[]{:S(2)}, u32[]{:S(2)}) collective-permute-start(bf16[4,48,512]{2,1,0:T(8,128)(2,1)S(1)} %get-tuple-element.53), channel_id=1, source_target_pairs={{0,4},{4,0},{8,12},{12,8},{16,20},{20,16},{24,28},{28,24},{1,5},{5... | collective-permute-start | bytes 589832 | tf_op jit(solution)/shard_map/ppermute | solution.py:119
  4.8 27.8 %collective-permute-start.16 = (bf16[4,48,512]{2,1,0:T(8,128)(2,1)S(1)}, bf16[4,48,512]{2,1,0:T(8,128)(2,1)S(1)}, u32[]{:S(2)}, u32[]{:S(2)}) collective-permute-start(bf16[4,48,512]{2,1,0:T(8,128)(2,1)S(1)} %get-tuple-element.62), channel_id=1, source_target_pairs={{0,4},{4,0},{8,12},{12,8},{16,20},{20,16},{24,28},{28,24},{1,5},{5... | collective-permute-start | bytes 589832 | tf_op jit(solution)/shard_map/ppermute | solution.py:119
  7.0 23.6 %collective-permute-start.9 = (bf16[96,512]{1,0:T(8,128)(2,1)S(1)}, bf16[96,512]{1,0:T(8,128)(2,1)S(1)}, u32[]{:S(2)}, u32[]{:S(2)}) collective-permute-start(bf16[96,512]{1,0:T(8,128)(2,1)S(1)} %get-tuple-element.55), channel_id=1, source_target_pairs={{0,8},{4,12},{8,0},{12,4},{16,24},{20,28},{24,16},{28,20},{1,9},{5... | collective-permute-start | bytes 294920 | tf_op jit(solution)/shard_map/ppermute | solution.py:124
  10.0 20.6 %collective-permute-start.10 = (bf16[96,512]{1,0:T(8,128)(2,1)S(1)}, bf16[96,512]{1,0:T(8,128)(2,1)S(1)}, u32[]{:S(2)}, u32[]{:S(2)}) collective-permute-start(bf16[96,512]{1,0:T(8,128)(2,1)S(1)} %get-tuple-element.56), channel_id=1, source_target_pairs={{0,16},{4,20},{8,24},{12,28},{16,0},{20,4},{24,8},{28,12},{1,17},{... | collective-permute-start | bytes 294920 | tf_op jit(solution)/shard_map/ppermute | solution.py:124
  12.6 18.0 %collective-permute-start.11 = (bf16[96,512]{1,0:T(8,128)(2,1)S(1)}, bf16[96,512]{1,0:T(8,128)(2,1)S(1)}, u32[]{:S(2)}, u32[]{:S(2)}) collective-permute-start(bf16[96,512]{1,0:T(8,128)(2,1)S(1)} %get-tuple-element.57), channel_id=1, source_target_pairs={{0,24},{4,28},{8,16},{12,20},{16,8},{20,12},{24,0},{28,4},{1,25},{... | collective-permute-start | bytes 294920 | tf_op jit(solution)/shard_map/ppermute | solution.py:124
  30.4 5.7 %collective-permute-start.1 = (bf16[96,512]{1,0:T(8,128)(2,1)S(1)}, bf16[96,512]{1,0:T(8,128)(2,1)S(1)}, u32[]{:S(2)}, u32[]{:S(2)}) collective-permute-start(bf16[96,512]{1,0:T(8,128)(2,1)S(1)} %get-tuple-element.46), channel_id=1, source_target_pairs={{0,8},{4,12},{8,0},{12,4},{16,24},{20,28},{24,16},{28,20},{1,9},{5... | collective-permute-start | bytes 294920 | tf_op jit(solution)/shard_map/ppermute | solution.py:124
  30.6 21.3 %collective-permute-start.13 = (bf16[192,512]{1,0:T(8,128)(2,1)S(1)}, bf16[192,512]{1,0:T(8,128)(2,1)S(1)}, u32[]{:S(2)}, u32[]{:S(2)}) collective-permute-start(bf16[192,512]{1,0:T(8,128)(2,1)S(1)} %get-tuple-element.59), channel_id=1, source_target_pairs={{1,2},{2,1},{5,6},{6,5},{9,10},{10,9},{13,14},{14,13},{17,18},{18,... | collective-permute-start | bytes 589832 | tf_op jit(solution)/shard_map/ppermute | solution.py:192
  31.3 22.1 %collective-permute-start.14 = (bf16[192,512]{1,0:T(8,128)(2,1)S(1)}, bf16[192,512]{1,0:T(8,128)(2,1)}, u32[]{:S(2)}, u32[]{:S(2)}) collective-permute-start(bf16[192,512]{1,0:T(8,128)(2,1)S(1)} %get-tuple-element.60), channel_id=1, source_target_pairs={{1,3},{2,0},{5,7},{6,4},{9,11},{10,8},{13,15},{14,12},{17,19},{18,... | collective-permute-start | bytes 589832 | tf_op jit(solution)/shard_map/ppermute | solution.py:191
  32.6 42.7 %copy-start.25 = (s32[4,12,3]{1,0,2:T(4,128)S(1)}, s32[4,12,3]{1,0,2:T(4,128)}, u32[]{:S(2)}) copy-start(s32[4,12,3]{1,0,2:T(4,128)} %param.15) | copy-start | bytes 1732
  32.6 42.8 %copy-start.4 = (bf16[2,512,512]{2,1,0:T(8,128)(2,1)S(1)}, bf16[2,512,512]{2,1,0:T(8,128)(2,1)}, u32[]{:S(2)}) copy-start(bf16[2,512,512]{2,1,0:T(8,128)(2,1)} %tt.3) | copy-start | bytes 3145732
  32.6 42.8 %copy-start.21 = (f32[6144]{0:T(1024)S(1)}, f32[6144]{0:T(1024)}, u32[]{:S(2)}) copy-start(f32[6144]{0:T(1024)} %param.11) | copy-start | bytes 73732
  32.6 42.8 %copy-start.24 = (s32[4,12]{1,0:T(4,128)S(1)}, s32[4,12]{1,0:T(4,128)}, u32[]{:S(2)}) copy-start(s32[4,12]{1,0:T(4,128)} %pm.1) | copy-start | bytes 580
  33.5 41.2 %copy-start.13 = (bf16[192,512]{1,0:T(8,128)(2,1)}, bf16[192,512]{1,0:T(8,128)(2,1)S(1)}, u32[]{:S(2)}) copy-start(bf16[192,512]{1,0:T(8,128)(2,1)S(1)} %get-tuple-element.63.refs_0_) | copy-start | bytes 589828
  33.5 21.2 %collective-permute-start.17 = (bf16[192,512]{1,0:T(8,128)(2,1)S(1)}, bf16[192,512]{1,0:T(8,128)(2,1)S(1)}, u32[]{:S(2)}, u32[]{:S(2)}) collective-permute-start(bf16[192,512]{1,0:T(8,128)(2,1)S(1)} %get-tuple-element.64), channel_id=1, source_target_pairs={{0,8},{4,12},{8,0},{12,4},{16,24},{20,28},{24,16},{28,20},{1,9},{5... | collective-permute-start | bytes 589832 | tf_op jit(solution)/shard_map/ppermute | solution.py:124
  35.5 10.7 %collective-permute-start.2 = (bf16[96,512]{1,0:T(8,128)(2,1)S(1)}, bf16[96,512]{1,0:T(8,128)(2,1)S(1)}, u32[]{:S(2)}, u32[]{:S(2)}) collective-permute-start(bf16[96,512]{1,0:T(8,128)(2,1)S(1)} %get-tuple-element.47), channel_id=1, source_target_pairs={{0,16},{4,20},{8,24},{12,28},{16,0},{20,4},{24,8},{28,12},{1,17},{... | collective-permute-start | bytes 294920 | tf_op jit(solution)/shard_map/ppermute | solution.py:124
  36.1 14.7 %collective-permute-start.3 = (bf16[96,512]{1,0:T(8,128)(2,1)S(1)}, bf16[96,512]{1,0:T(8,128)(2,1)S(1)}, u32[]{:S(2)}, u32[]{:S(2)}) collective-permute-start(bf16[96,512]{1,0:T(8,128)(2,1)S(1)} %get-tuple-element.48), channel_id=1, source_target_pairs={{0,24},{4,28},{8,16},{12,20},{16,8},{20,12},{24,0},{28,4},{1,25},{... | collective-permute-start | bytes 294920 | tf_op jit(solution)/shard_map/ppermute | solution.py:124
  46.3 36.9 %collective-permute-start.12 = (bf16[384,512]{1,0:T(8,128)(2,1)S(1)}, bf16[384,512]{1,0:T(8,128)(2,1)S(1)}, u32[]{:S(2)}, u32[]{:S(2)}) collective-permute-start(bf16[384,512]{1,0:T(8,128)(2,1)S(1)} %get-tuple-element.58.r1_ref), channel_id=1, source_target_pairs={{0,1},{1,0},{2,3},{3,2},{4,5},{5,4},{6,7},{7,6},{8,9},{9,8},{10,11... | collective-permute-start | bytes 1179656 | tf_op jit(solution)/shard_map/ppermute | solution.py:193
  50.9 13.1 %collective-permute-start.18 = (bf16[192,512]{1,0:T(8,128)(2,1)S(1)}, bf16[192,512]{1,0:T(8,128)(2,1)S(1)}, u32[]{:S(2)}, u32[]{:S(2)}) collective-permute-start(bf16[192,512]{1,0:T(8,128)(2,1)S(1)} %get-tuple-element.65), channel_id=1, source_target_pairs={{0,16},{4,20},{8,24},{12,28},{16,0},{20,4},{24,8},{28,12},{1,17},{... | collective-permute-start | bytes 589832 | tf_op jit(solution)/shard_map/ppermute | solution.py:124
  51.9 16.0 %collective-permute-start.19 = (bf16[192,512]{1,0:T(8,128)(2,1)S(1)}, bf16[192,512]{1,0:T(8,128)(2,1)S(1)}, u32[]{:S(2)}, u32[]{:S(2)}) collective-permute-start(bf16[192,512]{1,0:T(8,128)(2,1)S(1)} %get-tuple-element.66), channel_id=1, source_target_pairs={{0,24},{4,28},{8,16},{12,20},{16,8},{20,12},{24,0},{28,4},{1,25},{... | collective-permute-start | bytes 589832 | tf_op jit(solution)/shard_map/ppermute | solution.py:124
  53.4 16.0 %collective-permute-start.6 = (bf16[192,512]{1,0:T(8,128)(2,1)S(1)}, bf16[192,512]{1,0:T(8,128)(2,1)}, u32[]{:S(2)}, u32[]{:S(2)}) collective-permute-start(bf16[192,512]{1,0:T(8,128)(2,1)S(1)} %get-tuple-element.51), channel_id=1, source_target_pairs={{1,3},{2,0},{5,7},{6,4},{9,11},{10,8},{13,15},{14,12},{17,19},{18,... | collective-permute-start | bytes 589832 | tf_op jit(solution)/shard_map/ppermute | solution.py:191
  54.7 0.7 copy-start.15
  55.3 28.5 %collective-permute-start.4 = (bf16[384,512]{1,0:T(8,128)(2,1)S(1)}, bf16[384,512]{1,0:T(8,128)(2,1)S(1)}, u32[]{:S(2)}, u32[]{:S(2)}) collective-permute-start(bf16[384,512]{1,0:T(8,128)(2,1)S(1)} %get-tuple-element.49.p1_ref), channel_id=1, source_target_pairs={{0,1},{1,0},{2,3},{3,2},{4,5},{5,4},{6,7},{7,6},{8,9},{9,8},{10,11... | collective-permute-start | bytes 1179656 | tf_op jit(solution)/shard_map/ppermute | solution.py:193
  63.9 0.7 copy-start.17
  64.6 17.9 %collective-permute-start.15 = (bf16[192,512]{1,0:T(8,128)(2,1)}, bf16[192,512]{1,0:T(8,128)(2,1)S(1)}, u32[]{:S(2)}, u32[]{:S(2)}) collective-permute-start(bf16[192,512]{1,0:T(8,128)(2,1)} %collective-permute-done.14), channel_id=1, source_target_pairs={{3,2},{0,1},{7,6},{4,5},{11,10},{8,9},{15,14},{12,13},{19,18},{16,... | collective-permute-start | bytes 589832 | tf_op jit(solution)/shard_map/ppermute | solution.py:194
  68.0 0.7 copy-start.19
  68.7 14.5 %collective-permute-start.5 = (bf16[192,512]{1,0:T(8,128)(2,1)}, bf16[192,512]{1,0:T(8,128)(2,1)S(1)}, u32[]{:S(2)}, u32[]{:S(2)}) collective-permute-start(bf16[192,512]{1,0:T(8,128)(2,1)} %get-tuple-element.50), channel_id=1, source_target_pairs={{1,2},{2,1},{5,6},{6,5},{9,10},{10,9},{13,14},{14,13},{17,18},{18,... | collective-permute-start | bytes 589832 | tf_op jit(solution)/shard_map/ppermute | solution.py:192
  69.3 14.5 %collective-permute-start.7 = (bf16[192,512]{1,0:T(8,128)(2,1)}, bf16[192,512]{1,0:T(8,128)(2,1)}, u32[]{:S(2)}, u32[]{:S(2)}) collective-permute-start(bf16[192,512]{1,0:T(8,128)(2,1)} %collective-permute-done.6), channel_id=1, source_target_pairs={{3,2},{0,1},{7,6},{4,5},{11,10},{8,9},{15,14},{12,13},{19,18},{16,... | collective-permute-start | bytes 589832 | tf_op jit(solution)/shard_map/ppermute | solution.py:194
  75.4 0.9 copy-start.14
  76.4 0.9 copy-start.16
  77.3 0.9 copy-start.18
  78.2 0.9 copy-start.20
  82.5 0.7 copy-start.9
  83.2 0.7 copy-start.11
  83.9 0.7 copy-start.7
  84.6 1.0 copy-start.8
  85.6 0.9 copy-start.10
  86.6 0.9 copy-start.12
  90.3 0.8 copy-start.5
  92.5 22.7 %all-to-all-start.1 = ((bf16[8,48,512]{2,1,0:T(8,128)(2,1)}), bf16[8,48,512]{2,1,0:T(8,128)(2,1)S(1)}, u32[]{:S(2)}, u32[]{:S(2)}) async-start(bf16[8,48,512]{2,1,0:T(8,128)(2,1)} %get-tuple-element.80), calls=%async_computation.1 | async-start | bytes 786432 | tf_op jit(solution)/shard_map/all_to_all | solution.py:340
  96.5 9.2 %collective-permute-start.22 = (bf16[192,512]{1,0:T(8,128)(2,1)S(1)}, bf16[192,512]{1,0:T(8,128)(2,1)S(1)}, u32[]{:S(2)}, u32[]{:S(2)}) collective-permute-start(bf16[192,512]{1,0:T(8,128)(2,1)S(1)} %get-tuple-element.72), channel_id=1, source_target_pairs={{1,3},{2,0},{5,7},{6,4},{9,11},{10,8},{13,15},{14,12},{17,19},{18,... | collective-permute-start | bytes 589832 | tf_op jit(solution)/shard_map/ppermute | solution.py:191
  97.8 15.7 %collective-permute-start.20 = (bf16[384,512]{1,0:T(8,128)(2,1)S(1)}, bf16[384,512]{1,0:T(8,128)(2,1)S(1)}, u32[]{:S(2)}, u32[]{:S(2)}) collective-permute-start(bf16[384,512]{1,0:T(8,128)(2,1)S(1)} %get-tuple-element.70.d1_ref), channel_id=1, source_target_pairs={{0,1},{1,0},{2,3},{3,2},{4,5},{5,4},{6,7},{7,6},{8,9},{9,8},{10,11... | collective-permute-start | bytes 1179656 | tf_op jit(solution)/shard_map/ppermute | solution.py:193
  100.6 6.7 %collective-permute-start.21 = (bf16[192,512]{1,0:T(8,128)(2,1)S(1)}, bf16[192,512]{1,0:T(8,128)(2,1)S(1)}, u32[]{:S(2)}, u32[]{:S(2)}) collective-permute-start(bf16[192,512]{1,0:T(8,128)(2,1)S(1)} %get-tuple-element.71), channel_id=1, source_target_pairs={{1,2},{2,1},{5,6},{6,5},{9,10},{10,9},{13,14},{14,13},{17,18},{18,... | collective-permute-start | bytes 589832 | tf_op jit(solution)/shard_map/ppermute | solution.py:192
  105.7 7.8 %collective-permute-start.23 = (bf16[192,512]{1,0:T(8,128)(2,1)S(1)}, bf16[192,512]{1,0:T(8,128)(2,1)S(1)}, u32[]{:S(2)}, u32[]{:S(2)}) collective-permute-start(bf16[192,512]{1,0:T(8,128)(2,1)S(1)} %collective-permute-done.22), channel_id=1, source_target_pairs={{3,2},{0,1},{7,6},{4,5},{11,10},{8,9},{15,14},{12,13},{19,18},{16,... | collective-permute-start | bytes 589832 | tf_op jit(solution)/shard_map/ppermute | solution.py:194
  113.6 1.0 copy-start.6
  114.6 17.7 %copy-start.3 = (f32[48,6144]{1,0:T(8,128)S(1)}, f32[48,6144]{1,0:T(8,128)}, u32[]{:S(2)}) copy-start(f32[48,6144]{1,0:T(8,128)} %inn.3) | copy-start | bytes 3538948

commit v2 on v1

v2 whole, which is shorter than its diff:
```python
import math

import jax
import jax.numpy as jnp
from jax import lax
from jax.experimental import pallas as pl
from jax.experimental.pallas import tpu as pltpu
from jax.sharding import PartitionSpec as P

BF = jnp.bfloat16
F32 = jnp.float32
VMEM_LIMIT = 12 * 1024 * 1024

SMEM_SPEC = pl.BlockSpec(memory_space=pltpu.SMEM)
VMEM_SPEC = pl.BlockSpec(memory_space=pltpu.VMEM)
ANY_SPEC = pl.BlockSpec(memory_space=pl.ANY)
HBM_SPEC = pl.BlockSpec(memory_space=pltpu.HBM)


def kernel_call(body, outs, scalars, arrays, scratch=(), name=None, array_spec=VMEM_SPEC, after=(), vmem=VMEM_LIMIT):
    used, unread = len(scalars) + len(arrays), len(after)
    moved = sum(a.size * a.dtype.itemsize for a in arrays)
    moved += sum(jnp.dtype(d).itemsize * math.prod(s) for s, d in outs)

    def run(*refs):
        body(*refs[:used], *refs[used + unread :])

    return pl.pallas_call(
        run,
        out_shape=tuple(jax.ShapeDtypeStruct(s, d) for s, d in outs),
        in_specs=[SMEM_SPEC] * len(scalars) + [array_spec] * len(arrays) + [ANY_SPEC] * unread,
        out_specs=tuple(VMEM_SPEC for _ in outs),
        scratch_shapes=list(scratch),
        compiler_params=pltpu.CompilerParams(vmem_limit_bytes=vmem),
        cost_estimate=pl.CostEstimate(flops=3 * 10**9, bytes_accessed=3 * 10**7, transcendentals=0),
        name=name,
    )(*scalars, *arrays, *after)


def gate(x, after):
    def nothing(*refs):
        del refs

    return pl.pallas_call(
        nothing,
        out_shape=jax.ShapeDtypeStruct(x.shape, x.dtype),
        in_specs=[ANY_SPEC] * (1 + len(after)),
        out_specs=ANY_SPEC,
        input_output_aliases={0: 0},
        compiler_params=pltpu.CompilerParams(vmem_limit_bytes=1024 * 1024),
        name="gate",
    )(x, *after)


def dot_nn(a, b):
    return lax.dot_general(a, b, (((1,), (0,)), ((), ())), preferred_element_type=F32)


def dot_nt(a, b):
    return lax.dot_general(a, b, (((1,), (1,)), ((), ())), preferred_element_type=F32)


def dot_tn(a, b):
    return lax.dot_general(a, b, (((0,), (0,)), ((), ())), preferred_element_type=F32)


def region_start(rb, band, m):
    return lax.fori_loop(0, m, lambda i, acc: acc + rb[band, i], jnp.int32(0))


def block_cols(block, width):
    return pl.ds(pl.multiple_of(block * width, width), width)


def chebyshev(low, high, width):
    low = jnp.full((1, width), low, F32)
    high = jnp.full((1, width), high, F32)
    centre = 0.5 * (high + low)
    half = 0.5 * (high - low)
    s = centre / half
    q0 = 1.0 / s
    q1 = 1.0 / (2.0 * s - q0)
    q2 = 1.0 / (2.0 * s - q1)
    inv_c = 1.0 / centre
    keep1, gain1 = q1 * q0, 2.0 * q1 / half
    keep2, gain2 = q2 * q1, 2.0 * q2 / half
    return inv_c, keep1, gain1, keep2, gain2


def on_device(
    equivalents,
    innovations,
    obs_var,
    taper_tiles,
    region_blocks,
    pair_mask,
    taper_index,
    eig_low,
    eig_high,
):
    n = lax.axis_size("mem")
    n_lat = lax.axis_size("lat")
    chips = n // 2
    rows, cols = equivalents.shape
    B = taper_tiles.shape[1]
    nb = cols // B
    members = rows * n
    inv_scale = (members - 1) ** (-0.5)
    rp = -(-rows // 16) * 16
    mp = rp * n
    half = mp // 2

    def put_rows(ref_set, lo, value):
        ref_set(slice(lo, lo + rows), value)
        if rp > rows:
            ref_set(slice(lo + rows, lo + rp), jnp.zeros((rp - rows, B), value.dtype))

    tail_rows = 16
    msg = 2 * rp + tail_rows

    def mean_rows(x, offset):
        mean = jnp.sum(x, axis=0, keepdims=True) * (1.0 / rows)
        high = mean.astype(BF).astype(F32)
        mid = (mean - high).astype(BF).astype(F32)
        row = lax.broadcasted_iota(jnp.int32, (tail_rows, B), 0)
        tail = jnp.where(row == offset + 2, mean - high - mid, 0.0)
        tail = jnp.where(row == offset + 1, mid, tail)
        tail = jnp.where(row == offset, high, tail)
        return mean, tail.astype(BF)

    def blocks(rb, extra):
        me, band = lax.axis_index("mem"), lax.axis_index("lat")
        return [
            block_cols(jnp.minimum(region_start(rb, band, me ^ i) + extra, nb - 1), B) for i in range(n)
        ]

    def fill_p(own, oth, at_row, rb, eq, extra):
        for i, at in enumerate(blocks(rb, extra)):
            k, j = i // 2, i % 2
            out = oth if j else own
            x = eq[:, at]
            mean, tail = mean_rows(x, 8 * j)
            put = lambda s, v: out.__setitem__((k, s), v)
            put_rows(put, at_row, ((x - mean) * inv_scale).astype(BF))
            out[k, at_row + rp : at_row + rp + tail_rows, :] = tail

    def fill_r(own, oth, rb, inn, extra):
        for i, at in enumerate(blocks(rb, extra)):
            out = oth if i % 2 else own
            put_rows(lambda s, v: out.__setitem__((i // 2, s), v), 0, inn[:, at].astype(BF))

    def pack_first_body(rb_hbm, eq_hbm, inn_hbm, own, oth, eq, inn, rb, sems):
        copies = [
            pltpu.make_async_copy(src, dst, sems.at[i])
            for i, (src, dst) in enumerate(((rb_hbm, rb), (inn_hbm, inn), (eq_hbm, eq)))
        ]
        for copy in copies:
            copy.start()
        copies[0].wait()
        copies[1].wait()
        fill_r(own, oth, rb, inn, 0)
        copies[2].wait()
        fill_p(own, oth, rp, rb, eq, 0)

    slot_outs = [((chips, msg, B), BF)] * 2
    own1, oth1 = kernel_call(
        pack_first_body,
        slot_outs,
        [],
        [region_blocks, equivalents, innovations],
        scratch=[
            pltpu.VMEM((rows, cols), F32),
            pltpu.VMEM((rows, cols), F32),
            pltpu.SMEM(region_blocks.shape, jnp.int32),
            pltpu.SemaphoreType.DMA((3,)),
        ],
        name="pack_first",
        array_spec=HBM_SPEC,
        vmem=60 * 1024 * 1024,
    )
    oth1 = lax.ppermute(oth1, "mem", [(i, i ^ 1) for i in range(n)])

    def pack_second_body(rb, eq, inn, own, oth):
        fill_r(own, oth, rb, inn, 1)
        fill_p(own, oth, rp, rb, eq, 1)

    own2, oth2 = kernel_call(
        pack_second_body,
        slot_outs,
        [region_blocks],
        [equivalents, innovations],
        name="pack_second",
        after=[own1],
    )

    core_pairs = [(i, i ^ 1) for i in range(n)]

    def swap_core(x):
        return lax.ppermute(x, "mem", core_pairs)

    def z_exchange(parts, order):
        got = list(parts)
        for k in order:
            got[k] = lax.ppermute(parts[k], "mem", [(i, i ^ (2 * k)) for i in range(n)])
        return got

    far_first = list(range(1, chips))[::-1]
    step = 2 * rp

    def join_body(own, oth, *outs):
        for k in range(chips):
            out = outs[k]
            out[0:rp, :] = own[k, rp:step, :]
            out[rp:step, :] = oth[k, rp:step, :]
            out[step:msg, :] = own[k, step:msg, :] + oth[k, step:msg, :]
            out[msg : msg + rp, :] = own[k, 0:rp, :]
            out[msg + rp : msg + step, :] = oth[k, 0:rp, :]

    def join(own, oth, name, after=()):
        return kernel_call(
            join_body, [((msg + step, B), BF)] * chips, [], [own, oth], name=name, after=after
        )

    m1_got = z_exchange(join(own1, oth1, "join_first"), far_first)
    m2_parts = join(own2, swap_core(oth2), "join_second")
    m2_got = z_exchange(m2_parts, far_first)

    def corrected(pieces):
        mean = sum(m for _, m in pieces) * (1.0 / n)
        out = []
        for x, m in pieces:
            x = x.astype(F32) + (m - mean) * inv_scale
            if rp > rows:
                x = jnp.where(lax.broadcasted_iota(jnp.int32, (rp, B), 0) < rows, x, 0.0)
            out.append(x.astype(BF))
        return out

    odd = range(1, n_lat - 1, 2)
    pair_list = [(i, i ^ 1) for i in range(n_lat)]
    skew_list = [(i, i + 1) for i in odd] + [(i + 1, i) for i in odd]
    hop1_list = [(i, i + 2) for i in odd] + [(i + 1, i - 1) for i in odd]
    hop2_list = [(i + 2, i + 1) for i in odd] + [(i - 1, i) for i in odd]

    def lat_exchange(both, low, high, after=()):
        relay = lax.ppermute(high, "lat", hop1_list)
        pair = lax.ppermute(both, "lat", pair_list)
        skew_low = lax.ppermute(low, "lat", skew_list)
        skew_high = lax.ppermute(gate(relay, after) if after else relay, "lat", hop2_list)
        return pair, skew_low, skew_high

    block_out = ((mp, B), BF)
    half_out = ((half, B), BF)

    def group_rows(part):
        tail = part[step:msg, :].astype(F32)
        return [
            (part[j * rp : (j + 1) * rp, :], jnp.sum(tail[8 * j : 8 * j + 8, :], axis=0, keepdims=True))
            for j in range(2)
        ]

    def owner_body(*refs):
        parts, (both, low, high) = refs[:chips], refs[chips:]

        def put(lo, i, value):
            both[lo * 2 + i * rp : lo * 2 + (i + 1) * rp, :] = value
            out, at = (low, lo + i * rp) if i < chips else (high, lo + (i - chips) * rp)
            out[at : at + rp, :] = value

        for i in range(n):
            at = msg + (i % 2) * rp
            put(half, i, parts[i // 2][at : at + rp, :])
        for i, x in enumerate(corrected([g for part in parts for g in group_rows(part)])):
            put(0, i, x)

    both_out = ((2 * mp, B), BF)
    first, first_low, first_high = kernel_call(
        owner_body, [both_out, block_out, block_out], [], m1_got, name="owner_first", after=[m2_parts[0]]
    )
    pair, skew_low, skew_high = lat_exchange(first, first_low, first_high, after=[m2_got[1]])

    var_row = obs_var.reshape(1, cols)

    def whole(low, high):
        return jnp.concatenate([low[...], high[...]], axis=0)

    mat = ((B, B), BF)
    field = ((mp, B), F32)
    half_field = ((half, B), F32)

    def self_cov(tt, index, pv):
        tile = tt[index].astype(F32)
        tile = 0.5 * (tile + tile.T)
        return (tile * dot_tn(pv, pv)).astype(BF)

    def first_body(rb, ti, tt, first_ref, s1, z1):
        me, band = lax.axis_index("mem"), lax.axis_index("lat")
        first = region_start(rb, band, me)
        s1[...] = self_cov(tt, ti[band, first, 0], first_ref[0:mp, :])
        z1[...] = dot_nn(first_ref[mp:, :], s1[...])

    s1, z1 = kernel_call(
        first_body,
        [mat, field],
        [region_blocks, taper_index],
        [taper_tiles, first],
        name="first_cov",
    )

    def east_body(rb, pm, ti, tt, first_ref, *refs):
        parts, (z1_ref, ce, z1, p2, r2) = refs[:chips], refs[chips:]
        me, band = lax.axis_index("mem"), lax.axis_index("lat")
        first = region_start(rb, band, me)
        for k in range(chips):
            r2[k * step : (k + 1) * step, :] = parts[k][msg : msg + step, :]
        for i, x in enumerate(corrected([g for part in parts for g in group_rows(part)])):
            p2[i * rp : (i + 1) * rp, :] = x
        active = ((rb[band, me] > 1) & (pm[band, first] == 1)).astype(F32)
        tile_east = tt[ti[band, first, 1]].astype(F32) * active
        ce[...] = (tile_east * dot_tn(first_ref[0:mp, :], p2[...])).astype(BF)
        z1[...] = z1_ref[...] + dot_nt(r2[...], ce[...])

    ce, z1, p2, r2 = kernel_call(
        east_body,
        [mat, field, block_out, block_out],
        [region_blocks, pair_mask, taper_index],
        [taper_tiles, first, *m2_got, z1],
        name="east_cov",
    )

    def edge_body(rb, ti, tt, first_ref, pair_ref, sl, sh, qp, qs):
        me, band = lax.axis_index("mem"), lax.axis_index("lat")
        first = region_start(rb, band, me)
        below = jnp.maximum(band - 1, 0)
        first_below = region_start(rb, below, me)
        even = lax.rem(band, 2) == 0
        tile_up = tt[ti[band, first, 2]].astype(F32).T
        tile_down = tt[ti[below, first_below, 2]].astype(F32)
        p1v = first_ref[0:mp, :]
        skew = jnp.concatenate([sl[0:half, :], sh[0:half, :]], axis=0)
        qp[...] = (jnp.where(even, tile_up, tile_down) * dot_tn(pair_ref[0:mp, :], p1v)).astype(BF)
        qs[...] = (jnp.where(even, tile_down, tile_up) * dot_tn(skew, p1v)).astype(BF)

    qp, qs = kernel_call(
        edge_body,
        [mat, mat],
        [region_blocks, taper_index],
        [taper_tiles, first, pair, skew_low, skew_high],
        name="edge_cov",
    )

    def direction_body(rb, el, eh, var, qp_ref, qs_ref, first_ref, pair_ref, sl, sh, z1_ref, d1, d1l, d1h, t1):
        me, band = lax.axis_index("mem"), lax.axis_index("lat")
        first = region_start(rb, band, me)
        inv_c, keep1, gain1, keep2, gain2 = chebyshev(el[0], eh[0], B)
        var1 = var[:, block_cols(first, B)]
        skew = jnp.concatenate([sl[half:, :], sh[half:, :]], axis=0)
        prod = z1_ref[...] + dot_nn(pair_ref[mp:, :], qp_ref[...]) + dot_nn(skew, qs_ref[...])
        r1f = first_ref[mp:, :].astype(F32)
        d0 = r1f * inv_c
        res = r1f - (var1 * d0 + prod * inv_c)
        d = keep1 * d0 + gain1 * res
        db = d.astype(BF)
        d1[...] = db
        d1l[...] = db[0:half, :]
        d1h[...] = db[half:mp, :]
        t1[...] = (1.0 + keep2) * d + gain2 * (res - var1 * d)

    d1, d1_low, d1_high, t1 = kernel_call(
        direction_body,
        [block_out, half_out, half_out, field],
        [region_blocks, eig_low, eig_high],
        [var_row, qp, qs, first, pair, skew_low, skew_high, z1],
        name="direction_first",
    )
    d1_pair, d1_skew_low, d1_skew_high = lat_exchange(d1, d1_low, d1_high)

    def inner_body(
        rb, ti, el, eh, tt, var, p2_ref, r2_ref, first_ref, s1_ref, ce_ref, d1_ref, t1_ref, w1, *outs
    ):
        me, band = lax.axis_index("mem"), lax.axis_index("lat")
        second = jnp.minimum(region_start(rb, band, me) + 1, nb - 1)
        inv_c, keep1, gain1, keep2, gain2 = chebyshev(el[0], eh[0], B)
        d1v, r2v, cev = d1_ref[...], r2_ref[...], ce_ref[...]
        s2 = self_cov(tt, ti[band, second, 0], p2_ref[...])
        prod = dot_nn(r2v, s2) + dot_nn(first_ref[mp:, :], cev)
        var2 = var[:, block_cols(second, B)]
        r2f = r2v.astype(F32)
        d0 = r2f * inv_c
        res = r2f - (var2 * d0 + prod * inv_c)
        d2 = keep1 * d0 + gain1 * res
        d2b = d2.astype(BF)
        w1[...] = t1_ref[...] - gain2 * (dot_nn(d1v, s1_ref[...]) + dot_nt(d2b, cev))
        sol = (1.0 + keep2) * d2 + gain2 * (res - var2 * d2 - dot_nn(d2b, s2) - dot_nn(d1v, cev))
        for k in range(chips):
            outs[k][...] = sol[k * step : (k + 1) * step, :].astype(BF)

    w1, *sol2 = kernel_call(
        inner_body,
        [field] + [((step, B), BF)] * chips,
        [region_blocks, taper_index, eig_low, eig_high],
        [taper_tiles, var_row, p2, r2, first, s1, ce, d1, t1],
        name="inner_step",
    )
    sol2 = z_exchange(sol2, far_first)

    def peer_body(*refs):
        for k in range(chips):
            refs[chips][k] = refs[k][rp:step, :]

    (sol2_peer,) = kernel_call(peer_body, [((chips, rp, B), BF)], [], sol2, name="peer_rows")
    sol2_peer = swap_core(sol2_peer)

    def outer_body(el, eh, qp_ref, qs_ref, dp, dsl, dsh, w1_ref, *outs):
        gain2 = chebyshev(el[0], eh[0], B)[4]
        prod = dot_nn(dp[...], qp_ref[...]) + dot_nn(whole(dsl, dsh), qs_ref[...])
        sol = w1_ref[...] - gain2 * prod
        for i in range(n):
            outs[i][...] = sol[i * rp : (i + 1) * rp, :].astype(BF)

    sol1 = kernel_call(
        outer_body,
        [((rp, B), BF)] * n,
        [eig_low, eig_high],
        [qp, qs, d1_pair, d1_skew_low, d1_skew_high, w1],
        name="outer_step",
        after=sol2[1:],
    )
    sol1 = [
        x if i == 0 else lax.ppermute(x, "mem", [(q, q ^ i) for q in range(n)]) for i, x in enumerate(sol1)
    ]

    def unpack_body(rb, el, eh, inn, *refs):
        firsts, seconds, peer, out = refs[:n], refs[n : n + chips], refs[n + chips], refs[-1]
        me, band = lax.axis_index("mem"), lax.axis_index("lat")
        inv_c = chebyshev(el[0], eh[0], B)[0]
        for i in range(n):
            owner = me ^ i
            first = region_start(rb, band, owner)
            at = block_cols(first, B)
            out[:, at] = inn[:, at] * inv_c + firsts[i][0:rows, :].astype(F32)
            second = jnp.minimum(first + 1, nb - 1)

            @pl.when(rb[band, owner] > 1)
            def _(i=i, second=second):
                at2 = block_cols(second, B)
                add = peer[i // 2, 0:rows, :] if i % 2 else seconds[i // 2][0:rows, :]
                out[:, at2] = inn[:, at2] * inv_c + add.astype(F32)

    (out,) = kernel_call(
        unpack_body,
        [((rows, cols), F32)],
        [region_blocks, eig_low, eig_high],
        [innovations, *sol1, *sol2, sol2_peer],
        name="unpack",
    )
    return out


def solution(mesh):
    return jax.shard_map(
        on_device,
        mesh=mesh,
        in_specs=(P("mem", "lat"), P("mem", "lat"), P("lat"), P(), P(), P(), P(), P(), P()),
        out_specs=P("mem", "lat"),
        check_vma=False,
    )
```

time: 135 us -> 102 us (0.76)
  blocking collectives: 34.1 us -> 0 us
  local copies, waits for them, and re-layouts: 16 us -> 1.85 us
  Pallas kernels: 13.2 us -> 20.1 us
  waiting for transfers between devices: 26.1 us -> 30.9 us
  starting transfers between devices: 42.9 us -> 47.2 us
    all_to_all x1 -> x0, blocking collectives: 17.1 us -> none  [on_device(): lax.all_to_all(sol_1, 'mem', split_axis=0, concat_axis=0, tiled=True)]
    all_gather x1 -> x0, blocking collectives: 17 us -> none  [on_device(): sums = lax.all_gather(lsum, 'mem', axis=0, tiled=True)]
    unnamed x54 -> x25, local copies, waits for them, and re-layouts: 16 us -> 1.85 us
    ppermute x9, waiting for transfers between devices: 13.6 us -> 22.3 us  [z_exchange(): got[k] = lax.ppermute(parts[k], 'mem', [(i, i ^ 2 * k) for i in range(n)])]
    ppermute x9, starting transfers between devices: 12 us -> 19.3 us  [z_exchange(): got[k] = lax.ppermute(parts[k], 'mem', [(i, i ^ 2 * k) for i in range(n)])]
    pallas_call x11 -> x14, Pallas kernels: 13.2 us -> 20.1 us  [the longest x13 20.1 us: kernel_call(): pl.pallas_call(run, out_shape=tuple((jax.ShapeDtypeStruct(s, d) for s, d...]
    ppermute x3 -> x2, waiting for transfers between devices: 4.49 us -> 0.01 us  [lat_exchange(): relay = lax.ppermute(high, 'lat', hop1_list)]
    all_to_all x1 -> x0, starting transfers between devices: 4.03 us -> none  [on_device(): lax.all_to_all(sol_2, 'mem', split_axis=0, concat_axis=0, tiled=True)]
  transfers between devices with their start and end apart: 25 -> 27, of which waited for: 5 -> 8; matrix products, arithmetic and copies ran while one was open for 0% -> 0% of each run, Pallas kernels for 5% -> 10%
where the time goes in v2:
time: 102 us
  starting transfers between devices  47.2 us (46%)
  waiting for transfers between devices  30.9 us (30%)
  Pallas kernels  20.1 us (20%)
  local copies, waits for them, and re-layouts  1.85 us (2%)
  between operations  1.6 us (2%)
    ppermute x9, waiting for transfers between devices, z_exchange(): got[k] = lax.ppermute(parts[k], 'mem', [(i, i ^ 2 * k) for i in range(n)])  22.3 us
    pallas_call x13, Pallas kernels, kernel_call(): pl.pallas_call(run, out_shape=tuple((jax.ShapeDtypeStruct(s, d) for s, d...  20.1 us
    ppermute x9, starting transfers between devices, z_exchange(): got[k] = lax.ppermute(parts[k], 'mem', [(i, i ^ 2 * k) for i in range(n)])  19.3 us
    ppermute x2, starting transfers between devices, lat_exchange(): lax.ppermute(gate(relay, after) if after else relay, 'lat', hop2_list)  9.36 us
    ppermute x7, starting transfers between devices, on_device(): lax.ppermute(x, 'mem', [(q, q ^ i) for q in range(n)])  8.5 us
    ppermute x7, waiting for transfers between devices, on_device(): lax.ppermute(x, 'mem', [(q, q ^ i) for q in range(n)])  5.54 us
    ppermute x2, starting transfers between devices, lat_exchange(): pair = lax.ppermute(both, 'lat', pair_list)  5.44 us
    ppermute x2, waiting for transfers between devices, lat_exchange(): lax.ppermute(gate(relay, after) if after else relay, 'lat', hop2_list)  3.02 us
  transfers between devices with their start and end apart: 27, of which 8 were waited for; matrix products, arithmetic and copies ran while one was open for 0% of the time, Pallas kernels for 10%

profile of v2, /device:TPU:0, one launch (start us, length us, event | category | flops | bytes accessed | tf_op | source)
XLA Modules:
  0.0 101.6 jit_solution(13072018273419271345)
XLA Ops:
  0.0 2.9 %pack_first.1 = (bf16[4,112,512]{2,1,0:T(8,128)(2,1)}, bf16[4,112,512]{2,1,0:T(8,128)(2,1)}) custom-call(s32[4,8]{1,0:T(4,128)} %refs_0_.16, f32[48,6144]{1,0:T(8,128)} %refs_1_.10, f32[48,6144]{1,0:T(8,128)} %refs_3_.4), custom_call_target="tpu_custom_call" | custom-call | flops 3000000000 | bytes 30000000 | tf_op jit(solution)/shard_map/pack_first/pallas_call | solution.py:28
  2.9 0.5 collective-permute-start
  3.4 1.0 copy-done.7
  4.4 1.2 %pack_second.1 = (bf16[4,112,512]{2,1,0:T(8,128)(2,1)S(1)}, bf16[4,112,512]{2,1,0:T(8,128)(2,1)S(1)}) custom-call(s32[4,8]{1,0:T(4,128)S(1)} %copy-done.6, f32[48,6144]{1,0:T(8,128)S(1)} %copy-done, f32[48,6144]{1,0:T(8,128)S(1)} %copy-done.1, bf16[4,112,512]{2,1,0:T(8,128)(2,1)S(1)} %copy-done.7), custom_call_target="tpu_custom_call" | custom-call | flops 3000000000 | bytes 30000000 | tf_op jit(solution)/shard_map/pack_second/pallas_call | solution.py:28
  5.6 0.1 collective-permute-start.4
  5.8 0.0 collective-permute-done.refs_1_
  5.8 0.1 join_first.1
  5.8 3.1 %collective-permute-start.1 = (bf16[208,512]{1,0:T(8,128)(2,1)S(1)}, bf16[208,512]{1,0:T(8,128)(2,1)S(1)}, u32[]{:S(2)}, u32[]{:S(2)}) collective-permute-start(bf16[208,512]{1,0:T(8,128)(2,1)S(1)} %get-tuple-element.48), channel_id=1, source_target_pairs={{0,8},{4,12},{8,0},{12,4},{16,24},{20,28},{24,16},{28,20},{1,9},{5... | collective-permute-start | bytes 638984 | tf_op jit(solution)/shard_map/ppermute | solution.py:204
  8.9 2.6 %collective-permute-start.2 = (bf16[208,512]{1,0:T(8,128)(2,1)S(1)}, bf16[208,512]{1,0:T(8,128)(2,1)S(1)}, u32[]{:S(2)}, u32[]{:S(2)}) collective-permute-start(bf16[208,512]{1,0:T(8,128)(2,1)S(1)} %get-tuple-element.49), channel_id=1, source_target_pairs={{0,16},{4,20},{8,24},{12,28},{16,0},{20,4},{24,8},{28,12},{1,17},{... | collective-permute-start | bytes 638984 | tf_op jit(solution)/shard_map/ppermute | solution.py:204
  11.5 0.0 collective-permute-start.3
  11.5 0.0 collective-permute-done.4.refs_1_
  11.5 0.8 join_second.1
  12.3 0.7 copy-done.3
  13.0 5.3 %collective-permute-done.1.refs_1_ = bf16[208,512]{1,0:T(8,128)(2,1)S(1)} collective-permute-done((bf16[208,512]{1,0:T(8,128)(2,1)S(1)}, bf16[208,512]{1,0:T(8,128)(2,1)S(1)}, u32[]{:S(2)}, u32[]{:S(2)}) %collective-permute-start.1) | collective-permute-done | bytes 213024 | tf_op jit(solution)/shard_map/ppermute | solution.py:204
  18.3 8.8 %collective-permute-done.2.refs_2_ = bf16[208,512]{1,0:T(8,128)(2,1)S(1)} collective-permute-done((bf16[208,512]{1,0:T(8,128)(2,1)S(1)}, bf16[208,512]{1,0:T(8,128)(2,1)S(1)}, u32[]{:S(2)}, u32[]{:S(2)}) %collective-permute-start.2) | collective-permute-done | bytes 213024 | tf_op jit(solution)/shard_map/ppermute | solution.py:204
  27.1 0.0 collective-permute-done.3.refs_3_
  27.1 1.2 %owner_first.1 = (bf16[768,512]{1,0:T(8,128)(2,1)}, bf16[384,512]{1,0:T(8,128)(2,1)S(1)}, bf16[384,512]{1,0:T(8,128)(2,1)}) custom-call(bf16[208,512]{1,0:T(8,128)(2,1)S(1)} %get-tuple-element.47.refs_0_, bf16[208,512]{1,0:T(8,128)(2,1)S(1)} %collective-permute-done.1.refs_1_, bf16[208,512]{1,0:T(8,128)(2,1)S(1)} %collective-permute-done.2.refs_2_, ...), custom_call_target="tpu_custom_call" | custom-call | flops 3000000000 | bytes 30000000 | tf_op jit(solution)/shard_map/owner_first/pallas_call | solution.py:28
  28.3 1.3 %collective-permute-start.7 = (bf16[384,512]{1,0:T(8,128)(2,1)}, bf16[384,512]{1,0:T(8,128)(2,1)S(1)}, u32[]{:S(2)}, u32[]{:S(2)}) collective-permute-start(bf16[384,512]{1,0:T(8,128)(2,1)} %get-tuple-element.56), channel_id=1, source_target_pairs={{1,3},{2,0},{5,7},{6,4},{9,11},{10,8},{13,15},{14,12},{17,19},{18,... | collective-permute-start | bytes 1179656 | tf_op jit(solution)/shard_map/ppermute | solution.py:245
  29.6 3.7 %collective-permute-start.5 = (bf16[768,512]{1,0:T(8,128)(2,1)}, bf16[768,512]{1,0:T(8,128)(2,1)}, u32[]{:S(2)}, u32[]{:S(2)}) collective-permute-start(bf16[768,512]{1,0:T(8,128)(2,1)} %get-tuple-element.54.refs_3_.refs_4_.refs_6_.refs_8_), channel_id=1, source_target_pairs={{0,1},{1,0},{2,3},{3,2},{4,5},{5,4},{6,7},{7,6},{8,9},{9,8},{10,11... | collective-permute-start | bytes 2359304 | tf_op jit(solution)/shard_map/ppermute | solution.py:246
  33.3 3.9 %collective-permute-start.8 = (bf16[208,512]{1,0:T(8,128)(2,1)}, bf16[208,512]{1,0:T(8,128)(2,1)S(1)}, u32[]{:S(2)}, u32[]{:S(2)}) collective-permute-start(bf16[208,512]{1,0:T(8,128)(2,1)} %get-tuple-element.57), channel_id=1, source_target_pairs={{0,8},{4,12},{8,0},{12,4},{16,24},{20,28},{24,16},{28,20},{1,9},{5... | collective-permute-start | bytes 638984 | tf_op jit(solution)/shard_map/ppermute | solution.py:204
  37.2 0.1 copy.11.refs_1_.refs_2_
  38.6 1.1 %collective-permute-start.10 = (bf16[208,512]{1,0:T(8,128)(2,1)}, bf16[208,512]{1,0:T(8,128)(2,1)S(1)}, u32[]{:S(2)}, u32[]{:S(2)}) collective-permute-start(bf16[208,512]{1,0:T(8,128)(2,1)} %copy-done.3), channel_id=1, source_target_pairs={{0,16},{4,20},{8,24},{12,28},{16,0},{20,4},{24,8},{28,12},{1,17},{... | collective-permute-start | bytes 638984 | tf_op jit(solution)/shard_map/ppermute | solution.py:204
  39.7 1.5 %collective-permute-start.11 = (bf16[208,512]{1,0:T(8,128)(2,1)S(1)}, bf16[208,512]{1,0:T(8,128)(2,1)S(1)}, u32[]{:S(2)}, u32[]{:S(2)}) collective-permute-start(bf16[208,512]{1,0:T(8,128)(2,1)S(1)} %get-tuple-element.61), channel_id=1, source_target_pairs={{0,24},{4,28},{8,16},{12,20},{16,8},{20,12},{24,0},{28,4},{1,25},{... | collective-permute-start | bytes 638984 | tf_op jit(solution)/shard_map/ppermute | solution.py:204
  41.2 1.9 %collective-permute-done.8.refs_1_.refs_6_ = bf16[208,512]{1,0:T(8,128)(2,1)S(1)} collective-permute-done((bf16[208,512]{1,0:T(8,128)(2,1)}, bf16[208,512]{1,0:T(8,128)(2,1)S(1)}, u32[]{:S(2)}, u32[]{:S(2)}) %collective-permute-start.8) | collective-permute-done | bytes 213024 | tf_op jit(solution)/shard_map/ppermute | solution.py:204
  43.2 0.7 collective-permute-start.6
  43.9 0.0 copy-start.5
  43.9 4.0 %collective-permute-start.9 = (bf16[384,512]{1,0:T(8,128)(2,1)S(1)}, bf16[384,512]{1,0:T(8,128)(2,1)S(1)}, u32[]{:S(2)}, u32[]{:S(2)}) collective-permute-start(bf16[384,512]{1,0:T(8,128)(2,1)S(1)} %gate.1), channel_id=1, source_target_pairs={{3,2},{0,1},{7,6},{4,5},{11,10},{8,9},{15,14},{12,13},{19,18},{16,... | collective-permute-start | bytes 1179656 | tf_op jit(solution)/shard_map/ppermute | solution.py:248
  47.9 1.9 %first_cov.1 = (bf16[512,512]{1,0:T(8,128)(2,1)S(1)}, f32[384,512]{1,0:T(8,128)S(1)}) custom-call(s32[4,8]{1,0:T(4,128)S(1)} %copy-done.6, s32[4,12,3]{2,1,0:T(8,128)S(1)} %copy.11.refs_1_.refs_2_, bf16[2,512,512]{2,1,0:T(8,128)(2,1)S(1)} %copy-done.2, bf16[768,512]{1,0:T(8,128)(2,1)} %get-tuple-element.54.refs_3_.refs_4_.refs_6_.refs_8_), custom_call_target="tpu_custom_call" | custom-call | flops 3000000000 | bytes 30000000 | tf_op jit(solution)/shard_map/first_cov/pallas_call | solution.py:28
  49.8 6.0 %collective-permute-done.10.refs_7_ = bf16[208,512]{1,0:T(8,128)(2,1)S(1)} collective-permute-done((bf16[208,512]{1,0:T(8,128)(2,1)}, bf16[208,512]{1,0:T(8,128)(2,1)S(1)}, u32[]{:S(2)}, u32[]{:S(2)}) %collective-permute-start.10) | collective-permute-done | bytes 213024 | tf_op jit(solution)/shard_map/ppermute | solution.py:204
  55.8 2.0 %east_cov.1 = (bf16[512,512]{1,0:T(8,128)(2,1)S(1)}, f32[384,512]{1,0:T(8,128)S(1)}, bf16[384,512]{1,0:T(8,128)(2,1)S(1)}, bf16[384,512]{1,0:T(8,128)(2,1)S(1)}) custom-call(s32[4,8]{1,0:T(4,128)S(1)} %copy-done.6, s32[4,12]{1,0:T(4,128)S(1)} %copy-done.5, s32[4,12,3]{2,1,0:T(8,128)S(1)} %copy.11.refs_1_.refs_2_, bf16[2,512,512]{2,1,0:T(8,128)(2,1)S(1)} %copy-done.2, ...), custom_call_target="tpu_custom_call" | custom-call | flops 3000000000 | bytes 30000000 | tf_op jit(solution)/shard_map/east_cov/pallas_call | solution.py:28
  57.8 0.0 copy-start.4
  57.8 0.0 collective-permute-done.6.refs_5_.refs_8_
  57.8 0.0 collective-permute-done.5.refs_4_.refs_7_
  57.8 2.2 %edge_cov.1 = (bf16[512,512]{1,0:T(8,128)(2,1)S(1)}, bf16[512,512]{1,0:T(8,128)(2,1)S(1)}) custom-call(s32[4,8]{1,0:T(4,128)S(1)} %copy-done.6, s32[4,12,3]{2,1,0:T(8,128)S(1)} %copy.11.refs_1_.refs_2_, bf16[2,512,512]{2,1,0:T(8,128)(2,1)S(1)} %copy-done.2, bf16[768,512]{1,0:T(8,128)(2,1)} %get-tuple-element.54.refs_3_.refs_4_.refs_6_.refs_8_, ...), custom_call_target="tpu_custom_call" | custom-call | flops 3000000000 | bytes 30000000 | tf_op jit(solution)/shard_map/edge_cov/pallas_call | solution.py:28
  60.0 2.3 %direction_first.1 = (bf16[384,512]{1,0:T(8,128)(2,1)S(1)}, bf16[192,512]{1,0:T(8,128)(2,1)S(1)}, bf16[192,512]{1,0:T(8,128)(2,1)S(1)}, f32[384,512]{1,0:T(8,128)S(1)}) custom-call(s32[4,8]{1,0:T(4,128)S(1)} %copy-done.6, f32[1]{0:T(128)S(6)} %copy.16.refs_1_.refs_2_.refs_0_, f32[1]{0:T(128)S(6)} %copy.17.refs_2_.refs_3_.refs_1_, f32[1,6144]{1,0:T(1,128)S(1)} %bitcast.1, ...), custom_call_target="tpu_custom_call" | custom-call | flops 3000000000 | bytes 30000000 | tf_op jit(solution)/shard_map/direction_first/pallas_call | solution.py:28
  62.3 1.3 %collective-permute-start.14 = (bf16[192,512]{1,0:T(8,128)(2,1)S(1)}, bf16[192,512]{1,0:T(8,128)(2,1)S(1)}, u32[]{:S(2)}, u32[]{:S(2)}) collective-permute-start(bf16[192,512]{1,0:T(8,128)(2,1)S(1)} %get-tuple-element.66), channel_id=1, source_target_pairs={{1,3},{2,0},{5,7},{6,4},{9,11},{10,8},{13,15},{14,12},{17,19},{18,... | collective-permute-start | bytes 589832 | tf_op jit(solution)/shard_map/ppermute | solution.py:245
  63.6 1.7 %collective-permute-start.12 = (bf16[384,512]{1,0:T(8,128)(2,1)S(1)}, bf16[384,512]{1,0:T(8,128)(2,1)S(1)}, u32[]{:S(2)}, u32[]{:S(2)}) collective-permute-start(bf16[384,512]{1,0:T(8,128)(2,1)S(1)} %get-tuple-element.64.refs_11_), channel_id=1, source_target_pairs={{0,1},{1,0},{2,3},{3,2},{4,5},{5,4},{6,7},{7,6},{8,9},{9,8},{10,11... | collective-permute-start | bytes 1179656 | tf_op jit(solution)/shard_map/ppermute | solution.py:246
  65.4 3.2 %inner_step.1 = (f32[384,512]{1,0:T(8,128)S(1)}, bf16[96,512]{1,0:T(8,128)(2,1)S(1)}, bf16[96,512]{1,0:T(8,128)(2,1)S(1)}, bf16[96,512]{1,0:T(8,128)(2,1)S(1)}, bf16[96,512]{1,0:T(8,128)(2,1)S(1)}) custom-call(s32[4,8]{1,0:T(4,128)S(1)} %copy-done.6, s32[4,12,3]{2,1,0:T(8,128)S(1)} %copy.11.refs_1_.refs_2_, f32[1]{0:T(128)S(6)} %copy.16.refs_1_.refs_2_.refs_0_, ...), custom_call_target="tpu_custom_call" | custom-call | flops 3000000000 | bytes 30000000 | tf_op jit(solution)/shard_map/inner_step/pallas_call | solution.py:28
  68.5 4.5 %collective-permute-start.16 = (bf16[96,512]{1,0:T(8,128)(2,1)S(1)}, bf16[96,512]{1,0:T(8,128)(2,1)S(1)}, u32[]{:S(2)}, u32[]{:S(2)}) collective-permute-start(bf16[96,512]{1,0:T(8,128)(2,1)S(1)} %get-tuple-element.73), channel_id=1, source_target_pairs={{0,8},{4,12},{8,0},{12,4},{16,24},{20,28},{24,16},{28,20},{1,9},{5... | collective-permute-start | bytes 294920 | tf_op jit(solution)/shard_map/ppermute | solution.py:204
  73.1 1.1 %collective-permute-start.17 = (bf16[96,512]{1,0:T(8,128)(2,1)S(1)}, bf16[96,512]{1,0:T(8,128)(2,1)S(1)}, u32[]{:S(2)}, u32[]{:S(2)}) collective-permute-start(bf16[96,512]{1,0:T(8,128)(2,1)S(1)} %get-tuple-element.74), channel_id=1, source_target_pairs={{0,16},{4,20},{8,24},{12,28},{16,0},{20,4},{24,8},{28,12},{1,17},{... | collective-permute-start | bytes 294920 | tf_op jit(solution)/shard_map/ppermute | solution.py:204
  74.2 1.4 %collective-permute-start.18 = (bf16[96,512]{1,0:T(8,128)(2,1)S(1)}, bf16[96,512]{1,0:T(8,128)(2,1)S(1)}, u32[]{:S(2)}, u32[]{:S(2)}) collective-permute-start(bf16[96,512]{1,0:T(8,128)(2,1)S(1)} %get-tuple-element.75), channel_id=1, source_target_pairs={{0,24},{4,28},{8,16},{12,20},{16,8},{20,12},{24,0},{28,4},{1,25},{... | collective-permute-start | bytes 294920 | tf_op jit(solution)/shard_map/ppermute | solution.py:204
  75.6 0.2 collective-permute-done.16.refs_8_.refs_1_.refs_13_
  75.8 0.7 collective-permute-start.13
  76.5 5.4 %collective-permute-start.15 = (bf16[192,512]{1,0:T(8,128)(2,1)S(1)}, bf16[192,512]{1,0:T(8,128)(2,1)S(1)}, u32[]{:S(2)}, u32[]{:S(2)}) collective-permute-start(bf16[192,512]{1,0:T(8,128)(2,1)S(1)} %collective-permute-done.14), channel_id=1, source_target_pairs={{3,2},{0,1},{7,6},{4,5},{11,10},{8,9},{15,14},{12,13},{19,18},{16,... | collective-permute-start | bytes 589832 | tf_op jit(solution)/shard_map/ppermute | solution.py:248
  81.9 0.0 collective-permute-done.17.refs_9_.refs_2_.refs_14_
  81.9 0.0 collective-permute-done.18.refs_10_.refs_3_.refs_15_
  82.0 0.1 collective-permute-start.26
  82.0 0.0 collective-permute-done.13.refs_5_
  82.0 0.0 collective-permute-done.12.refs_4_
  82.1 3.0 %collective-permute-done.15.refs_6_ = bf16[192,512]{1,0:T(8,128)(2,1)S(1)} collective-permute-done((bf16[192,512]{1,0:T(8,128)(2,1)S(1)}, bf16[192,512]{1,0:T(8,128)(2,1)S(1)}, u32[]{:S(2)}, u32[]{:S(2)}) %collective-permute-start.15) | collective-permute-done | bytes 196640 | tf_op jit(solution)/shard_map/ppermute | solution.py:248
  85.1 0.6 outer_step.1
  85.7 0.1 collective-permute-start.19
  85.7 1.7 %collective-permute-start.20 = (bf16[48,512]{1,0:T(8,128)(2,1)S(1)}, bf16[48,512]{1,0:T(8,128)(2,1)S(1)}, u32[]{:S(2)}, u32[]{:S(2)}) collective-permute-start(bf16[48,512]{1,0:T(8,128)(2,1)S(1)} %get-tuple-element.78), channel_id=1, source_target_pairs={{0,8},{4,12},{8,0},{12,4},{16,24},{20,28},{24,16},{28,20},{1,9},{5... | collective-permute-start | bytes 147464 | tf_op jit(solution)/shard_map/ppermute | solution.py:429
  87.5 0.1 collective-permute-start.21
  87.6 2.7 %collective-permute-start.22 = (bf16[48,512]{1,0:T(8,128)(2,1)S(1)}, bf16[48,512]{1,0:T(8,128)(2,1)S(1)}, u32[]{:S(2)}, u32[]{:S(2)}) collective-permute-start(bf16[48,512]{1,0:T(8,128)(2,1)S(1)} %get-tuple-element.80), channel_id=1, source_target_pairs={{0,16},{4,20},{8,24},{12,28},{16,0},{20,4},{24,8},{28,12},{1,17},{... | collective-permute-start | bytes 147464 | tf_op jit(solution)/shard_map/ppermute | solution.py:429
  90.3 3.8 %collective-permute-start.24 = (bf16[48,512]{1,0:T(8,128)(2,1)S(1)}, bf16[48,512]{1,0:T(8,128)(2,1)S(1)}, u32[]{:S(2)}, u32[]{:S(2)}) collective-permute-start(bf16[48,512]{1,0:T(8,128)(2,1)S(1)} %get-tuple-element.82), channel_id=1, source_target_pairs={{0,24},{4,28},{8,16},{12,20},{16,8},{20,12},{24,0},{28,4},{1,25},{... | collective-permute-start | bytes 147464 | tf_op jit(solution)/shard_map/ppermute | solution.py:429
  94.0 0.0 collective-permute-done.20.refs_6_
  94.0 0.1 collective-permute-start.25
  94.2 0.0 collective-permute-done.21.refs_7_
  94.2 0.0 collective-permute-done.22.refs_8_
  94.2 3.7 %collective-permute-done.23.refs_9_ = bf16[48,512]{1,0:T(8,128)(2,1)S(1)} collective-permute-done((bf16[48,512]{1,0:T(8,128)(2,1)S(1)}, bf16[48,512]{1,0:T(8,128)(2,1)S(1)}, u32[]{:S(2)}, u32[]{:S(2)}) %collective-permute-start.23) | collective-permute-done | bytes 49184 | tf_op jit(solution)/shard_map/ppermute | solution.py:429
  97.9 0.0 collective-permute-done.24.refs_10_
  97.9 1.8 %collective-permute-done.25.refs_11_ = bf16[48,512]{1,0:T(8,128)(2,1)S(1)} collective-permute-done((bf16[48,512]{1,0:T(8,128)(2,1)S(1)}, bf16[48,512]{1,0:T(8,128)(2,1)S(1)}, u32[]{:S(2)}, u32[]{:S(2)}) %collective-permute-start.25) | collective-permute-done | bytes 49184 | tf_op jit(solution)/shard_map/ppermute | solution.py:429
  99.7 1.9 %unpack.1 = f32[48,6144]{1,0:T(8,128)} custom-call(s32[4,8]{1,0:T(4,128)S(1)} %copy-done.6, f32[1]{0:T(128)S(6)} %copy.16.refs_1_.refs_2_.refs_0_, f32[1]{0:T(128)S(6)} %copy.17.refs_2_.refs_3_.refs_1_, f32[48,6144]{1,0:T(8,128)S(1)} %copy-done.1, bf16[48,512]{1,0:T(8,128)(2,1)S(1)} %get-tuple-element.76.refs_4_, ...), custom_call_target="tpu_custom_call" | custom-call | flops 3000000000 | bytes 30000000 | tf_op jit(solution)/shard_map/unpack/pallas_call | solution.py:28
  (29 shorter events, 0.1 us)
Async XLA Ops:
  0.0 3.4 %copy-start.1 = (f32[48,6144]{1,0:T(8,128)S(1)}, f32[48,6144]{1,0:T(8,128)}, u32[]{:S(2)}) copy-start(f32[48,6144]{1,0:T(8,128)} %refs_3_.4) | copy-start | bytes 3538948
  0.0 3.4 %copy-start.6 = (s32[4,8]{1,0:T(4,128)S(1)}, s32[4,8]{1,0:T(4,128)}, u32[]{:S(2)}) copy-start(s32[4,8]{1,0:T(4,128)} %refs_0_.16) | copy-start | bytes 388
  0.0 3.4 %copy-start = (f32[48,6144]{1,0:T(8,128)S(1)}, f32[48,6144]{1,0:T(8,128)}, u32[]{:S(2)}) copy-start(f32[48,6144]{1,0:T(8,128)} %refs_1_.10) | copy-start | bytes 3538948
  2.9 2.9 %collective-permute-start = (bf16[4,112,512]{2,1,0:T(8,128)(2,1)}, bf16[4,112,512]{2,1,0:T(8,128)(2,1)S(1)}, u32[]{:S(2)}, u32[]{:S(2)}) collective-permute-start(bf16[4,112,512]{2,1,0:T(8,128)(2,1)} %get-tuple-element.46), channel_id=1, source_target_pairs={{0,4},{4,0},{8,12},{12,8},{16,20},{20,16},{24,28},{28,24},{1,5},{5... | collective-permute-start | bytes 1376264 | tf_op jit(solution)/shard_map/ppermute | solution.py:181
  3.4 1.0 %copy-start.7 = (bf16[4,112,512]{2,1,0:T(8,128)(2,1)S(1)}, bf16[4,112,512]{2,1,0:T(8,128)(2,1)}, u32[]{:S(2)}) copy-start(bf16[4,112,512]{2,1,0:T(8,128)(2,1)} %get-tuple-element.45.refs_0_.refs_3_) | copy-start | bytes 1376260
  4.4 1.3 %copy-start.8 = (bf16[4,112,512]{2,1,0:T(8,128)(2,1)S(1)}, bf16[4,112,512]{2,1,0:T(8,128)(2,1)}, u32[]{:S(2)}) copy-start(bf16[4,112,512]{2,1,0:T(8,128)(2,1)} %get-tuple-element.45.refs_0_.refs_3_) | copy-start | bytes 1376260
  5.6 5.9 %collective-permute-start.4 = (bf16[4,112,512]{2,1,0:T(8,128)(2,1)S(1)}, bf16[4,112,512]{2,1,0:T(8,128)(2,1)S(1)}, u32[]{:S(2)}, u32[]{:S(2)}) collective-permute-start(bf16[4,112,512]{2,1,0:T(8,128)(2,1)S(1)} %get-tuple-element.52), channel_id=1, source_target_pairs={{0,4},{4,0},{8,12},{12,8},{16,20},{20,16},{24,28},{28,24},{1,5},{5... | collective-permute-start | bytes 1376264 | tf_op jit(solution)/shard_map/ppermute | solution.py:199
  5.8 12.5 %collective-permute-start.1 = (bf16[208,512]{1,0:T(8,128)(2,1)S(1)}, bf16[208,512]{1,0:T(8,128)(2,1)S(1)}, u32[]{:S(2)}, u32[]{:S(2)}) collective-permute-start(bf16[208,512]{1,0:T(8,128)(2,1)S(1)} %get-tuple-element.48), channel_id=1, source_target_pairs={{0,8},{4,12},{8,0},{12,4},{16,24},{20,28},{24,16},{28,20},{1,9},{5... | collective-permute-start | bytes 638984 | tf_op jit(solution)/shard_map/ppermute | solution.py:204
  8.9 18.2 %collective-permute-start.2 = (bf16[208,512]{1,0:T(8,128)(2,1)S(1)}, bf16[208,512]{1,0:T(8,128)(2,1)S(1)}, u32[]{:S(2)}, u32[]{:S(2)}) collective-permute-start(bf16[208,512]{1,0:T(8,128)(2,1)S(1)} %get-tuple-element.49), channel_id=1, source_target_pairs={{0,16},{4,20},{8,24},{12,28},{16,0},{20,4},{24,8},{28,12},{1,17},{... | collective-permute-start | bytes 638984 | tf_op jit(solution)/shard_map/ppermute | solution.py:204
  11.5 15.6 %collective-permute-start.3 = (bf16[208,512]{1,0:T(8,128)(2,1)S(1)}, bf16[208,512]{1,0:T(8,128)(2,1)S(1)}, u32[]{:S(2)}, u32[]{:S(2)}) collective-permute-start(bf16[208,512]{1,0:T(8,128)(2,1)S(1)} %get-tuple-element.50), channel_id=1, source_target_pairs={{0,24},{4,28},{8,16},{12,20},{16,8},{20,12},{24,0},{28,4},{1,25},{... | collective-permute-start | bytes 638984 | tf_op jit(solution)/shard_map/ppermute | solution.py:204
  12.3 0.7 copy-start.3
  13.0 15.3 %copy-start.9 = (bf16[208,512]{1,0:T(8,128)(2,1)}, bf16[208,512]{1,0:T(8,128)(2,1)S(1)}, u32[]{:S(2)}) copy-start(bf16[208,512]{1,0:T(8,128)(2,1)S(1)} %get-tuple-element.53.refs_4_.refs_5_) | copy-start | bytes 638980
  27.1 10.1 %copy-start.11 = (s32[4,12,3]{1,0,2:T(4,128)S(1)}, s32[4,12,3]{1,0,2:T(4,128)}, u32[]{:S(2)}) copy-start(s32[4,12,3]{1,0,2:T(4,128)} %param.15) | copy-start | bytes 1732
  27.1 20.7 %copy-start.2 = (bf16[2,512,512]{2,1,0:T(8,128)(2,1)S(1)}, bf16[2,512,512]{2,1,0:T(8,128)(2,1)}, u32[]{:S(2)}) copy-start(bf16[2,512,512]{2,1,0:T(8,128)(2,1)} %refs_4_.1) | copy-start | bytes 3145732
  28.3 15.6 %collective-permute-start.7 = (bf16[384,512]{1,0:T(8,128)(2,1)}, bf16[384,512]{1,0:T(8,128)(2,1)S(1)}, u32[]{:S(2)}, u32[]{:S(2)}) collective-permute-start(bf16[384,512]{1,0:T(8,128)(2,1)} %get-tuple-element.56), channel_id=1, source_target_pairs={{1,3},{2,0},{5,7},{6,4},{9,11},{10,8},{13,15},{14,12},{17,19},{18,... | collective-permute-start | bytes 1179656 | tf_op jit(solution)/shard_map/ppermute | solution.py:245
  29.6 28.3 %collective-permute-start.5 = (bf16[768,512]{1,0:T(8,128)(2,1)}, bf16[768,512]{1,0:T(8,128)(2,1)}, u32[]{:S(2)}, u32[]{:S(2)}) collective-permute-start(bf16[768,512]{1,0:T(8,128)(2,1)} %get-tuple-element.54.refs_3_.refs_4_.refs_6_.refs_8_), channel_id=1, source_target_pairs={{0,1},{1,0},{2,3},{3,2},{4,5},{5,4},{6,7},{7,6},{8,9},{9,8},{10,11... | collective-permute-start | bytes 2359304 | tf_op jit(solution)/shard_map/ppermute | solution.py:246
  33.3 9.9 %collective-permute-start.8 = (bf16[208,512]{1,0:T(8,128)(2,1)}, bf16[208,512]{1,0:T(8,128)(2,1)S(1)}, u32[]{:S(2)}, u32[]{:S(2)}) collective-permute-start(bf16[208,512]{1,0:T(8,128)(2,1)} %get-tuple-element.57), channel_id=1, source_target_pairs={{0,8},{4,12},{8,0},{12,4},{16,24},{20,28},{24,16},{28,20},{1,9},{5... | collective-permute-start | bytes 638984 | tf_op jit(solution)/shard_map/ppermute | solution.py:204
  38.6 17.2 %collective-permute-start.10 = (bf16[208,512]{1,0:T(8,128)(2,1)}, bf16[208,512]{1,0:T(8,128)(2,1)S(1)}, u32[]{:S(2)}, u32[]{:S(2)}) collective-permute-start(bf16[208,512]{1,0:T(8,128)(2,1)} %copy-done.3), channel_id=1, source_target_pairs={{0,16},{4,20},{8,24},{12,28},{16,0},{20,4},{24,8},{28,12},{1,17},{... | collective-permute-start | bytes 638984 | tf_op jit(solution)/shard_map/ppermute | solution.py:204
  39.7 16.1 %collective-permute-start.11 = (bf16[208,512]{1,0:T(8,128)(2,1)S(1)}, bf16[208,512]{1,0:T(8,128)(2,1)S(1)}, u32[]{:S(2)}, u32[]{:S(2)}) collective-permute-start(bf16[208,512]{1,0:T(8,128)(2,1)S(1)} %get-tuple-element.61), channel_id=1, source_target_pairs={{0,24},{4,28},{8,16},{12,20},{16,8},{20,12},{24,0},{28,4},{1,25},{... | collective-permute-start | bytes 638984 | tf_op jit(solution)/shard_map/ppermute | solution.py:204
  43.2 14.6 %collective-permute-start.6 = (bf16[384,512]{1,0:T(8,128)(2,1)S(1)}, bf16[384,512]{1,0:T(8,128)(2,1)S(1)}, u32[]{:S(2)}, u32[]{:S(2)}) collective-permute-start(bf16[384,512]{1,0:T(8,128)(2,1)S(1)} %get-tuple-element.55), channel_id=1, source_target_pairs={{1,2},{2,1},{5,6},{6,5},{9,10},{10,9},{13,14},{14,13},{17,18},{18,... | collective-permute-start | bytes 1179656 | tf_op jit(solution)/shard_map/ppermute | solution.py:247
  43.9 11.9 %copy-start.5 = (s32[4,12]{1,0:T(4,128)S(1)}, s32[4,12]{1,0:T(4,128)}, u32[]{:S(2)}) copy-start(s32[4,12]{1,0:T(4,128)} %refs_1_.11) | copy-start | bytes 580
  43.9 11.9 %copy-start.10 = (bf16[208,512]{1,0:T(8,128)(2,1)S(1)}, bf16[208,512]{1,0:T(8,128)(2,1)}, u32[]{:S(2)}) copy-start(bf16[208,512]{1,0:T(8,128)(2,1)} %copy-done.9) | copy-start | bytes 638980
  43.9 13.9 %collective-permute-start.9 = (bf16[384,512]{1,0:T(8,128)(2,1)S(1)}, bf16[384,512]{1,0:T(8,128)(2,1)S(1)}, u32[]{:S(2)}, u32[]{:S(2)}) collective-permute-start(bf16[384,512]{1,0:T(8,128)(2,1)S(1)} %gate.1), channel_id=1, source_target_pairs={{3,2},{0,1},{7,6},{4,5},{11,10},{8,9},{15,14},{12,13},{19,18},{16,... | collective-permute-start | bytes 1179656 | tf_op jit(solution)/shard_map/ppermute | solution.py:248
  57.8 2.2 %copy-start.4 = (f32[6144]{0:T(1024)S(1)}, f32[6144]{0:T(1024)}, u32[]{:S(2)}) copy-start(f32[6144]{0:T(1024)} %param.11) | copy-start | bytes 73732
  62.3 14.2 %collective-permute-start.14 = (bf16[192,512]{1,0:T(8,128)(2,1)S(1)}, bf16[192,512]{1,0:T(8,128)(2,1)S(1)}, u32[]{:S(2)}, u32[]{:S(2)}) collective-permute-start(bf16[192,512]{1,0:T(8,128)(2,1)S(1)} %get-tuple-element.66), channel_id=1, source_target_pairs={{1,3},{2,0},{5,7},{6,4},{9,11},{10,8},{13,15},{14,12},{17,19},{18,... | collective-permute-start | bytes 589832 | tf_op jit(solution)/shard_map/ppermute | solution.py:245
  63.6 18.4 %collective-permute-start.12 = (bf16[384,512]{1,0:T(8,128)(2,1)S(1)}, bf16[384,512]{1,0:T(8,128)(2,1)S(1)}, u32[]{:S(2)}, u32[]{:S(2)}) collective-permute-start(bf16[384,512]{1,0:T(8,128)(2,1)S(1)} %get-tuple-element.64.refs_11_), channel_id=1, source_target_pairs={{0,1},{1,0},{2,3},{3,2},{4,5},{5,4},{6,7},{7,6},{8,9},{9,8},{10,11... | collective-permute-start | bytes 1179656 | tf_op jit(solution)/shard_map/ppermute | solution.py:246
  68.5 7.3 %collective-permute-start.16 = (bf16[96,512]{1,0:T(8,128)(2,1)S(1)}, bf16[96,512]{1,0:T(8,128)(2,1)S(1)}, u32[]{:S(2)}, u32[]{:S(2)}) collective-permute-start(bf16[96,512]{1,0:T(8,128)(2,1)S(1)} %get-tuple-element.73), channel_id=1, source_target_pairs={{0,8},{4,12},{8,0},{12,4},{16,24},{20,28},{24,16},{28,20},{1,9},{5... | collective-permute-start | bytes 294920 | tf_op jit(solution)/shard_map/ppermute | solution.py:204
  73.1 8.9 %collective-permute-start.17 = (bf16[96,512]{1,0:T(8,128)(2,1)S(1)}, bf16[96,512]{1,0:T(8,128)(2,1)S(1)}, u32[]{:S(2)}, u32[]{:S(2)}) collective-permute-start(bf16[96,512]{1,0:T(8,128)(2,1)S(1)} %get-tuple-element.74), channel_id=1, source_target_pairs={{0,16},{4,20},{8,24},{12,28},{16,0},{20,4},{24,8},{28,12},{1,17},{... | collective-permute-start | bytes 294920 | tf_op jit(solution)/shard_map/ppermute | solution.py:204
  74.2 7.7 %collective-permute-start.18 = (bf16[96,512]{1,0:T(8,128)(2,1)S(1)}, bf16[96,512]{1,0:T(8,128)(2,1)S(1)}, u32[]{:S(2)}, u32[]{:S(2)}) collective-permute-start(bf16[96,512]{1,0:T(8,128)(2,1)S(1)} %get-tuple-element.75), channel_id=1, source_target_pairs={{0,24},{4,28},{8,16},{12,20},{16,8},{20,12},{24,0},{28,4},{1,25},{... | collective-permute-start | bytes 294920 | tf_op jit(solution)/shard_map/ppermute | solution.py:204
  75.8 6.2 %collective-permute-start.13 = (bf16[192,512]{1,0:T(8,128)(2,1)S(1)}, bf16[192,512]{1,0:T(8,128)(2,1)S(1)}, u32[]{:S(2)}, u32[]{:S(2)}) collective-permute-start(bf16[192,512]{1,0:T(8,128)(2,1)S(1)} %get-tuple-element.65), channel_id=1, source_target_pairs={{1,2},{2,1},{5,6},{6,5},{9,10},{10,9},{13,14},{14,13},{17,18},{18,... | collective-permute-start | bytes 589832 | tf_op jit(solution)/shard_map/ppermute | solution.py:247
  76.5 8.6 %collective-permute-start.15 = (bf16[192,512]{1,0:T(8,128)(2,1)S(1)}, bf16[192,512]{1,0:T(8,128)(2,1)S(1)}, u32[]{:S(2)}, u32[]{:S(2)}) collective-permute-start(bf16[192,512]{1,0:T(8,128)(2,1)S(1)} %collective-permute-done.14), channel_id=1, source_target_pairs={{3,2},{0,1},{7,6},{4,5},{11,10},{8,9},{15,14},{12,13},{19,18},{16,... | collective-permute-start | bytes 589832 | tf_op jit(solution)/shard_map/ppermute | solution.py:248
  82.0 8.3 %collective-permute-start.26 = (bf16[4,48,512]{2,1,0:T(8,128)(2,1)S(1)}, bf16[4,48,512]{2,1,0:T(8,128)(2,1)S(1)}, u32[]{:S(2)}, u32[]{:S(2)}) collective-permute-start(bf16[4,48,512]{2,1,0:T(8,128)(2,1)S(1)} %peer_rows.1), channel_id=1, source_target_pairs={{0,4},{4,0},{8,12},{12,8},{16,20},{20,16},{24,28},{28,24},{1,5},{5... | collective-permute-start | bytes 589832 | tf_op jit(solution)/shard_map/ppermute | solution.py:199
  85.7 4.6 %collective-permute-start.19 = (bf16[48,512]{1,0:T(8,128)(2,1)S(1)}, bf16[48,512]{1,0:T(8,128)(2,1)S(1)}, u32[]{:S(2)}, u32[]{:S(2)}) collective-permute-start(bf16[48,512]{1,0:T(8,128)(2,1)S(1)} %get-tuple-element.77), channel_id=1, source_target_pairs={{0,4},{4,0},{8,12},{12,8},{16,20},{20,16},{24,28},{28,24},{1,5},{5... | collective-permute-start | bytes 147464 | tf_op jit(solution)/shard_map/ppermute | solution.py:429
  85.7 8.3 %collective-permute-start.20 = (bf16[48,512]{1,0:T(8,128)(2,1)S(1)}, bf16[48,512]{1,0:T(8,128)(2,1)S(1)}, u32[]{:S(2)}, u32[]{:S(2)}) collective-permute-start(bf16[48,512]{1,0:T(8,128)(2,1)S(1)} %get-tuple-element.78), channel_id=1, source_target_pairs={{0,8},{4,12},{8,0},{12,4},{16,24},{20,28},{24,16},{28,20},{1,9},{5... | collective-permute-start | bytes 147464 | tf_op jit(solution)/shard_map/ppermute | solution.py:429
  87.5 6.7 %collective-permute-start.21 = (bf16[48,512]{1,0:T(8,128)(2,1)S(1)}, bf16[48,512]{1,0:T(8,128)(2,1)S(1)}, u32[]{:S(2)}, u32[]{:S(2)}) collective-permute-start(bf16[48,512]{1,0:T(8,128)(2,1)S(1)} %get-tuple-element.79), channel_id=1, source_target_pairs={{0,12},{4,8},{8,4},{12,0},{16,28},{20,24},{24,20},{28,16},{1,13},{... | collective-permute-start | bytes 147464 | tf_op jit(solution)/shard_map/ppermute | solution.py:429
  87.6 6.6 %collective-permute-start.22 = (bf16[48,512]{1,0:T(8,128)(2,1)S(1)}, bf16[48,512]{1,0:T(8,128)(2,1)S(1)}, u32[]{:S(2)}, u32[]{:S(2)}) collective-permute-start(bf16[48,512]{1,0:T(8,128)(2,1)S(1)} %get-tuple-element.80), channel_id=1, source_target_pairs={{0,16},{4,20},{8,24},{12,28},{16,0},{20,4},{24,8},{28,12},{1,17},{... | collective-permute-start | bytes 147464 | tf_op jit(solution)/shard_map/ppermute | solution.py:429
  90.3 7.6 %collective-permute-start.23 = (bf16[48,512]{1,0:T(8,128)(2,1)S(1)}, bf16[48,512]{1,0:T(8,128)(2,1)S(1)}, u32[]{:S(2)}, u32[]{:S(2)}) collective-permute-start(bf16[48,512]{1,0:T(8,128)(2,1)S(1)} %get-tuple-element.81), channel_id=1, source_target_pairs={{0,20},{4,16},{8,28},{12,24},{16,4},{20,0},{24,12},{28,8},{1,21},{... | collective-permute-start | bytes 147464 | tf_op jit(solution)/shard_map/ppermute | solution.py:429
  90.3 7.6 %collective-permute-start.24 = (bf16[48,512]{1,0:T(8,128)(2,1)S(1)}, bf16[48,512]{1,0:T(8,128)(2,1)S(1)}, u32[]{:S(2)}, u32[]{:S(2)}) collective-permute-start(bf16[48,512]{1,0:T(8,128)(2,1)S(1)} %get-tuple-element.82), channel_id=1, source_target_pairs={{0,24},{4,28},{8,16},{12,20},{16,8},{20,12},{24,0},{28,4},{1,25},{... | collective-permute-start | bytes 147464 | tf_op jit(solution)/shard_map/ppermute | solution.py:429
  94.0 5.7 %collective-permute-start.25 = (bf16[48,512]{1,0:T(8,128)(2,1)S(1)}, bf16[48,512]{1,0:T(8,128)(2,1)S(1)}, u32[]{:S(2)}, u32[]{:S(2)}) collective-permute-start(bf16[48,512]{1,0:T(8,128)(2,1)S(1)} %get-tuple-element.83), channel_id=1, source_target_pairs={{0,28},{4,24},{8,20},{12,16},{16,12},{20,8},{24,4},{28,0},{1,29},{... | collective-permute-start | bytes 147464 | tf_op jit(solution)/shard_map/ppermute | solution.py:429

commit v3 on v2

v3 whole, which is shorter than its diff:
```python
import math

import jax
import jax.numpy as jnp
from jax import lax
from jax.experimental import pallas as pl
from jax.experimental.pallas import tpu as pltpu
from jax.sharding import PartitionSpec as P

BF = jnp.bfloat16
F32 = jnp.float32
VMEM_LIMIT = 12 * 1024 * 1024

SMEM_SPEC = pl.BlockSpec(memory_space=pltpu.SMEM)
VMEM_SPEC = pl.BlockSpec(memory_space=pltpu.VMEM)
ANY_SPEC = pl.BlockSpec(memory_space=pl.ANY)
HBM_SPEC = pl.BlockSpec(memory_space=pltpu.HBM)


def kernel_call(body, outs, scalars, arrays, scratch=(), name=None, array_spec=VMEM_SPEC, after=(), vmem=VMEM_LIMIT):
    used, unread = len(scalars) + len(arrays), len(after)
    moved = sum(a.size * a.dtype.itemsize for a in arrays)
    moved += sum(jnp.dtype(d).itemsize * math.prod(s) for s, d in outs)

    def run(*refs):
        body(*refs[:used], *refs[used + unread :])

    return pl.pallas_call(
        run,
        out_shape=tuple(jax.ShapeDtypeStruct(s, d) for s, d in outs),
        in_specs=[SMEM_SPEC] * len(scalars) + [array_spec] * len(arrays) + [ANY_SPEC] * unread,
        out_specs=tuple(VMEM_SPEC for _ in outs),
        scratch_shapes=list(scratch),
        compiler_params=pltpu.CompilerParams(vmem_limit_bytes=vmem),
        cost_estimate=pl.CostEstimate(flops=3 * 10**9, bytes_accessed=3 * 10**7, transcendentals=0),
        name=name,
    )(*scalars, *arrays, *after)


def gate(x, after):
    def nothing(*refs):
        del refs

    return pl.pallas_call(
        nothing,
        out_shape=jax.ShapeDtypeStruct(x.shape, x.dtype),
        in_specs=[ANY_SPEC] * (1 + len(after)),
        out_specs=ANY_SPEC,
        input_output_aliases={0: 0},
        compiler_params=pltpu.CompilerParams(vmem_limit_bytes=1024 * 1024),
        name="gate",
    )(x, *after)


def dot_nn(a, b):
    return lax.dot_general(a, b, (((1,), (0,)), ((), ())), preferred_element_type=F32)


def dot_nt(a, b):
    return lax.dot_general(a, b, (((1,), (1,)), ((), ())), preferred_element_type=F32)


def dot_tn(a, b):
    return lax.dot_general(a, b, (((0,), (0,)), ((), ())), preferred_element_type=F32)


def region_start(rb, band, m):
    return lax.fori_loop(0, m, lambda i, acc: acc + rb[band, i], jnp.int32(0))


def block_cols(block, width):
    return pl.ds(pl.multiple_of(block * width, width), width)


def chebyshev(low, high, width):
    low = jnp.broadcast_to(low, (8, width))
    high = jnp.broadcast_to(high, (8, width))
    centre = 0.5 * (high + low)
    half = 0.5 * (high - low)
    s = centre / half
    q0 = 1.0 / s
    q1 = 1.0 / (2.0 * s - q0)
    q2 = 1.0 / (2.0 * s - q1)
    row = lax.broadcasted_iota(jnp.int32, (8, width), 0)
    out = 1.0 / centre
    for i, value in enumerate((q1 * q0, 2.0 * q1 / half, q2 * q1, 2.0 * q2 / half)):
        out = jnp.where(row == i + 1, value, out)
    return out


def coefficients(coef):
    return [coef[i : i + 1, :] for i in range(5)]


def on_device(
    equivalents,
    innovations,
    obs_var,
    taper_tiles,
    region_blocks,
    pair_mask,
    taper_index,
    eig_low,
    eig_high,
):
    n = lax.axis_size("mem")
    n_lat = lax.axis_size("lat")
    chips = n // 2
    rows, cols = equivalents.shape
    B = taper_tiles.shape[1]
    nb = cols // B
    members = rows * n
    inv_scale = (members - 1) ** (-0.5)
    rp = -(-rows // 16) * 16
    mp = rp * n
    half = mp // 2

    def put_rows(ref_set, lo, value):
        ref_set(slice(lo, lo + rows), value)
        if rp > rows:
            ref_set(slice(lo + rows, lo + rp), jnp.zeros((rp - rows, B), value.dtype))

    tail_rows = 8
    msg = 2 * rp + tail_rows
    step = 2 * rp

    def mean_rows(x, offset):
        mean = jnp.sum(x, axis=0, keepdims=True) * (1.0 / rows)
        high = mean.astype(BF).astype(F32)
        mid = (mean - high).astype(BF).astype(F32)
        row = lax.broadcasted_iota(jnp.int32, (tail_rows, B), 0)
        tail = jnp.where(row == offset + 2, mean - high - mid, 0.0)
        tail = jnp.where(row == offset + 1, mid, tail)
        tail = jnp.where(row == offset, high, tail)
        return mean, tail.astype(BF)

    def blocks(rb, extra):
        me, band = lax.axis_index("mem"), lax.axis_index("lat")
        return [
            block_cols(jnp.minimum(region_start(rb, band, me ^ i) + extra, nb - 1), B) for i in range(n)
        ]

    def fill_p(own, oth, at_row, rb, eq, extra):
        for i, at in enumerate(blocks(rb, extra)):
            k, j = i // 2, i % 2
            out = oth if j else own
            x = eq[:, at]
            mean, tail = mean_rows(x, 3 * j)
            put = lambda s, v: out.__setitem__((k, s), v)
            put_rows(put, at_row, ((x - mean) * inv_scale).astype(BF))
            out[k, step:msg, :] = tail

    def fill_r(own, oth, rb, inn, extra):
        for i, at in enumerate(blocks(rb, extra)):
            out = oth if i % 2 else own
            put_rows(lambda s, v: out.__setitem__((i // 2, s), v), 0, inn[:, at].astype(BF))

    def pack_body(rb_hbm, eq_hbm, inn_hbm, own1, oth1, own2, oth2, eq, inn, rb, sems):
        copies = [
            pltpu.make_async_copy(src, dst, sems.at[i])
            for i, (src, dst) in enumerate(((rb_hbm, rb), (inn_hbm, inn), (eq_hbm, eq)))
        ]
        for copy in copies:
            copy.start()
        copies[0].wait()
        copies[1].wait()
        fill_r(own1, oth1, rb, inn, 0)
        fill_r(own2, oth2, rb, inn, 1)
        copies[2].wait()
        fill_p(own1, oth1, rp, rb, eq, 0)
        fill_p(own2, oth2, rp, rb, eq, 1)

    own1, oth1, own2, oth2 = kernel_call(
        pack_body,
        [((chips, msg, B), BF)] * 4,
        [],
        [region_blocks, equivalents, innovations],
        scratch=[
            pltpu.VMEM((rows, cols), F32),
            pltpu.VMEM((rows, cols), F32),
            pltpu.SMEM(region_blocks.shape, jnp.int32),
            pltpu.SemaphoreType.DMA((3,)),
        ],
        name="pack",
        array_spec=HBM_SPEC,
        vmem=52 * 1024 * 1024,
    )
    core_pairs = [(i, i ^ 1) for i in range(n)]

    def swap_core(x):
        return lax.ppermute(x, "mem", core_pairs)

    def z_exchange(parts, order):
        got = list(parts)
        for k in order:
            got[k] = lax.ppermute(parts[k], "mem", [(i, i ^ (2 * k)) for i in range(n)])
        return got

    far_first = list(range(1, chips))[::-1]
    top = chips // 2

    def z_send(x, k):
        return lax.ppermute(x, "mem", [(i, i ^ (2 * k)) for i in range(n)])


    def join_body(own, oth, *outs):
        for k in range(chips):
            out = outs[k]
            out[0:rp, :] = own[k, rp:step, :]
            out[rp:step, :] = oth[k, rp:step, :]
            out[step : step + rp, :] = own[k, 0:rp, :]
            out[step + rp : 2 * step, :] = oth[k, 0:rp, :]
            out[2 * step :, :] = own[k, step:msg, :] + oth[k, step:msg, :]

    def join(own, oth, name, after=()):
        return kernel_call(
            join_body, [((msg + step, B), BF)] * chips, [], [own, oth], name=name, after=after
        )

    m1_got = z_exchange(join(own1, swap_core(oth1), "join_first"), far_first)
    coef = chebyshev(eig_low[0], eig_high[0], B)
    m2_parts = join(
        own2, swap_core(oth2), "join_second", after=[taper_index, pair_mask, region_blocks, coef]
    )
    m2_got = z_exchange(m2_parts, far_first)

    def corrected(pieces):
        mean = sum(m for _, m in pieces) * (1.0 / n)
        out = []
        for x, m in pieces:
            x = x.astype(F32) + (m - mean) * inv_scale
            if rp > rows:
                x = jnp.where(lax.broadcasted_iota(jnp.int32, (rp, B), 0) < rows, x, 0.0)
            out.append(x.astype(BF))
        return out

    odd = range(1, n_lat - 1, 2)
    pair_list = [(i, i ^ 1) for i in range(n_lat)]
    skew_list = [(i, i + 1) for i in odd] + [(i + 1, i) for i in odd]
    hop1_list = [(i, i + 2) for i in odd] + [(i + 1, i - 1) for i in odd]
    hop2_list = [(i + 2, i + 1) for i in odd] + [(i - 1, i) for i in odd]

    def lat_exchange(both, low, high, after=(), low_after=()):
        relay = lax.ppermute(high, "lat", hop1_list)
        pair = lax.ppermute(both, "lat", pair_list)
        skew_low = lax.ppermute(gate(low, low_after) if low_after else low, "lat", skew_list)
        skew_high = lax.ppermute(gate(relay, after) if after else relay, "lat", hop2_list)
        return pair, skew_low, skew_high, relay

    block_out = ((mp, B), BF)
    half_out = ((half, B), BF)

    def group_rows(part):
        tail = part[2 * step :, :].astype(F32)
        return [
            (part[j * rp : (j + 1) * rp, :], jnp.sum(tail[3 * j : 3 * j + 3, :], axis=0, keepdims=True))
            for j in range(2)
        ]

    def owner_body(*refs):
        parts, (both, low, high) = refs[:chips], refs[chips:]

        def put(lo, i, value):
            both[lo * 2 + i * rp : lo * 2 + (i + 1) * rp, :] = value
            out, at = (low, lo + i * rp) if i < chips else (high, lo + (i - chips) * rp)
            out[at : at + rp, :] = value

        for i in range(n):
            at = step + (i % 2) * rp
            put(half, i, parts[i // 2][at : at + rp, :])
        for i, x in enumerate(corrected([g for part in parts for g in group_rows(part)])):
            put(0, i, x)

    both_out = ((2 * mp, B), BF)
    first, first_low, first_high = kernel_call(
        owner_body, [both_out, block_out, block_out], [], m1_got, name="owner_first", after=[m2_parts[0]]
    )
    pair, skew_low, skew_high, relay = lat_exchange(first, first_low, first_high, after=[m2_got[1]])

    var_row = obs_var.reshape(1, cols)

    def whole(low, high):
        return jnp.concatenate([low[...], high[...]], axis=0)

    mat = ((B, B), BF)
    field = ((mp, B), F32)
    half_field = ((half, B), F32)

    def tiles_body(rb, ti, tt, first_ref, t_first, t_second, t_pair, t_skew, p1t):
        me, band = lax.axis_index("mem"), lax.axis_index("lat")
        first = region_start(rb, band, me)
        second = jnp.minimum(first + 1, nb - 1)
        below = jnp.maximum(band - 1, 0)
        even = lax.rem(band, 2) == 0
        for block, out in ((first, t_first), (second, t_second)):
            tile = tt[ti[band, block, 0]].astype(F32)
            out[...] = 0.5 * (tile + tile.T)
        up = tt[ti[band, first, 2]].astype(F32)
        down = tt[ti[below, region_start(rb, below, me), 2]].astype(F32).T
        t_pair[...] = jnp.where(even, up, down).astype(BF)
        t_skew[...] = jnp.where(even, down, up).astype(BF)
        p1t[...] = first_ref[0:mp, :].astype(F32).T.astype(BF)

    square = ((B, B), F32)
    t_first, t_second, t_pair, t_skew, p1t = kernel_call(
        tiles_body,
        [square, square, mat, mat, ((B, mp), BF)],
        [region_blocks, taper_index],
        [taper_tiles, first],
        name="tiles",
    )

    def first_body(first_ref, t_ref, p1t_ref, s1, z1):
        s1[...] = (t_ref[...] * dot_nn(p1t_ref[...], first_ref[0:mp, :])).astype(BF)
        z1[...] = dot_nn(first_ref[mp:, :], s1[...])

    s1, z1 = kernel_call(
        first_body, [mat, field], [], [first, t_first, p1t], name="first_cov"
    )

    def pair_body(t_ref, p1t_ref, pair_ref, z1_ref, qp, z1):
        qp[...] = (t_ref[...].astype(F32) * dot_nn(p1t_ref[...], pair_ref[0:mp, :])).astype(BF)
        z1[...] = z1_ref[...] + dot_nt(pair_ref[mp:, :], qp[...])

    qp, z1 = kernel_call(
        pair_body,
        [mat, field],
        [],
        [t_pair, p1t, pair, z1],
        name="pair_cov",
    )

    def east_body(rb, pm, ti, tt, p1t_ref, *refs):
        parts, (z1_ref, ce, z1, p2, r2) = refs[:chips], refs[chips:]
        me, band = lax.axis_index("mem"), lax.axis_index("lat")
        first = region_start(rb, band, me)
        for k in range(chips):
            r2[k * step : (k + 1) * step, :] = parts[k][step : 2 * step, :]
        for i, x in enumerate(corrected([g for part in parts for g in group_rows(part)])):
            p2[i * rp : (i + 1) * rp, :] = x
        active = ((rb[band, me] > 1) & (pm[band, first] == 1)).astype(F32)
        tile_east = tt[ti[band, first, 1]].astype(F32) * active
        ce[...] = (tile_east * dot_nn(p1t_ref[...], p2[...])).astype(BF)
        z1[...] = z1_ref[...] + dot_nt(r2[...], ce[...])

    ce, z1, p2, r2 = kernel_call(
        east_body,
        [mat, field, block_out, block_out],
        [region_blocks, pair_mask, taper_index],
        [taper_tiles, p1t, *m2_got, z1],
        name="east_cov",
    )

    def skew_body(t_ref, p1t_ref, sl, sh, z1_ref, qs, z1):
        skew_p = jnp.concatenate([sl[0:half, :], sh[0:half, :]], axis=0)
        skew_r = jnp.concatenate([sl[half:, :], sh[half:, :]], axis=0)
        qs[...] = (t_ref[...].astype(F32) * dot_nn(p1t_ref[...], skew_p)).astype(BF)
        z1[...] = z1_ref[...] + dot_nt(skew_r, qs[...])

    qs, z1 = kernel_call(
        skew_body,
        [mat, field],
        [],
        [t_skew, p1t, skew_low, skew_high, z1],
        name="skew_cov",
    )

    def direction_body(rb, coef, var, first_ref, z1_ref, d1, d1l, d1h, t1):
        me, band = lax.axis_index("mem"), lax.axis_index("lat")
        first = region_start(rb, band, me)
        inv_c, keep1, gain1, keep2, gain2 = coefficients(coef)
        var1 = var[:, block_cols(first, B)]
        prod = z1_ref[...]
        r1f = first_ref[mp:, :].astype(F32)
        d0 = r1f * inv_c
        res = r1f - (var1 * d0 + prod * inv_c)
        d = keep1 * d0 + gain1 * res
        db = d.astype(BF)
        d1[...] = db
        d1l[...] = db[0:half, :]
        d1h[...] = db[half:mp, :]
        t1[...] = (1.0 + keep2) * d + gain2 * (res - var1 * d)

    d1, d1_low, d1_high, t1 = kernel_call(
        direction_body,
        [block_out, half_out, half_out, field],
        [region_blocks],
        [coef, var_row, first, z1],
        name="direction_first",
    )
    def inner_body(
        rb, coef, t_ref, var, p2_ref, r2_ref, first_ref, s1_ref, ce_ref, d1_ref, t1_ref, w1, *outs
    ):
        me, band = lax.axis_index("mem"), lax.axis_index("lat")
        second = jnp.minimum(region_start(rb, band, me) + 1, nb - 1)
        inv_c, keep1, gain1, keep2, gain2 = coefficients(coef)
        d1v, r2v, cev = d1_ref[...], r2_ref[...], ce_ref[...]
        s2 = (t_ref[...] * dot_tn(p2_ref[...], p2_ref[...])).astype(BF)
        prod = dot_nn(r2v, s2) + dot_nn(first_ref[mp:, :], cev)
        var2 = var[:, block_cols(second, B)]
        r2f = r2v.astype(F32)
        d0 = r2f * inv_c
        res = r2f - (var2 * d0 + prod * inv_c)
        d2 = keep1 * d0 + gain1 * res
        d2b = d2.astype(BF)
        w1[...] = t1_ref[...] - gain2 * (dot_nn(d1v, s1_ref[...]) + dot_nt(d2b, cev))
        sol = (1.0 + keep2) * d2 + gain2 * (res - var2 * d2 - dot_nn(d2b, s2) - dot_nn(d1v, cev))
        outs[0][...] = sol[0:half, :].astype(BF)
        for k in range(top, chips):
            outs[k - top + 1][...] = sol[k * step : (k + 1) * step, :].astype(BF)

    w1, sol2_near, *sol2_far = kernel_call(
        inner_body,
        [field, half_out] + [((step, B), BF)] * top,
        [region_blocks],
        [coef, t_second, var_row, p2, r2, first, s1, ce, d1, t1],
        name="inner_step",
    )
    d1_pair, d1_skew_low, d1_skew_high, d1_relay = lat_exchange(d1, d1_low, d1_high, low_after=[w1], after=[w1])
    sol2_far = [z_send(gate(x, [d1_relay]), k + top) for k, x in list(enumerate(sol2_far))[::-1]][::-1]

    def outer_body(coef, qp_ref, qs_ref, dp, dsl, dsh, w1_ref, near_ref, *outs):
        gain2 = coefficients(coef)[4]
        prod = dot_nt(dp[...], qp_ref[...]) + dot_nt(whole(dsl, dsh), qs_ref[...])
        sol = w1_ref[...] - gain2 * prod
        for i in range(n):
            rows_i = slice(i * rp, (i + 1) * rp)
            if i < chips:
                outs[i][0:rp, :] = sol[rows_i, :].astype(BF)
                outs[i][rp:step, :] = near_ref[rows_i, :]
            else:
                at = (i % 2) * rp
                outs[chips + (i - chips) // 2][at : at + rp, :] = sol[rows_i, :].astype(BF)

    sol1 = kernel_call(
        outer_body,
        [((step, B), BF)] * (chips + top),
        [],
        [coef, qp, qs, d1_pair, d1_skew_low, d1_skew_high, w1, sol2_near],
        name="outer_step",
    )
    sol1_far = [z_send(x, k + top) for k, x in list(enumerate(sol1[chips:]))[::-1]][::-1]
    sol1_near = [
        x if i == 0 else lax.ppermute(x, "mem", [(q, q ^ i) for q in range(n)])
        for i, x in enumerate(sol1[:chips])
    ]

    def peer_body(*refs):
        for k in range(2 * top):
            refs[2 * top][k] = refs[k][rp:step, :]

    (peer,) = kernel_call(
        peer_body, [((2 * top, rp, B), BF)], [], [*sol1_far, *sol2_far], name="peer_rows", after=sol1_near[1:]
    )
    peer = swap_core(peer)

    def unpack_body(rb, coef, inn, *refs):
        near, far1, far2 = refs[:chips], refs[chips : chips + top], refs[chips + top : 2 * chips]
        peer, out = refs[2 * chips :]
        me, band = lax.axis_index("mem"), lax.axis_index("lat")
        inv_c = coefficients(coef)[0]

        def pieces(i):
            k = i // 2 - top
            if k < 0:
                return near[i][0:rows, :], near[i][rp : rp + rows, :]
            if i % 2:
                return peer[k, 0:rows, :], peer[top + k, 0:rows, :]
            return far1[k][0:rows, :], far2[k][0:rows, :]

        for i in range(n):
            owner = me ^ i
            first = region_start(rb, band, owner)
            at = block_cols(first, B)
            out[:, at] = inn[:, at] * inv_c + pieces(i)[0].astype(F32)
            second = jnp.minimum(first + 1, nb - 1)

            @pl.when(rb[band, owner] > 1)
            def _(i=i, second=second):
                at2 = block_cols(second, B)
                out[:, at2] = inn[:, at2] * inv_c + pieces(i)[1].astype(F32)

    (out,) = kernel_call(
        unpack_body,
        [((rows, cols), F32)],
        [region_blocks],
        [coef, innovations, *sol1_near, *sol1_far, *sol2_far, peer],
        name="unpack",
    )
    return out


def solution(mesh):
    return jax.shard_map(
        on_device,
        mesh=mesh,
        in_specs=(P("mem", "lat"), P("mem", "lat"), P("lat"), P(), P(), P(), P(), P(), P()),
        out_specs=P("mem", "lat"),
        check_vma=False,
    )
```

time: 102 us -> 90.1 us (0.88)
  starting transfers between devices: 47.2 us -> 37.3 us
  Pallas kernels: 20.1 us -> 14.9 us
  waiting for transfers between devices: 30.9 us -> 34.8 us
  local copies, waits for them, and re-layouts: 1.85 us -> 0.82 us
    ppermute x3 -> x6, starting transfers between devices: 1.86 us -> 10.1 us  [the longest x4 8.73 us: z_send(): return lax.ppermute(x, 'mem', [(i, i ^ 2 * k) for i in range(n)])]
    ppermute x9 -> x6, starting transfers between devices: 19.3 us -> 11.9 us  [z_exchange(): got[k] = lax.ppermute(parts[k], 'mem', [(i, i ^ 2 * k) for i in range(n)])]
    ppermute x7 -> x3, starting transfers between devices: 8.5 us -> 1.93 us  [on_device(): lax.ppermute(x, 'mem', [(q, q ^ i) for q in range(n)])]
    ppermute x2, waiting for transfers between devices: 0.01 us -> 6.48 us  [lat_exchange(): relay = lax.ppermute(high, 'lat', hop1_list)]
    ppermute x9 -> x6, waiting for transfers between devices: 22.3 us -> 16.6 us  [z_exchange(): got[k] = lax.ppermute(parts[k], 'mem', [(i, i ^ 2 * k) for i in range(n)])]
    pallas_call x13 -> x14, Pallas kernels: 20.1 us -> 14.9 us  [kernel_call(): pl.pallas_call(run, out_shape=tuple((jax.ShapeDtypeStruct(s, d) for s, d...]
    ppermute x3 -> x6, waiting for transfers between devices: 0.01 us -> 4.41 us  [the longest x4 4.41 us: z_send(): return lax.ppermute(x, 'mem', [(i, i ^ 2 * k) for i in range(n)])]
    ppermute x2, starting transfers between devices: 9.36 us -> 5.84 us  [lat_exchange(): lax.ppermute(gate(relay, after) if after else relay, 'lat', hop2_list)]
  transfers between devices with their start and end apart: 27 -> 24, of which waited for: 8 -> 13; matrix products, arithmetic and copies ran while one was open for 0% -> 0% of each run, Pallas kernels for 10% -> 10%
where the time goes in v3:
time: 90.1 us; the launch traced here: 89.8 us
  starting transfers between devices  37.3 us (41%)
  waiting for transfers between devices  34.8 us (39%)
  Pallas kernels  14.9 us (17%)
  between operations  1.86 us (2%)
    ppermute x6, waiting for transfers between devices, z_exchange(): got[k] = lax.ppermute(parts[k], 'mem', [(i, i ^ 2 * k) for i in range(n)])  16.6 us
    pallas_call x14, Pallas kernels, kernel_call(): pl.pallas_call(run, out_shape=tuple((jax.ShapeDtypeStruct(s, d) for s, d...  14.9 us
    ppermute x6, starting transfers between devices, z_exchange(): got[k] = lax.ppermute(parts[k], 'mem', [(i, i ^ 2 * k) for i in range(n)])  11.9 us
    ppermute x4, starting transfers between devices, z_send(): return lax.ppermute(x, 'mem', [(i, i ^ 2 * k) for i in range(n)])  8.73 us
    ppermute x2, waiting for transfers between devices, lat_exchange(): relay = lax.ppermute(high, 'lat', hop1_list)  6.48 us
    ppermute x2, starting transfers between devices, lat_exchange(): lax.ppermute(gate(relay, after) if after else relay, 'lat', hop2_list)  5.84 us
    ppermute x4, waiting for transfers between devices, z_send(): return lax.ppermute(x, 'mem', [(i, i ^ 2 * k) for i in range(n)])  4.41 us
    ppermute x3, waiting for transfers between devices, on_device(): lax.ppermute(x, 'mem', [(q, q ^ i) for q in range(n)])  4.34 us
  transfers between devices with their start and end apart: 24, of which 13 were waited for; matrix products, arithmetic and copies ran while one was open for 0% of the time, Pallas kernels for 10%

profile of v3, /device:TPU:0, one launch (start us, length us, event | category | flops | bytes accessed | tf_op | source)
XLA Modules:
  0.0 89.8 jit_solution(6745960028481484176)
XLA Ops:
  0.0 0.7 copy-done.4
  0.7 2.3 %pack.1 = (bf16[4,104,512]{2,1,0:T(8,128)(2,1)S(1)}, bf16[4,104,512]{2,1,0:T(8,128)(2,1)S(1)}, bf16[4,104,512]{2,1,0:T(8,128)(2,1)S(1)}, bf16[4,104,512]{2,1,0:T(8,128)(2,1)S(1)}) custom-call(s32[4,8]{1,0:T(4,128)S(1)} %copy-done.4, f32[48,6144]{1,0:T(8,128)} %refs_1_.3, f32[48,6144]{1,0:T(8,128)} %refs_2_.7), custom_call_target="tpu_custom_call" | custom-call | flops 3000000000 | bytes 30000000 | tf_op jit(solution)/shard_map/pack/pallas_call | solution.py:28
  3.0 0.5 collective-permute-start
  3.5 0.1 collective-permute-start.4
  5.2 0.1 copy.16.refs_2_.refs_1_
  5.3 0.1 select_select_fusion.refs_5_.refs_1_.refs_0_
  5.4 0.0 collective-permute-done.refs_1_
  5.4 0.0 copy-start.5
  5.5 0.1 join_first.1
  5.5 3.1 %collective-permute-start.1 = (bf16[200,512]{1,0:T(8,128)(2,1)S(1)}, bf16[200,512]{1,0:T(8,128)(2,1)S(1)}, u32[]{:S(2)}, u32[]{:S(2)}) collective-permute-start(bf16[200,512]{1,0:T(8,128)(2,1)S(1)} %get-tuple-element.52), channel_id=1, source_target_pairs={{0,8},{4,12},{8,0},{12,4},{16,24},{20,28},{24,16},{28,20},{1,9},{5... | collective-permute-start | bytes 614408 | tf_op jit(solution)/shard_map/ppermute | solution.py:196
  8.6 2.6 %collective-permute-start.2 = (bf16[200,512]{1,0:T(8,128)(2,1)S(1)}, bf16[200,512]{1,0:T(8,128)(2,1)S(1)}, u32[]{:S(2)}, u32[]{:S(2)}) collective-permute-start(bf16[200,512]{1,0:T(8,128)(2,1)S(1)} %get-tuple-element.53), channel_id=1, source_target_pairs={{0,16},{4,20},{8,24},{12,28},{16,0},{20,4},{24,8},{28,12},{1,17},{... | collective-permute-start | bytes 614408 | tf_op jit(solution)/shard_map/ppermute | solution.py:196
  11.2 0.0 collective-permute-start.3
  11.2 0.0 collective-permute-done.4.refs_1_
  11.2 0.1 join_second.1
  11.3 6.4 %collective-permute-done.1.refs_1_ = bf16[200,512]{1,0:T(8,128)(2,1)S(1)} collective-permute-done((bf16[200,512]{1,0:T(8,128)(2,1)S(1)}, bf16[200,512]{1,0:T(8,128)(2,1)S(1)}, u32[]{:S(2)}, u32[]{:S(2)}) %collective-permute-start.1) | collective-permute-done | bytes 204832 | tf_op jit(solution)/shard_map/ppermute | solution.py:196
  17.7 8.6 %collective-permute-done.2.refs_2_ = bf16[200,512]{1,0:T(8,128)(2,1)S(1)} collective-permute-done((bf16[200,512]{1,0:T(8,128)(2,1)S(1)}, bf16[200,512]{1,0:T(8,128)(2,1)S(1)}, u32[]{:S(2)}, u32[]{:S(2)}) %collective-permute-start.2) | collective-permute-done | bytes 204832 | tf_op jit(solution)/shard_map/ppermute | solution.py:196
  26.2 0.0 collective-permute-done.3.refs_3_
  26.2 0.2 owner_first.1
  26.4 1.6 %collective-permute-start.5 = (bf16[768,512]{1,0:T(8,128)(2,1)S(1)}, bf16[768,512]{1,0:T(8,128)(2,1)S(1)}, u32[]{:S(2)}, u32[]{:S(2)}) collective-permute-start(bf16[768,512]{1,0:T(8,128)(2,1)S(1)} %get-tuple-element.58.refs_3_.refs_0_.refs_6_), channel_id=1, source_target_pairs={{0,1},{1,0},{2,3},{3,2},{4,5},{5,4},{6,7},{7,6},{8,9},{9,8},{10,11... | collective-permute-start | bytes 2359304 | tf_op jit(solution)/shard_map/ppermute | solution.py:245
  28.0 3.8 %collective-permute-start.8 = (bf16[200,512]{1,0:T(8,128)(2,1)S(1)}, bf16[200,512]{1,0:T(8,128)(2,1)S(1)}, u32[]{:S(2)}, u32[]{:S(2)}) collective-permute-start(bf16[200,512]{1,0:T(8,128)(2,1)S(1)} %get-tuple-element.67), channel_id=1, source_target_pairs={{0,8},{4,12},{8,0},{12,4},{16,24},{20,28},{24,16},{28,20},{1,9},{5... | collective-permute-start | bytes 614408 | tf_op jit(solution)/shard_map/ppermute | solution.py:196
  31.8 1.0 %collective-permute-start.10 = (bf16[200,512]{1,0:T(8,128)(2,1)S(1)}, bf16[200,512]{1,0:T(8,128)(2,1)S(1)}, u32[]{:S(2)}, u32[]{:S(2)}) collective-permute-start(bf16[200,512]{1,0:T(8,128)(2,1)S(1)} %get-tuple-element.68), channel_id=1, source_target_pairs={{0,16},{4,20},{8,24},{12,28},{16,0},{20,4},{24,8},{28,12},{1,17},{... | collective-permute-start | bytes 614408 | tf_op jit(solution)/shard_map/ppermute | solution.py:196
  32.8 1.5 %collective-permute-start.11 = (bf16[200,512]{1,0:T(8,128)(2,1)S(1)}, bf16[200,512]{1,0:T(8,128)(2,1)S(1)}, u32[]{:S(2)}, u32[]{:S(2)}) collective-permute-start(bf16[200,512]{1,0:T(8,128)(2,1)S(1)} %get-tuple-element.69), channel_id=1, source_target_pairs={{0,24},{4,28},{8,16},{12,20},{16,8},{20,12},{24,0},{28,4},{1,25},{... | collective-permute-start | bytes 614408 | tf_op jit(solution)/shard_map/ppermute | solution.py:196
  34.2 1.3 %collective-permute-start.7 = (bf16[384,512]{1,0:T(8,128)(2,1)S(1)}, bf16[384,512]{1,0:T(8,128)(2,1)S(1)}, u32[]{:S(2)}, u32[]{:S(2)}) collective-permute-start(bf16[384,512]{1,0:T(8,128)(2,1)S(1)} %get-tuple-element.66), channel_id=1, source_target_pairs={{1,3},{2,0},{5,7},{6,4},{9,11},{10,8},{13,15},{14,12},{17,19},{18,... | collective-permute-start | bytes 1179656 | tf_op jit(solution)/shard_map/ppermute | solution.py:244
  35.5 2.0 %tiles.1 = (f32[512,512]{1,0:T(8,128)S(1)}, f32[512,512]{1,0:T(8,128)S(1)}, bf16[512,512]{1,0:T(8,128)(2,1)S(1)}, bf16[512,512]{1,0:T(8,128)(2,1)S(1)}, bf16[512,384]{1,0:T(8,128)(2,1)S(1)}) custom-call(s32[4,8]{1,0:T(4,128)S(1)} %copy-done.5, s32[4,12,3]{2,1,0:T(8,128)S(1)} %copy.16.refs_2_.refs_1_, bf16[2,512,512]{2,1,0:T(8,128)(2,1)S(1)} %copy-done.1, ...), custom_call_target="tpu_custom_call" | custom-call | flops 3000000000 | bytes 30000000 | tf_op jit(solution)/shard_map/tiles/pallas_call | solution.py:28
  37.6 0.7 first_cov.1
  38.3 0.1 collective-permute-done.8.refs_1_.refs_6_
  38.4 0.7 collective-permute-start.6
  39.1 6.2 %collective-permute-done.7.refs_0_ = bf16[384,512]{1,0:T(8,128)(2,1)S(1)} collective-permute-done((bf16[384,512]{1,0:T(8,128)(2,1)S(1)}, bf16[384,512]{1,0:T(8,128)(2,1)S(1)}, u32[]{:S(2)}, u32[]{:S(2)}) %collective-permute-start.7) | collective-permute-done | bytes 393248 | tf_op jit(solution)/shard_map/ppermute | solution.py:244
  45.3 1.5 %collective-permute-start.9 = (bf16[384,512]{1,0:T(8,128)(2,1)S(1)}, bf16[384,512]{1,0:T(8,128)(2,1)S(1)}, u32[]{:S(2)}, u32[]{:S(2)}) collective-permute-start(bf16[384,512]{1,0:T(8,128)(2,1)S(1)} %gate.5), channel_id=1, source_target_pairs={{3,2},{0,1},{7,6},{4,5},{11,10},{8,9},{15,14},{12,13},{19,18},{16,... | collective-permute-start | bytes 1179656 | tf_op jit(solution)/shard_map/ppermute | solution.py:247
  46.8 0.0 collective-permute-done.5.refs_2_
  46.8 0.8 pair_cov.1
  47.5 1.5 %collective-permute-done.10.refs_7_ = bf16[200,512]{1,0:T(8,128)(2,1)S(1)} collective-permute-done((bf16[200,512]{1,0:T(8,128)(2,1)S(1)}, bf16[200,512]{1,0:T(8,128)(2,1)S(1)}, u32[]{:S(2)}, u32[]{:S(2)}) %collective-permute-start.10) | collective-permute-done | bytes 204832 | tf_op jit(solution)/shard_map/ppermute | solution.py:196
  49.1 0.0 collective-permute-done.11.refs_8_
  49.1 2.0 %east_cov.1 = (bf16[512,512]{1,0:T(8,128)(2,1)S(1)}, f32[384,512]{1,0:T(8,128)S(1)}, bf16[384,512]{1,0:T(8,128)(2,1)S(1)}, bf16[384,512]{1,0:T(8,128)(2,1)S(1)}) custom-call(s32[4,8]{1,0:T(4,128)S(1)} %copy-done.5, s32[4,12]{1,0:T(4,128)S(1)} %copy-done.3, s32[4,12,3]{2,1,0:T(8,128)S(1)} %copy.16.refs_2_.refs_1_, bf16[2,512,512]{2,1,0:T(8,128)(2,1)S(1)} %copy-done.1, ...), custom_call_target="tpu_custom_call" | custom-call | flops 3000000000 | bytes 30000000 | tf_op jit(solution)/shard_map/east_cov/pallas_call | solution.py:28
  51.1 0.0 collective-permute-done.6.refs_2_
  51.1 1.5 %collective-permute-done.9.refs_3_ = bf16[384,512]{1,0:T(8,128)(2,1)S(1)} collective-permute-done((bf16[384,512]{1,0:T(8,128)(2,1)S(1)}, bf16[384,512]{1,0:T(8,128)(2,1)S(1)}, u32[]{:S(2)}, u32[]{:S(2)}) %collective-permute-start.9) | collective-permute-done | bytes 393248 | tf_op jit(solution)/shard_map/ppermute | solution.py:247
  52.6 0.8 skew_cov.1
  53.3 1.0 %direction_first.1 = (bf16[384,512]{1,0:T(8,128)(2,1)S(1)}, bf16[192,512]{1,0:T(8,128)(2,1)S(1)}, bf16[192,512]{1,0:T(8,128)(2,1)S(1)}, f32[384,512]{1,0:T(8,128)S(1)}) custom-call(s32[4,8]{1,0:T(4,128)S(1)} %copy-done.5, f32[8,512]{1,0:T(8,128)S(1)} %select_select_fusion.refs_5_.refs_1_.refs_0_, f32[1,6144]{1,0:T(1,128)S(1)} %bitcast.3, ...), custom_call_target="tpu_custom_call" | custom-call | flops 3000000000 | bytes 30000000 | tf_op jit(solution)/shard_map/direction_first/pallas_call | solution.py:28
  54.3 1.3 %collective-permute-start.14 = (bf16[192,512]{1,0:T(8,128)(2,1)S(1)}, bf16[192,512]{1,0:T(8,128)(2,1)S(1)}, u32[]{:S(2)}, u32[]{:S(2)}) collective-permute-start(bf16[192,512]{1,0:T(8,128)(2,1)S(1)} %get-tuple-element.83), channel_id=1, source_target_pairs={{1,3},{2,0},{5,7},{6,4},{9,11},{10,8},{13,15},{14,12},{17,19},{18,... | collective-permute-start | bytes 589832 | tf_op jit(solution)/shard_map/ppermute | solution.py:244
  55.6 2.7 %collective-permute-start.12 = (bf16[384,512]{1,0:T(8,128)(2,1)S(1)}, bf16[384,512]{1,0:T(8,128)(2,1)S(1)}, u32[]{:S(2)}, u32[]{:S(2)}) collective-permute-start(bf16[384,512]{1,0:T(8,128)(2,1)S(1)} %get-tuple-element.74.refs_9_), channel_id=1, source_target_pairs={{0,1},{1,0},{2,3},{3,2},{4,5},{5,4},{6,7},{7,6},{8,9},{9,8},{10,11... | collective-permute-start | bytes 1179656 | tf_op jit(solution)/shard_map/ppermute | solution.py:245
  58.3 2.5 %inner_step.1 = (f32[384,512]{1,0:T(8,128)S(1)}, bf16[192,512]{1,0:T(8,128)(2,1)S(1)}, bf16[96,512]{1,0:T(8,128)(2,1)S(1)}, bf16[96,512]{1,0:T(8,128)(2,1)S(1)}) custom-call(s32[4,8]{1,0:T(4,128)S(1)} %copy-done.5, f32[8,512]{1,0:T(8,128)S(1)} %select_select_fusion.refs_5_.refs_1_.refs_0_, f32[512,512]{1,0:T(8,128)S(1)} %get-tuple-element.76.refs_2_, ...), custom_call_target="tpu_custom_call" | custom-call | flops 3000000000 | bytes 30000000 | tf_op jit(solution)/shard_map/inner_step/pallas_call | solution.py:28
  60.9 0.7 collective-permute-start.13
  61.6 0.3 collective-permute-done.14.refs_0_.refs_1_
  61.9 4.3 %collective-permute-start.15 = (bf16[192,512]{1,0:T(8,128)(2,1)S(1)}, bf16[192,512]{1,0:T(8,128)(2,1)S(1)}, u32[]{:S(2)}, u32[]{:S(2)}) collective-permute-start(bf16[192,512]{1,0:T(8,128)(2,1)S(1)} %gate.7), channel_id=1, source_target_pairs={{3,2},{0,1},{7,6},{4,5},{11,10},{8,9},{15,14},{12,13},{19,18},{16,... | collective-permute-start | bytes 589832 | tf_op jit(solution)/shard_map/ppermute | solution.py:247
  66.2 4.7 %collective-permute-start.21 = (bf16[96,512]{1,0:T(8,128)(2,1)S(1)}, bf16[96,512]{1,0:T(8,128)(2,1)S(1)}, u32[]{:S(2)}, u32[]{:S(2)}) collective-permute-start(bf16[96,512]{1,0:T(8,128)(2,1)S(1)} %gate.8), channel_id=1, source_target_pairs={{0,16},{4,20},{8,24},{12,28},{16,0},{20,4},{24,8},{28,12},{1,17},{... | collective-permute-start | bytes 294920 | tf_op jit(solution)/shard_map/ppermute | solution.py:203
  70.9 1.3 %collective-permute-start.22 = (bf16[96,512]{1,0:T(8,128)(2,1)S(1)}, bf16[96,512]{1,0:T(8,128)(2,1)S(1)}, u32[]{:S(2)}, u32[]{:S(2)}) collective-permute-start(bf16[96,512]{1,0:T(8,128)(2,1)S(1)} %gate.9), channel_id=1, source_target_pairs={{0,24},{4,28},{8,16},{12,20},{16,8},{20,12},{24,0},{28,4},{1,25},{... | collective-permute-start | bytes 294920 | tf_op jit(solution)/shard_map/ppermute | solution.py:203
  72.2 0.0 collective-permute-done.13.refs_4_
  72.2 0.0 collective-permute-done.15.refs_5_
  72.2 0.6 outer_step.1
  72.9 0.1 collective-permute-start.16
  72.9 1.3 %collective-permute-start.17 = (bf16[96,512]{1,0:T(8,128)(2,1)S(1)}, bf16[96,512]{1,0:T(8,128)(2,1)S(1)}, u32[]{:S(2)}, u32[]{:S(2)}) collective-permute-start(bf16[96,512]{1,0:T(8,128)(2,1)S(1)} %get-tuple-element.87), channel_id=1, source_target_pairs={{0,8},{4,12},{8,0},{12,4},{16,24},{20,28},{24,16},{28,20},{1,9},{5... | collective-permute-start | bytes 294920 | tf_op jit(solution)/shard_map/ppermute | solution.py:444
  74.2 0.6 collective-permute-start.18
  74.8 0.8 collective-permute-done.21.refs_2_.refs_9_
  75.6 1.5 %collective-permute-start.19 = (bf16[96,512]{1,0:T(8,128)(2,1)S(1)}, bf16[96,512]{1,0:T(8,128)(2,1)S(1)}, u32[]{:S(2)}, u32[]{:S(2)}) collective-permute-start(bf16[96,512]{1,0:T(8,128)(2,1)S(1)} %get-tuple-element.89), channel_id=1, source_target_pairs={{0,16},{4,20},{8,24},{12,28},{16,0},{20,4},{24,8},{28,12},{1,17},{... | collective-permute-start | bytes 294920 | tf_op jit(solution)/shard_map/ppermute | solution.py:203
  77.1 0.4 collective-permute-done.22.refs_3_.refs_10_
  77.5 1.2 %collective-permute-start.20 = (bf16[96,512]{1,0:T(8,128)(2,1)S(1)}, bf16[96,512]{1,0:T(8,128)(2,1)S(1)}, u32[]{:S(2)}, u32[]{:S(2)}) collective-permute-start(bf16[96,512]{1,0:T(8,128)(2,1)S(1)} %get-tuple-element.90), channel_id=1, source_target_pairs={{0,24},{4,28},{8,16},{12,20},{16,8},{20,12},{24,0},{28,4},{1,25},{... | collective-permute-start | bytes 294920 | tf_op jit(solution)/shard_map/ppermute | solution.py:203
  78.7 0.0 collective-permute-done.16.refs_4_
  78.7 2.4 %collective-permute-done.17.refs_5_ = bf16[96,512]{1,0:T(8,128)(2,1)S(1)} collective-permute-done((bf16[96,512]{1,0:T(8,128)(2,1)S(1)}, bf16[96,512]{1,0:T(8,128)(2,1)S(1)}, u32[]{:S(2)}, u32[]{:S(2)}) %collective-permute-start.17) | collective-permute-done | bytes 98336 | tf_op jit(solution)/shard_map/ppermute | solution.py:444
  81.2 1.9 %collective-permute-done.18.refs_6_ = bf16[96,512]{1,0:T(8,128)(2,1)S(1)} collective-permute-done((bf16[96,512]{1,0:T(8,128)(2,1)S(1)}, bf16[96,512]{1,0:T(8,128)(2,1)S(1)}, u32[]{:S(2)}, u32[]{:S(2)}) %collective-permute-start.18) | collective-permute-done | bytes 98336 | tf_op jit(solution)/shard_map/ppermute | solution.py:444
  83.1 3.2 %collective-permute-done.19.refs_0_.refs_7_ = bf16[96,512]{1,0:T(8,128)(2,1)S(1)} collective-permute-done((bf16[96,512]{1,0:T(8,128)(2,1)S(1)}, bf16[96,512]{1,0:T(8,128)(2,1)S(1)}, u32[]{:S(2)}, u32[]{:S(2)}) %collective-permute-start.19) | collective-permute-done | bytes 98336 | tf_op jit(solution)/shard_map/ppermute | solution.py:203
  86.3 0.0 collective-permute-done.20.refs_1_.refs_8_
  86.3 0.1 collective-permute-start.23
  86.4 1.4 %collective-permute-done.23.refs_11_ = bf16[4,48,512]{2,1,0:T(8,128)(2,1)S(1)} collective-permute-done((bf16[4,48,512]{2,1,0:T(8,128)(2,1)S(1)}, bf16[4,48,512]{2,1,0:T(8,128)(2,1)S(1)}, u32[]{:S(2)}, u32[]{:S(2)}) %collective-permute-start.23) | collective-permute-done | bytes 196640 | tf_op jit(solution)/shard_map/ppermute | solution.py:191
  87.8 1.9 %unpack.1 = f32[48,6144]{1,0:T(8,128)} custom-call(s32[4,8]{1,0:T(4,128)S(1)} %copy-done.5, f32[8,512]{1,0:T(8,128)S(1)} %select_select_fusion.refs_5_.refs_1_.refs_0_, f32[48,6144]{1,0:T(8,128)S(1)} %copy-done, bf16[96,512]{1,0:T(8,128)(2,1)S(1)} %get-tuple-element.85.refs_3_, bf16[96,512]{1,0:T(8,128)(2,1)S(1)} %collective-permute-done.16.refs_4_, ...), custom_call_target="tpu_custom_call" | custom-call | flops 3000000000 | bytes 30000000 | tf_op jit(solution)/shard_map/unpack/pallas_call | solution.py:28
  (22 shorter events, 0.1 us)
Async XLA Ops:
  0.0 0.7 copy-start.4
  0.7 4.5 %copy-start.6 = (s32[4,12,3]{1,0,2:T(4,128)S(1)}, s32[4,12,3]{1,0,2:T(4,128)}, u32[]{:S(2)}) copy-start(s32[4,12,3]{1,0,2:T(4,128)} %param.15) | copy-start | bytes 1732
  3.0 2.4 %collective-permute-start = (bf16[4,104,512]{2,1,0:T(8,128)(2,1)S(1)}, bf16[4,104,512]{2,1,0:T(8,128)(2,1)S(1)}, u32[]{:S(2)}, u32[]{:S(2)}) collective-permute-start(bf16[4,104,512]{2,1,0:T(8,128)(2,1)S(1)} %get-tuple-element.50), channel_id=1, source_target_pairs={{0,4},{4,0},{8,12},{12,8},{16,20},{20,16},{24,28},{28,24},{1,5},{5... | collective-permute-start | bytes 1277960 | tf_op jit(solution)/shard_map/ppermute | solution.py:191
  3.5 7.7 %collective-permute-start.4 = (bf16[4,104,512]{2,1,0:T(8,128)(2,1)S(1)}, bf16[4,104,512]{2,1,0:T(8,128)(2,1)S(1)}, u32[]{:S(2)}, u32[]{:S(2)}) collective-permute-start(bf16[4,104,512]{2,1,0:T(8,128)(2,1)S(1)} %get-tuple-element.56), channel_id=1, source_target_pairs={{0,4},{4,0},{8,12},{12,8},{16,20},{20,16},{24,28},{28,24},{1,5},{5... | collective-permute-start | bytes 1277960 | tf_op jit(solution)/shard_map/ppermute | solution.py:191
  5.4 5.8 %copy-start.3 = (s32[4,12]{1,0:T(4,128)S(1)}, s32[4,12]{1,0:T(4,128)}, u32[]{:S(2)}) copy-start(s32[4,12]{1,0:T(4,128)} %refs_1_.4) | copy-start | bytes 580
  5.4 5.8 %copy-start.5 = (s32[4,8]{1,0:T(4,128)S(1)}, s32[4,8]{1,0:T(4,128)}, u32[]{:S(2)}) copy-start(s32[4,8]{1,0:T(4,128)} %refs_0_.11) | copy-start | bytes 388
  5.5 12.1 %collective-permute-start.1 = (bf16[200,512]{1,0:T(8,128)(2,1)S(1)}, bf16[200,512]{1,0:T(8,128)(2,1)S(1)}, u32[]{:S(2)}, u32[]{:S(2)}) collective-permute-start(bf16[200,512]{1,0:T(8,128)(2,1)S(1)} %get-tuple-element.52), channel_id=1, source_target_pairs={{0,8},{4,12},{8,0},{12,4},{16,24},{20,28},{24,16},{28,20},{1,9},{5... | collective-permute-start | bytes 614408 | tf_op jit(solution)/shard_map/ppermute | solution.py:196
  8.6 17.6 %collective-permute-start.2 = (bf16[200,512]{1,0:T(8,128)(2,1)S(1)}, bf16[200,512]{1,0:T(8,128)(2,1)S(1)}, u32[]{:S(2)}, u32[]{:S(2)}) collective-permute-start(bf16[200,512]{1,0:T(8,128)(2,1)S(1)} %get-tuple-element.53), channel_id=1, source_target_pairs={{0,16},{4,20},{8,24},{12,28},{16,0},{20,4},{24,8},{28,12},{1,17},{... | collective-permute-start | bytes 614408 | tf_op jit(solution)/shard_map/ppermute | solution.py:196
  11.2 15.1 %collective-permute-start.3 = (bf16[200,512]{1,0:T(8,128)(2,1)S(1)}, bf16[200,512]{1,0:T(8,128)(2,1)S(1)}, u32[]{:S(2)}, u32[]{:S(2)}) collective-permute-start(bf16[200,512]{1,0:T(8,128)(2,1)S(1)} %get-tuple-element.54), channel_id=1, source_target_pairs={{0,24},{4,28},{8,16},{12,20},{16,8},{20,12},{24,0},{28,4},{1,25},{... | collective-permute-start | bytes 614408 | tf_op jit(solution)/shard_map/ppermute | solution.py:196
  26.2 9.3 %copy-start.1 = (bf16[2,512,512]{2,1,0:T(8,128)(2,1)S(1)}, bf16[2,512,512]{2,1,0:T(8,128)(2,1)}, u32[]{:S(2)}) copy-start(bf16[2,512,512]{2,1,0:T(8,128)(2,1)} %refs_3_.3) | copy-start | bytes 3145732
  26.4 20.4 %collective-permute-start.5 = (bf16[768,512]{1,0:T(8,128)(2,1)S(1)}, bf16[768,512]{1,0:T(8,128)(2,1)S(1)}, u32[]{:S(2)}, u32[]{:S(2)}) collective-permute-start(bf16[768,512]{1,0:T(8,128)(2,1)S(1)} %get-tuple-element.58.refs_3_.refs_0_.refs_6_), channel_id=1, source_target_pairs={{0,1},{1,0},{2,3},{3,2},{4,5},{5,4},{6,7},{7,6},{8,9},{9,8},{10,11... | collective-permute-start | bytes 2359304 | tf_op jit(solution)/shard_map/ppermute | solution.py:245
  28.0 10.4 %collective-permute-start.8 = (bf16[200,512]{1,0:T(8,128)(2,1)S(1)}, bf16[200,512]{1,0:T(8,128)(2,1)S(1)}, u32[]{:S(2)}, u32[]{:S(2)}) collective-permute-start(bf16[200,512]{1,0:T(8,128)(2,1)S(1)} %get-tuple-element.67), channel_id=1, source_target_pairs={{0,8},{4,12},{8,0},{12,4},{16,24},{20,28},{24,16},{28,20},{1,9},{5... | collective-permute-start | bytes 614408 | tf_op jit(solution)/shard_map/ppermute | solution.py:196
  31.8 17.3 %collective-permute-start.10 = (bf16[200,512]{1,0:T(8,128)(2,1)S(1)}, bf16[200,512]{1,0:T(8,128)(2,1)S(1)}, u32[]{:S(2)}, u32[]{:S(2)}) collective-permute-start(bf16[200,512]{1,0:T(8,128)(2,1)S(1)} %get-tuple-element.68), channel_id=1, source_target_pairs={{0,16},{4,20},{8,24},{12,28},{16,0},{20,4},{24,8},{28,12},{1,17},{... | collective-permute-start | bytes 614408 | tf_op jit(solution)/shard_map/ppermute | solution.py:196
  32.8 16.3 %collective-permute-start.11 = (bf16[200,512]{1,0:T(8,128)(2,1)S(1)}, bf16[200,512]{1,0:T(8,128)(2,1)S(1)}, u32[]{:S(2)}, u32[]{:S(2)}) collective-permute-start(bf16[200,512]{1,0:T(8,128)(2,1)S(1)} %get-tuple-element.69), channel_id=1, source_target_pairs={{0,24},{4,28},{8,16},{12,20},{16,8},{20,12},{24,0},{28,4},{1,25},{... | collective-permute-start | bytes 614408 | tf_op jit(solution)/shard_map/ppermute | solution.py:196
  34.2 11.0 %collective-permute-start.7 = (bf16[384,512]{1,0:T(8,128)(2,1)S(1)}, bf16[384,512]{1,0:T(8,128)(2,1)S(1)}, u32[]{:S(2)}, u32[]{:S(2)}) collective-permute-start(bf16[384,512]{1,0:T(8,128)(2,1)S(1)} %get-tuple-element.66), channel_id=1, source_target_pairs={{1,3},{2,0},{5,7},{6,4},{9,11},{10,8},{13,15},{14,12},{17,19},{18,... | collective-permute-start | bytes 1179656 | tf_op jit(solution)/shard_map/ppermute | solution.py:244
  38.4 12.7 %collective-permute-start.6 = (bf16[384,512]{1,0:T(8,128)(2,1)S(1)}, bf16[384,512]{1,0:T(8,128)(2,1)S(1)}, u32[]{:S(2)}, u32[]{:S(2)}) collective-permute-start(bf16[384,512]{1,0:T(8,128)(2,1)S(1)} %get-tuple-element.65), channel_id=1, source_target_pairs={{1,2},{2,1},{5,6},{6,5},{9,10},{10,9},{13,14},{14,13},{17,18},{18,... | collective-permute-start | bytes 1179656 | tf_op jit(solution)/shard_map/ppermute | solution.py:246
  45.3 7.3 %collective-permute-start.9 = (bf16[384,512]{1,0:T(8,128)(2,1)S(1)}, bf16[384,512]{1,0:T(8,128)(2,1)S(1)}, u32[]{:S(2)}, u32[]{:S(2)}) collective-permute-start(bf16[384,512]{1,0:T(8,128)(2,1)S(1)} %gate.5), channel_id=1, source_target_pairs={{3,2},{0,1},{7,6},{4,5},{11,10},{8,9},{15,14},{12,13},{19,18},{16,... | collective-permute-start | bytes 1179656 | tf_op jit(solution)/shard_map/ppermute | solution.py:247
  52.6 0.8 copy-start.2
  54.3 7.6 %collective-permute-start.14 = (bf16[192,512]{1,0:T(8,128)(2,1)S(1)}, bf16[192,512]{1,0:T(8,128)(2,1)S(1)}, u32[]{:S(2)}, u32[]{:S(2)}) collective-permute-start(bf16[192,512]{1,0:T(8,128)(2,1)S(1)} %get-tuple-element.83), channel_id=1, source_target_pairs={{1,3},{2,0},{5,7},{6,4},{9,11},{10,8},{13,15},{14,12},{17,19},{18,... | collective-permute-start | bytes 589832 | tf_op jit(solution)/shard_map/ppermute | solution.py:244
  55.6 16.6 %collective-permute-start.12 = (bf16[384,512]{1,0:T(8,128)(2,1)S(1)}, bf16[384,512]{1,0:T(8,128)(2,1)S(1)}, u32[]{:S(2)}, u32[]{:S(2)}) collective-permute-start(bf16[384,512]{1,0:T(8,128)(2,1)S(1)} %get-tuple-element.74.refs_9_), channel_id=1, source_target_pairs={{0,1},{1,0},{2,3},{3,2},{4,5},{5,4},{6,7},{7,6},{8,9},{9,8},{10,11... | collective-permute-start | bytes 1179656 | tf_op jit(solution)/shard_map/ppermute | solution.py:245
  60.9 11.3 %collective-permute-start.13 = (bf16[192,512]{1,0:T(8,128)(2,1)S(1)}, bf16[192,512]{1,0:T(8,128)(2,1)S(1)}, u32[]{:S(2)}, u32[]{:S(2)}) collective-permute-start(bf16[192,512]{1,0:T(8,128)(2,1)S(1)} %gate.6), channel_id=1, source_target_pairs={{1,2},{2,1},{5,6},{6,5},{9,10},{10,9},{13,14},{14,13},{17,18},{18,... | collective-permute-start | bytes 589832 | tf_op jit(solution)/shard_map/ppermute | solution.py:246
  61.9 10.4 %collective-permute-start.15 = (bf16[192,512]{1,0:T(8,128)(2,1)S(1)}, bf16[192,512]{1,0:T(8,128)(2,1)S(1)}, u32[]{:S(2)}, u32[]{:S(2)}) collective-permute-start(bf16[192,512]{1,0:T(8,128)(2,1)S(1)} %gate.7), channel_id=1, source_target_pairs={{3,2},{0,1},{7,6},{4,5},{11,10},{8,9},{15,14},{12,13},{19,18},{16,... | collective-permute-start | bytes 589832 | tf_op jit(solution)/shard_map/ppermute | solution.py:247
  66.2 9.3 %collective-permute-start.21 = (bf16[96,512]{1,0:T(8,128)(2,1)S(1)}, bf16[96,512]{1,0:T(8,128)(2,1)S(1)}, u32[]{:S(2)}, u32[]{:S(2)}) collective-permute-start(bf16[96,512]{1,0:T(8,128)(2,1)S(1)} %gate.8), channel_id=1, source_target_pairs={{0,16},{4,20},{8,24},{12,28},{16,0},{20,4},{24,8},{28,12},{1,17},{... | collective-permute-start | bytes 294920 | tf_op jit(solution)/shard_map/ppermute | solution.py:203
  70.9 6.6 %collective-permute-start.22 = (bf16[96,512]{1,0:T(8,128)(2,1)S(1)}, bf16[96,512]{1,0:T(8,128)(2,1)S(1)}, u32[]{:S(2)}, u32[]{:S(2)}) collective-permute-start(bf16[96,512]{1,0:T(8,128)(2,1)S(1)} %gate.9), channel_id=1, source_target_pairs={{0,24},{4,28},{8,16},{12,20},{16,8},{20,12},{24,0},{28,4},{1,25},{... | collective-permute-start | bytes 294920 | tf_op jit(solution)/shard_map/ppermute | solution.py:203
  72.9 5.9 %collective-permute-start.16 = (bf16[96,512]{1,0:T(8,128)(2,1)S(1)}, bf16[96,512]{1,0:T(8,128)(2,1)S(1)}, u32[]{:S(2)}, u32[]{:S(2)}) collective-permute-start(bf16[96,512]{1,0:T(8,128)(2,1)S(1)} %get-tuple-element.86), channel_id=1, source_target_pairs={{0,4},{4,0},{8,12},{12,8},{16,20},{20,16},{24,28},{28,24},{1,5},{5... | collective-permute-start | bytes 294920 | tf_op jit(solution)/shard_map/ppermute | solution.py:444
  72.9 8.2 %collective-permute-start.17 = (bf16[96,512]{1,0:T(8,128)(2,1)S(1)}, bf16[96,512]{1,0:T(8,128)(2,1)S(1)}, u32[]{:S(2)}, u32[]{:S(2)}) collective-permute-start(bf16[96,512]{1,0:T(8,128)(2,1)S(1)} %get-tuple-element.87), channel_id=1, source_target_pairs={{0,8},{4,12},{8,0},{12,4},{16,24},{20,28},{24,16},{28,20},{1,9},{5... | collective-permute-start | bytes 294920 | tf_op jit(solution)/shard_map/ppermute | solution.py:444
  74.2 8.8 %collective-permute-start.18 = (bf16[96,512]{1,0:T(8,128)(2,1)S(1)}, bf16[96,512]{1,0:T(8,128)(2,1)S(1)}, u32[]{:S(2)}, u32[]{:S(2)}) collective-permute-start(bf16[96,512]{1,0:T(8,128)(2,1)S(1)} %get-tuple-element.88), channel_id=1, source_target_pairs={{0,12},{4,8},{8,4},{12,0},{16,28},{20,24},{24,20},{28,16},{1,13},{... | collective-permute-start | bytes 294920 | tf_op jit(solution)/shard_map/ppermute | solution.py:444
  75.6 10.7 %collective-permute-start.19 = (bf16[96,512]{1,0:T(8,128)(2,1)S(1)}, bf16[96,512]{1,0:T(8,128)(2,1)S(1)}, u32[]{:S(2)}, u32[]{:S(2)}) collective-permute-start(bf16[96,512]{1,0:T(8,128)(2,1)S(1)} %get-tuple-element.89), channel_id=1, source_target_pairs={{0,16},{4,20},{8,24},{12,28},{16,0},{20,4},{24,8},{28,12},{1,17},{... | collective-permute-start | bytes 294920 | tf_op jit(solution)/shard_map/ppermute | solution.py:203
  77.5 10.3 %copy-start = (f32[48,6144]{1,0:T(8,128)S(1)}, f32[48,6144]{1,0:T(8,128)}, u32[]{:S(2)}) copy-start(f32[48,6144]{1,0:T(8,128)} %refs_2_.7) | copy-start | bytes 3538948
  77.5 8.8 %collective-permute-start.20 = (bf16[96,512]{1,0:T(8,128)(2,1)S(1)}, bf16[96,512]{1,0:T(8,128)(2,1)S(1)}, u32[]{:S(2)}, u32[]{:S(2)}) collective-permute-start(bf16[96,512]{1,0:T(8,128)(2,1)S(1)} %get-tuple-element.90), channel_id=1, source_target_pairs={{0,24},{4,28},{8,16},{12,20},{16,8},{20,12},{24,0},{28,4},{1,25},{... | collective-permute-start | bytes 294920 | tf_op jit(solution)/shard_map/ppermute | solution.py:203
  86.3 1.5 %collective-permute-start.23 = (bf16[4,48,512]{2,1,0:T(8,128)(2,1)S(1)}, bf16[4,48,512]{2,1,0:T(8,128)(2,1)S(1)}, u32[]{:S(2)}, u32[]{:S(2)}) collective-permute-start(bf16[4,48,512]{2,1,0:T(8,128)(2,1)S(1)} %peer_rows.1), channel_id=1, source_target_pairs={{0,4},{4,0},{8,12},{12,8},{16,20},{20,16},{24,28},{28,24},{1,5},{5... | collective-permute-start | bytes 589832 | tf_op jit(solution)/shard_map/ppermute | solution.py:191

commit v4 on v3

--- a/solution.py
+++ b/solution.py
@@ -134,14 +134,19 @@
         tail = jnp.where(row == offset, high, tail)
         return mean, tail.astype(BF)
 
-    def blocks(rb, extra):
+    def owner_starts(rb):
         me, band = lax.axis_index("mem"), lax.axis_index("lat")
-        return [
-            block_cols(jnp.minimum(region_start(rb, band, me ^ i) + extra, nb - 1), B) for i in range(n)
-        ]
-
-    def fill_p(own, oth, at_row, rb, eq, extra):
-        for i, at in enumerate(blocks(rb, extra)):
+        prefix, starts = jnp.int32(0), [jnp.int32(0)] * n
+        for m in range(n):
+            starts = [jnp.where((me ^ i) == m, prefix, s) for i, s in enumerate(starts)]
+            prefix = prefix + rb[band, m]
+        return starts
+
+    def blocks(starts, extra):
+        return [block_cols(jnp.minimum(first + extra, nb - 1), B) for first in starts]
+
+    def fill_p(own, oth, at_row, starts, eq, extra):
+        for i, at in enumerate(blocks(starts, extra)):
             k, j = i // 2, i % 2
             out = oth if j else own
             x = eq[:, at]
@@ -150,8 +155,8 @@
             put_rows(put, at_row, ((x - mean) * inv_scale).astype(BF))
             out[k, step:msg, :] = tail
 
-    def fill_r(own, oth, rb, inn, extra):
-        for i, at in enumerate(blocks(rb, extra)):
+    def fill_r(own, oth, starts, inn, extra):
+        for i, at in enumerate(blocks(starts, extra)):
             out = oth if i % 2 else own
             put_rows(lambda s, v: out.__setitem__((i // 2, s), v), 0, inn[:, at].astype(BF))
 
@@ -163,12 +168,13 @@
         for copy in copies:
             copy.start()
         copies[0].wait()
+        starts = owner_starts(rb)
         copies[1].wait()
-        fill_r(own1, oth1, rb, inn, 0)
-        fill_r(own2, oth2, rb, inn, 1)
+        fill_r(own1, oth1, starts, inn, 0)
+        fill_r(own2, oth2, starts, inn, 1)
         copies[2].wait()
-        fill_p(own1, oth1, rp, rb, eq, 0)
-        fill_p(own2, oth2, rp, rb, eq, 1)
+        fill_p(own1, oth1, rp, starts, eq, 0)
+        fill_p(own2, oth2, rp, starts, eq, 1)
 
     own1, oth1, own2, oth2 = kernel_call(
         pack_body,
@@ -441,53 +447,82 @@
     )
     sol1_far = [z_send(x, k + top) for k, x in list(enumerate(sol1[chips:]))[::-1]][::-1]
     sol1_near = [
-        x if i == 0 else lax.ppermute(x, "mem", [(q, q ^ i) for q in range(n)])
+        x if i < 2 else lax.ppermute(x, "mem", [(q, q ^ i) for q in range(n)])
         for i, x in enumerate(sol1[:chips])
     ]
 
     def peer_body(*refs):
+        out = refs[-1]
         for k in range(2 * top):
-            refs[2 * top][k] = refs[k][rp:step, :]
+            out[k] = refs[k][rp:step, :]
+        out[2 * top] = refs[2 * top][0:rp, :]
+        out[2 * top + 1] = refs[2 * top][rp:step, :]
 
     (peer,) = kernel_call(
-        peer_body, [((2 * top, rp, B), BF)], [], [*sol1_far, *sol2_far], name="peer_rows", after=sol1_near[1:]
+        peer_body,
+        [((2 * top + 2, rp, B), BF)],
+        [],
+        [*sol1_far, *sol2_far, sol1_near[1]],
+        name="peer_rows",
+        after=sol1_near[2:],
     )
     peer = swap_core(peer)
 
     def unpack_body(rb, coef, inn, *refs):
         near, far1, far2 = refs[:chips], refs[chips : chips + top], refs[chips + top : 2 * chips]
-        peer, out = refs[2 * chips :]
+        peer, out, buf, sems = refs[2 * chips :]
         me, band = lax.axis_index("mem"), lax.axis_index("lat")
         inv_c = coefficients(coef)[0]
 
         def pieces(i):
             k = i // 2 - top
+            if i == 1:
+                return peer[2 * top, 0:rows, :], peer[2 * top + 1, 0:rows, :]
             if k < 0:
                 return near[i][0:rows, :], near[i][rp : rp + rows, :]
             if i % 2:
                 return peer[k, 0:rows, :], peer[top + k, 0:rows, :]
             return far1[k][0:rows, :], far2[k][0:rows, :]
 
+        waits, starts = [], owner_starts(rb)
+
+        def write(at, number, value):
+            buf[number] = inn[:, at] * inv_c + value.astype(F32)
+            copy = pltpu.make_async_copy(buf.at[number], out.at[:, at], sems.at[number])
+            copy.start()
+            return copy
+
         for i in range(n):
             owner = me ^ i
-            first = region_start(rb, band, owner)
-            at = block_cols(first, B)
-            out[:, at] = inn[:, at] * inv_c + pieces(i)[0].astype(F32)
-            second = jnp.minimum(first + 1, nb - 1)
+            first = starts[i]
+            waits.append(write(block_cols(first, B), 2 * i, pieces(i)[0]))
+            at = block_cols(jnp.minimum(first + 1, nb - 1), B)
 
             @pl.when(rb[band, owner] > 1)
-            def _(i=i, second=second):
-                at2 = block_cols(second, B)
-                out[:, at2] = inn[:, at2] * inv_c + pieces(i)[1].astype(F32)
-
-    (out,) = kernel_call(
+            def _(i=i, at=at):
+                write(at, 2 * i + 1, pieces(i)[1])
+
+        for i in range(n):
+            waits[i].wait()
+            owner = me ^ i
+            at = block_cols(jnp.minimum(starts[i] + 1, nb - 1), B)
+
+            @pl.when(rb[band, owner] > 1)
+            def _(i=i, at=at):
+                number = 2 * i + 1
+                pltpu.make_async_copy(buf.at[number], out.at[:, at], sems.at[number]).wait()
+
+    arrays = [coef, innovations, *sol1_near, *sol1_far, *sol2_far, peer]
+    return pl.pallas_call(
         unpack_body,
-        [((rows, cols), F32)],
-        [region_blocks],
-        [coef, innovations, *sol1_near, *sol1_far, *sol2_far, peer],
+        out_shape=jax.ShapeDtypeStruct((rows, cols), F32),
+        in_specs=[SMEM_SPEC] + [VMEM_SPEC] * len(arrays),
+        out_specs=HBM_SPEC,
+        scratch_shapes=[pltpu.VMEM((2 * n, rows, B), F32), pltpu.SemaphoreType.DMA((2 * n,))],
+        compiler_params=pltpu.CompilerParams(vmem_limit_bytes=VMEM_LIMIT),
+        cost_estimate=pl.CostEstimate(flops=3 * 10**9, bytes_accessed=3 * 10**7, transcendentals=0),
         name="unpack",
-    )
-    return out
+    )(region_blocks, *arrays)
 
 
 def solution(mesh):

time: 90.1 us -> 89.2 us (0.990)
    pallas_call x14 -> x13, Pallas kernels: 14.9 us -> 12.6 us  [kernel_call(): pl.pallas_call(run, out_shape=tuple((jax.ShapeDtypeStruct(s, d) for s, d...]
    pallas_call x0 -> x1, Pallas kernels: none -> 1.78 us  [on_device(): pl.pallas_call(unpack_body, out_shape=jax.ShapeDtypeStruct((rows, cols),...]
    ppermute x3 -> x2, starting transfers between devices: 1.93 us -> 1.29 us  [on_device(): lax.ppermute(x, 'mem', [(q, q ^ i) for q in range(n)])]
    ppermute x3 -> x2, waiting for transfers between devices: 4.34 us -> 4.14 us  [on_device(): lax.ppermute(x, 'mem', [(q, q ^ i) for q in range(n)])]
  transfers between devices with their start and end apart: 24 -> 23, of which waited for: 13 -> 12; matrix products, arithmetic and copies ran while one was open for 0% -> 0% of each run, Pallas kernels for 10% -> 10%
where the time goes in v4:
time: 89.2 us; the launch traced here: 88.8 us
  starting transfers between devices  37.2 us (42%)
  waiting for transfers between devices  34.5 us (39%)
  Pallas kernels  14.4 us (16%)
  between operations  1.85 us (2%)
    ppermute x6, waiting for transfers between devices, z_exchange(): got[k] = lax.ppermute(parts[k], 'mem', [(i, i ^ 2 * k) for i in range(n)])  16.6 us
    pallas_call x13, Pallas kernels, kernel_call(): pl.pallas_call(run, out_shape=tuple((jax.ShapeDtypeStruct(s, d) for s, d...  12.6 us
    ppermute x6, starting transfers between devices, z_exchange(): got[k] = lax.ppermute(parts[k], 'mem', [(i, i ^ 2 * k) for i in range(n)])  11.9 us
    ppermute x4, starting transfers between devices, z_send(): return lax.ppermute(x, 'mem', [(i, i ^ 2 * k) for i in range(n)])  9.19 us
    ppermute x2, waiting for transfers between devices, lat_exchange(): relay = lax.ppermute(high, 'lat', hop1_list)  6.48 us
    ppermute x2, starting transfers between devices, lat_exchange(): lax.ppermute(gate(relay, after) if after else relay, 'lat', hop2_list)  5.85 us
    ppermute x2, starting transfers between devices, lat_exchange(): pair = lax.ppermute(both, 'lat', pair_list)  4.3 us
    ppermute x4, waiting for transfers between devices, z_send(): return lax.ppermute(x, 'mem', [(i, i ^ 2 * k) for i in range(n)])  4.19 us
  transfers between devices with their start and end apart: 23, of which 12 were waited for; matrix products, arithmetic and copies ran while one was open for 0% of the time, Pallas kernels for 10%

profile of v4, /device:TPU:0, one launch (start us, length us, event | category | flops | bytes accessed | tf_op | source)
XLA Modules:
  0.0 88.8 jit_solution(7672992237513315163)
XLA Ops:
  0.0 0.7 copy-done.4
  0.7 2.0 %pack.1 = (bf16[4,104,512]{2,1,0:T(8,128)(2,1)S(1)}, bf16[4,104,512]{2,1,0:T(8,128)(2,1)S(1)}, bf16[4,104,512]{2,1,0:T(8,128)(2,1)S(1)}, bf16[4,104,512]{2,1,0:T(8,128)(2,1)S(1)}) custom-call(s32[4,8]{1,0:T(4,128)S(1)} %copy-done.4, f32[48,6144]{1,0:T(8,128)} %refs_1_.3, f32[48,6144]{1,0:T(8,128)} %inn.1), custom_call_target="tpu_custom_call" | custom-call | flops 3000000000 | bytes 30000000 | tf_op jit(solution)/shard_map/pack/pallas_call | solution.py:28
  2.7 0.5 collective-permute-start
  3.2 0.1 collective-permute-start.4
  4.9 0.0 copy-done.6
  4.9 0.1 copy.16.refs_2_.refs_1_
  5.0 0.1 select_select_fusion.refs_5_.refs_1_.refs_0_.coef
  5.1 0.0 collective-permute-done.refs_1_
  5.1 0.0 copy-start.5
  5.1 0.1 join_first.1
  5.2 3.1 %collective-permute-start.1 = (bf16[200,512]{1,0:T(8,128)(2,1)S(1)}, bf16[200,512]{1,0:T(8,128)(2,1)S(1)}, u32[]{:S(2)}, u32[]{:S(2)}) collective-permute-start(bf16[200,512]{1,0:T(8,128)(2,1)S(1)} %get-tuple-element.52), channel_id=1, source_target_pairs={{0,8},{4,12},{8,0},{12,4},{16,24},{20,28},{24,16},{28,20},{1,9},{5... | collective-permute-start | bytes 614408 | tf_op jit(solution)/shard_map/ppermute | solution.py:202
  8.3 2.6 %collective-permute-start.2 = (bf16[200,512]{1,0:T(8,128)(2,1)S(1)}, bf16[200,512]{1,0:T(8,128)(2,1)S(1)}, u32[]{:S(2)}, u32[]{:S(2)}) collective-permute-start(bf16[200,512]{1,0:T(8,128)(2,1)S(1)} %get-tuple-element.53), channel_id=1, source_target_pairs={{0,16},{4,20},{8,24},{12,28},{16,0},{20,4},{24,8},{28,12},{1,17},{... | collective-permute-start | bytes 614408 | tf_op jit(solution)/shard_map/ppermute | solution.py:202
  10.9 0.0 collective-permute-start.3
  10.9 0.0 collective-permute-done.4.refs_1_
  10.9 0.1 join_second.1
  10.9 6.4 %collective-permute-done.1.refs_1_ = bf16[200,512]{1,0:T(8,128)(2,1)S(1)} collective-permute-done((bf16[200,512]{1,0:T(8,128)(2,1)S(1)}, bf16[200,512]{1,0:T(8,128)(2,1)S(1)}, u32[]{:S(2)}, u32[]{:S(2)}) %collective-permute-start.1) | collective-permute-done | bytes 204832 | tf_op jit(solution)/shard_map/ppermute | solution.py:202
  17.3 8.6 %collective-permute-done.2.refs_2_ = bf16[200,512]{1,0:T(8,128)(2,1)S(1)} collective-permute-done((bf16[200,512]{1,0:T(8,128)(2,1)S(1)}, bf16[200,512]{1,0:T(8,128)(2,1)S(1)}, u32[]{:S(2)}, u32[]{:S(2)}) %collective-permute-start.2) | collective-permute-done | bytes 204832 | tf_op jit(solution)/shard_map/ppermute | solution.py:202
  25.9 0.0 collective-permute-done.3.refs_3_
  25.9 0.2 owner_first.1
  26.1 1.6 %collective-permute-start.5 = (bf16[768,512]{1,0:T(8,128)(2,1)S(1)}, bf16[768,512]{1,0:T(8,128)(2,1)S(1)}, u32[]{:S(2)}, u32[]{:S(2)}) collective-permute-start(bf16[768,512]{1,0:T(8,128)(2,1)S(1)} %get-tuple-element.58.refs_3_.refs_0_.refs_6_), channel_id=1, source_target_pairs={{0,1},{1,0},{2,3},{3,2},{4,5},{5,4},{6,7},{7,6},{8,9},{9,8},{10,11... | collective-permute-start | bytes 2359304 | tf_op jit(solution)/shard_map/ppermute | solution.py:251
  27.6 3.8 %collective-permute-start.8 = (bf16[200,512]{1,0:T(8,128)(2,1)S(1)}, bf16[200,512]{1,0:T(8,128)(2,1)S(1)}, u32[]{:S(2)}, u32[]{:S(2)}) collective-permute-start(bf16[200,512]{1,0:T(8,128)(2,1)S(1)} %get-tuple-element.67), channel_id=1, source_target_pairs={{0,8},{4,12},{8,0},{12,4},{16,24},{20,28},{24,16},{28,20},{1,9},{5... | collective-permute-start | bytes 614408 | tf_op jit(solution)/shard_map/ppermute | solution.py:202
  31.4 1.0 %collective-permute-start.10 = (bf16[200,512]{1,0:T(8,128)(2,1)S(1)}, bf16[200,512]{1,0:T(8,128)(2,1)S(1)}, u32[]{:S(2)}, u32[]{:S(2)}) collective-permute-start(bf16[200,512]{1,0:T(8,128)(2,1)S(1)} %get-tuple-element.68), channel_id=1, source_target_pairs={{0,16},{4,20},{8,24},{12,28},{16,0},{20,4},{24,8},{28,12},{1,17},{... | collective-permute-start | bytes 614408 | tf_op jit(solution)/shard_map/ppermute | solution.py:202
  32.5 1.5 %collective-permute-start.11 = (bf16[200,512]{1,0:T(8,128)(2,1)S(1)}, bf16[200,512]{1,0:T(8,128)(2,1)S(1)}, u32[]{:S(2)}, u32[]{:S(2)}) collective-permute-start(bf16[200,512]{1,0:T(8,128)(2,1)S(1)} %get-tuple-element.69), channel_id=1, source_target_pairs={{0,24},{4,28},{8,16},{12,20},{16,8},{20,12},{24,0},{28,4},{1,25},{... | collective-permute-start | bytes 614408 | tf_op jit(solution)/shard_map/ppermute | solution.py:202
  33.9 1.3 %collective-permute-start.7 = (bf16[384,512]{1,0:T(8,128)(2,1)S(1)}, bf16[384,512]{1,0:T(8,128)(2,1)S(1)}, u32[]{:S(2)}, u32[]{:S(2)}) collective-permute-start(bf16[384,512]{1,0:T(8,128)(2,1)S(1)} %get-tuple-element.66), channel_id=1, source_target_pairs={{1,3},{2,0},{5,7},{6,4},{9,11},{10,8},{13,15},{14,12},{17,19},{18,... | collective-permute-start | bytes 1179656 | tf_op jit(solution)/shard_map/ppermute | solution.py:250
  35.2 2.0 %tiles.1 = (f32[512,512]{1,0:T(8,128)S(1)}, f32[512,512]{1,0:T(8,128)S(1)}, bf16[512,512]{1,0:T(8,128)(2,1)S(1)}, bf16[512,512]{1,0:T(8,128)(2,1)S(1)}, bf16[512,384]{1,0:T(8,128)(2,1)S(1)}) custom-call(s32[4,8]{1,0:T(4,128)S(1)} %copy-done.5, s32[4,12,3]{2,1,0:T(8,128)S(1)} %copy.16.refs_2_.refs_1_, bf16[2,512,512]{2,1,0:T(8,128)(2,1)S(1)} %copy-done.1, ...), custom_call_target="tpu_custom_call" | custom-call | flops 3000000000 | bytes 30000000 | tf_op jit(solution)/shard_map/tiles/pallas_call | solution.py:28
  37.2 0.7 first_cov.1
  38.0 0.1 collective-permute-done.8.refs_1_.refs_6_
  38.1 0.7 collective-permute-start.6
  38.8 6.2 %collective-permute-done.7.refs_0_ = bf16[384,512]{1,0:T(8,128)(2,1)S(1)} collective-permute-done((bf16[384,512]{1,0:T(8,128)(2,1)S(1)}, bf16[384,512]{1,0:T(8,128)(2,1)S(1)}, u32[]{:S(2)}, u32[]{:S(2)}) %collective-permute-start.7) | collective-permute-done | bytes 393248 | tf_op jit(solution)/shard_map/ppermute | solution.py:250
  44.9 1.5 %collective-permute-start.9 = (bf16[384,512]{1,0:T(8,128)(2,1)S(1)}, bf16[384,512]{1,0:T(8,128)(2,1)S(1)}, u32[]{:S(2)}, u32[]{:S(2)}) collective-permute-start(bf16[384,512]{1,0:T(8,128)(2,1)S(1)} %gate.5), channel_id=1, source_target_pairs={{3,2},{0,1},{7,6},{4,5},{11,10},{8,9},{15,14},{12,13},{19,18},{16,... | collective-permute-start | bytes 1179656 | tf_op jit(solution)/shard_map/ppermute | solution.py:253
  46.4 0.0 collective-permute-done.5.refs_2_
  46.4 0.8 pair_cov.1
  47.2 1.5 %collective-permute-done.10.refs_7_ = bf16[200,512]{1,0:T(8,128)(2,1)S(1)} collective-permute-done((bf16[200,512]{1,0:T(8,128)(2,1)S(1)}, bf16[200,512]{1,0:T(8,128)(2,1)S(1)}, u32[]{:S(2)}, u32[]{:S(2)}) %collective-permute-start.10) | collective-permute-done | bytes 204832 | tf_op jit(solution)/shard_map/ppermute | solution.py:202
  48.7 0.0 collective-permute-done.11.refs_8_
  48.7 2.0 %east_cov.1 = (bf16[512,512]{1,0:T(8,128)(2,1)S(1)}, f32[384,512]{1,0:T(8,128)S(1)}, bf16[384,512]{1,0:T(8,128)(2,1)S(1)}, bf16[384,512]{1,0:T(8,128)(2,1)S(1)}) custom-call(s32[4,8]{1,0:T(4,128)S(1)} %copy-done.5, s32[4,12]{1,0:T(4,128)S(1)} %copy-done.3, s32[4,12,3]{2,1,0:T(8,128)S(1)} %copy.16.refs_2_.refs_1_, bf16[2,512,512]{2,1,0:T(8,128)(2,1)S(1)} %copy-done.1, ...), custom_call_target="tpu_custom_call" | custom-call | flops 3000000000 | bytes 30000000 | tf_op jit(solution)/shard_map/east_cov/pallas_call | solution.py:28
  50.7 0.0 collective-permute-done.6.refs_2_
  50.7 1.5 %collective-permute-done.9.refs_3_ = bf16[384,512]{1,0:T(8,128)(2,1)S(1)} collective-permute-done((bf16[384,512]{1,0:T(8,128)(2,1)S(1)}, bf16[384,512]{1,0:T(8,128)(2,1)S(1)}, u32[]{:S(2)}, u32[]{:S(2)}) %collective-permute-start.9) | collective-permute-done | bytes 393248 | tf_op jit(solution)/shard_map/ppermute | solution.py:253
  52.2 0.8 skew_cov.1
  53.0 1.0 %direction_first.1 = (bf16[384,512]{1,0:T(8,128)(2,1)S(1)}, bf16[192,512]{1,0:T(8,128)(2,1)S(1)}, bf16[192,512]{1,0:T(8,128)(2,1)S(1)}, f32[384,512]{1,0:T(8,128)S(1)}) custom-call(s32[4,8]{1,0:T(4,128)S(1)} %copy-done.5, f32[8,512]{1,0:T(8,128)S(1)} %select_select_fusion.refs_5_.refs_1_.refs_0_.coef, f32[1,6144]{1,0:T(1,128)S(1)} %bitcast.3, ...), custom_call_target="tpu_custom_call" | custom-call | flops 3000000000 | bytes 30000000 | tf_op jit(solution)/shard_map/direction_first/pallas_call | solution.py:28
  54.0 1.3 %collective-permute-start.14 = (bf16[192,512]{1,0:T(8,128)(2,1)S(1)}, bf16[192,512]{1,0:T(8,128)(2,1)S(1)}, u32[]{:S(2)}, u32[]{:S(2)}) collective-permute-start(bf16[192,512]{1,0:T(8,128)(2,1)S(1)} %get-tuple-element.83), channel_id=1, source_target_pairs={{1,3},{2,0},{5,7},{6,4},{9,11},{10,8},{13,15},{14,12},{17,19},{18,... | collective-permute-start | bytes 589832 | tf_op jit(solution)/shard_map/ppermute | solution.py:250
  55.3 2.7 %collective-permute-start.12 = (bf16[384,512]{1,0:T(8,128)(2,1)S(1)}, bf16[384,512]{1,0:T(8,128)(2,1)S(1)}, u32[]{:S(2)}, u32[]{:S(2)}) collective-permute-start(bf16[384,512]{1,0:T(8,128)(2,1)S(1)} %get-tuple-element.74.refs_9_), channel_id=1, source_target_pairs={{0,1},{1,0},{2,3},{3,2},{4,5},{5,4},{6,7},{7,6},{8,9},{9,8},{10,11... | collective-permute-start | bytes 1179656 | tf_op jit(solution)/shard_map/ppermute | solution.py:251
  58.0 2.5 %inner_step.1 = (f32[384,512]{1,0:T(8,128)S(1)}, bf16[192,512]{1,0:T(8,128)(2,1)S(1)}, bf16[96,512]{1,0:T(8,128)(2,1)S(1)}, bf16[96,512]{1,0:T(8,128)(2,1)S(1)}) custom-call(s32[4,8]{1,0:T(4,128)S(1)} %copy-done.5, f32[8,512]{1,0:T(8,128)S(1)} %select_select_fusion.refs_5_.refs_1_.refs_0_.coef, f32[512,512]{1,0:T(8,128)S(1)} %get-tuple-element.76.refs_2_, ...), custom_call_target="tpu_custom_call" | custom-call | flops 3000000000 | bytes 30000000 | tf_op jit(solution)/shard_map/inner_step/pallas_call | solution.py:28
  60.6 0.7 collective-permute-start.13
  61.2 0.3 collective-permute-done.14.refs_0_.refs_1_
  61.5 4.4 %collective-permute-start.15 = (bf16[192,512]{1,0:T(8,128)(2,1)S(1)}, bf16[192,512]{1,0:T(8,128)(2,1)S(1)}, u32[]{:S(2)}, u32[]{:S(2)}) collective-permute-start(bf16[192,512]{1,0:T(8,128)(2,1)S(1)} %gate.7), channel_id=1, source_target_pairs={{3,2},{0,1},{7,6},{4,5},{11,10},{8,9},{15,14},{12,13},{19,18},{16,... | collective-permute-start | bytes 589832 | tf_op jit(solution)/shard_map/ppermute | solution.py:253
  65.9 4.7 %collective-permute-start.20 = (bf16[96,512]{1,0:T(8,128)(2,1)S(1)}, bf16[96,512]{1,0:T(8,128)(2,1)S(1)}, u32[]{:S(2)}, u32[]{:S(2)}) collective-permute-start(bf16[96,512]{1,0:T(8,128)(2,1)S(1)} %gate.8), channel_id=1, source_target_pairs={{0,16},{4,20},{8,24},{12,28},{16,0},{20,4},{24,8},{28,12},{1,17},{... | collective-permute-start | bytes 294920 | tf_op jit(solution)/shard_map/ppermute | solution.py:209
  70.6 1.3 %collective-permute-start.21 = (bf16[96,512]{1,0:T(8,128)(2,1)S(1)}, bf16[96,512]{1,0:T(8,128)(2,1)S(1)}, u32[]{:S(2)}, u32[]{:S(2)}) collective-permute-start(bf16[96,512]{1,0:T(8,128)(2,1)S(1)} %gate.9), channel_id=1, source_target_pairs={{0,24},{4,28},{8,16},{12,20},{16,8},{20,12},{24,0},{28,4},{1,25},{... | collective-permute-start | bytes 294920 | tf_op jit(solution)/shard_map/ppermute | solution.py:209
  71.9 0.0 collective-permute-done.13.refs_4_
  71.9 0.0 collective-permute-done.12.refs_3_
  71.9 0.0 collective-permute-done.15.refs_5_
  72.0 0.6 outer_step.1
  72.6 1.3 %collective-permute-start.16 = (bf16[96,512]{1,0:T(8,128)(2,1)S(1)}, bf16[96,512]{1,0:T(8,128)(2,1)S(1)}, u32[]{:S(2)}, u32[]{:S(2)}) collective-permute-start(bf16[96,512]{1,0:T(8,128)(2,1)S(1)} %get-tuple-element.87), channel_id=1, source_target_pairs={{0,8},{4,12},{8,0},{12,4},{16,24},{20,28},{24,16},{28,20},{1,9},{5... | collective-permute-start | bytes 294920 | tf_op jit(solution)/shard_map/ppermute | solution.py:450
  73.9 0.0 collective-permute-start.17
  73.9 1.8 %collective-permute-start.18 = (bf16[96,512]{1,0:T(8,128)(2,1)S(1)}, bf16[96,512]{1,0:T(8,128)(2,1)S(1)}, u32[]{:S(2)}, u32[]{:S(2)}) collective-permute-start(bf16[96,512]{1,0:T(8,128)(2,1)S(1)} %get-tuple-element.89), channel_id=1, source_target_pairs={{0,16},{4,20},{8,24},{12,28},{16,0},{20,4},{24,8},{28,12},{1,17},{... | collective-permute-start | bytes 294920 | tf_op jit(solution)/shard_map/ppermute | solution.py:209
  75.7 0.0 collective-permute-done.20.refs_2_.refs_6_
  75.7 1.3 %collective-permute-start.19 = (bf16[96,512]{1,0:T(8,128)(2,1)S(1)}, bf16[96,512]{1,0:T(8,128)(2,1)S(1)}, u32[]{:S(2)}, u32[]{:S(2)}) collective-permute-start(bf16[96,512]{1,0:T(8,128)(2,1)S(1)} %get-tuple-element.90), channel_id=1, source_target_pairs={{0,24},{4,28},{8,16},{12,20},{16,8},{20,12},{24,0},{28,4},{1,25},{... | collective-permute-start | bytes 294920 | tf_op jit(solution)/shard_map/ppermute | solution.py:209
  77.0 0.5 collective-permute-done.21.refs_3_.refs_7_
  77.5 3.5 %collective-permute-done.16.refs_5_.refs_2_ = bf16[96,512]{1,0:T(8,128)(2,1)S(1)} collective-permute-done((bf16[96,512]{1,0:T(8,128)(2,1)S(1)}, bf16[96,512]{1,0:T(8,128)(2,1)S(1)}, u32[]{:S(2)}, u32[]{:S(2)}) %collective-permute-start.16) | collective-permute-done | bytes 98336 | tf_op jit(solution)/shard_map/ppermute | solution.py:450
  81.0 0.6 collective-permute-done.17.refs_6_.refs_3_
  81.6 0.0 collective-permute-done.18.refs_0_.refs_4_
  81.6 3.7 %collective-permute-done.19.refs_1_.refs_5_ = bf16[96,512]{1,0:T(8,128)(2,1)S(1)} collective-permute-done((bf16[96,512]{1,0:T(8,128)(2,1)S(1)}, bf16[96,512]{1,0:T(8,128)(2,1)S(1)}, u32[]{:S(2)}, u32[]{:S(2)}) %collective-permute-start.19) | collective-permute-done | bytes 98336 | tf_op jit(solution)/shard_map/ppermute | solution.py:209
  85.4 0.1 collective-permute-start.22
  85.5 1.6 %collective-permute-done.22.refs_8_ = bf16[6,48,512]{2,1,0:T(8,128)(2,1)S(1)} collective-permute-done((bf16[6,48,512]{2,1,0:T(8,128)(2,1)S(1)}, bf16[6,48,512]{2,1,0:T(8,128)(2,1)S(1)}, u32[]{:S(2)}, u32[]{:S(2)}) %collective-permute-start.22) | collective-permute-done | bytes 294944 | tf_op jit(solution)/shard_map/ppermute | solution.py:197
  87.0 1.8 %unpack.1 = f32[48,6144]{1,0:T(8,128)} custom-call(s32[4,8]{1,0:T(4,128)S(1)} %copy-done.5, f32[8,512]{1,0:T(8,128)S(1)} %select_select_fusion.refs_5_.refs_1_.refs_0_.coef, f32[48,6144]{1,0:T(8,128)S(1)} %copy-done, bf16[96,512]{1,0:T(8,128)(2,1)S(1)} %get-tuple-element.85.refs_0_, bf16[96,512]{1,0:T(8,128)(2,1)S(1)} %get-tuple-element.86.refs_4_.refs_1_, ...), custom_call_target="tpu_custom_call" | custom-call | flops 3000000000 | bytes 30000000 | tf_op jit(solution)/shard_map/unpack/pallas_call | solution.py:516
  (20 shorter events, 0.1 us)
Async XLA Ops:
  0.0 0.7 copy-start.4
  0.7 4.2 %copy-start.6 = (s32[4,12,3]{1,0,2:T(4,128)S(1)}, s32[4,12,3]{1,0,2:T(4,128)}, u32[]{:S(2)}) copy-start(s32[4,12,3]{1,0,2:T(4,128)} %param.15) | copy-start | bytes 1732
  2.7 2.4 %collective-permute-start = (bf16[4,104,512]{2,1,0:T(8,128)(2,1)S(1)}, bf16[4,104,512]{2,1,0:T(8,128)(2,1)S(1)}, u32[]{:S(2)}, u32[]{:S(2)}) collective-permute-start(bf16[4,104,512]{2,1,0:T(8,128)(2,1)S(1)} %get-tuple-element.50), channel_id=1, source_target_pairs={{0,4},{4,0},{8,12},{12,8},{16,20},{20,16},{24,28},{28,24},{1,5},{5... | collective-permute-start | bytes 1277960 | tf_op jit(solution)/shard_map/ppermute | solution.py:197
  3.2 7.7 %collective-permute-start.4 = (bf16[4,104,512]{2,1,0:T(8,128)(2,1)S(1)}, bf16[4,104,512]{2,1,0:T(8,128)(2,1)S(1)}, u32[]{:S(2)}, u32[]{:S(2)}) collective-permute-start(bf16[4,104,512]{2,1,0:T(8,128)(2,1)S(1)} %get-tuple-element.56), channel_id=1, source_target_pairs={{0,4},{4,0},{8,12},{12,8},{16,20},{20,16},{24,28},{28,24},{1,5},{5... | collective-permute-start | bytes 1277960 | tf_op jit(solution)/shard_map/ppermute | solution.py:197
  5.1 5.8 %copy-start.3 = (s32[4,12]{1,0:T(4,128)S(1)}, s32[4,12]{1,0:T(4,128)}, u32[]{:S(2)}) copy-start(s32[4,12]{1,0:T(4,128)} %refs_1_.4) | copy-start | bytes 580
  5.1 5.7 %copy-start.5 = (s32[4,8]{1,0:T(4,128)S(1)}, s32[4,8]{1,0:T(4,128)}, u32[]{:S(2)}) copy-start(s32[4,8]{1,0:T(4,128)} %rb.1) | copy-start | bytes 388
  5.2 12.1 %collective-permute-start.1 = (bf16[200,512]{1,0:T(8,128)(2,1)S(1)}, bf16[200,512]{1,0:T(8,128)(2,1)S(1)}, u32[]{:S(2)}, u32[]{:S(2)}) collective-permute-start(bf16[200,512]{1,0:T(8,128)(2,1)S(1)} %get-tuple-element.52), channel_id=1, source_target_pairs={{0,8},{4,12},{8,0},{12,4},{16,24},{20,28},{24,16},{28,20},{1,9},{5... | collective-permute-start | bytes 614408 | tf_op jit(solution)/shard_map/ppermute | solution.py:202
  8.3 17.6 %collective-permute-start.2 = (bf16[200,512]{1,0:T(8,128)(2,1)S(1)}, bf16[200,512]{1,0:T(8,128)(2,1)S(1)}, u32[]{:S(2)}, u32[]{:S(2)}) collective-permute-start(bf16[200,512]{1,0:T(8,128)(2,1)S(1)} %get-tuple-element.53), channel_id=1, source_target_pairs={{0,16},{4,20},{8,24},{12,28},{16,0},{20,4},{24,8},{28,12},{1,17},{... | collective-permute-start | bytes 614408 | tf_op jit(solution)/shard_map/ppermute | solution.py:202
  10.9 15.1 %collective-permute-start.3 = (bf16[200,512]{1,0:T(8,128)(2,1)S(1)}, bf16[200,512]{1,0:T(8,128)(2,1)S(1)}, u32[]{:S(2)}, u32[]{:S(2)}) collective-permute-start(bf16[200,512]{1,0:T(8,128)(2,1)S(1)} %get-tuple-element.54), channel_id=1, source_target_pairs={{0,24},{4,28},{8,16},{12,20},{16,8},{20,12},{24,0},{28,4},{1,25},{... | collective-permute-start | bytes 614408 | tf_op jit(solution)/shard_map/ppermute | solution.py:202
  25.9 9.3 %copy-start.1 = (bf16[2,512,512]{2,1,0:T(8,128)(2,1)S(1)}, bf16[2,512,512]{2,1,0:T(8,128)(2,1)}, u32[]{:S(2)}) copy-start(bf16[2,512,512]{2,1,0:T(8,128)(2,1)} %refs_3_.3) | copy-start | bytes 3145732
  26.1 20.4 %collective-permute-start.5 = (bf16[768,512]{1,0:T(8,128)(2,1)S(1)}, bf16[768,512]{1,0:T(8,128)(2,1)S(1)}, u32[]{:S(2)}, u32[]{:S(2)}) collective-permute-start(bf16[768,512]{1,0:T(8,128)(2,1)S(1)} %get-tuple-element.58.refs_3_.refs_0_.refs_6_), channel_id=1, source_target_pairs={{0,1},{1,0},{2,3},{3,2},{4,5},{5,4},{6,7},{7,6},{8,9},{9,8},{10,11... | collective-permute-start | bytes 2359304 | tf_op jit(solution)/shard_map/ppermute | solution.py:251
  27.6 10.4 %collective-permute-start.8 = (bf16[200,512]{1,0:T(8,128)(2,1)S(1)}, bf16[200,512]{1,0:T(8,128)(2,1)S(1)}, u32[]{:S(2)}, u32[]{:S(2)}) collective-permute-start(bf16[200,512]{1,0:T(8,128)(2,1)S(1)} %get-tuple-element.67), channel_id=1, source_target_pairs={{0,8},{4,12},{8,0},{12,4},{16,24},{20,28},{24,16},{28,20},{1,9},{5... | collective-permute-start | bytes 614408 | tf_op jit(solution)/shard_map/ppermute | solution.py:202
  31.4 17.3 %collective-permute-start.10 = (bf16[200,512]{1,0:T(8,128)(2,1)S(1)}, bf16[200,512]{1,0:T(8,128)(2,1)S(1)}, u32[]{:S(2)}, u32[]{:S(2)}) collective-permute-start(bf16[200,512]{1,0:T(8,128)(2,1)S(1)} %get-tuple-element.68), channel_id=1, source_target_pairs={{0,16},{4,20},{8,24},{12,28},{16,0},{20,4},{24,8},{28,12},{1,17},{... | collective-permute-start | bytes 614408 | tf_op jit(solution)/shard_map/ppermute | solution.py:202
  32.5 16.3 %collective-permute-start.11 = (bf16[200,512]{1,0:T(8,128)(2,1)S(1)}, bf16[200,512]{1,0:T(8,128)(2,1)S(1)}, u32[]{:S(2)}, u32[]{:S(2)}) collective-permute-start(bf16[200,512]{1,0:T(8,128)(2,1)S(1)} %get-tuple-element.69), channel_id=1, source_target_pairs={{0,24},{4,28},{8,16},{12,20},{16,8},{20,12},{24,0},{28,4},{1,25},{... | collective-permute-start | bytes 614408 | tf_op jit(solution)/shard_map/ppermute | solution.py:202
  33.9 11.0 %collective-permute-start.7 = (bf16[384,512]{1,0:T(8,128)(2,1)S(1)}, bf16[384,512]{1,0:T(8,128)(2,1)S(1)}, u32[]{:S(2)}, u32[]{:S(2)}) collective-permute-start(bf16[384,512]{1,0:T(8,128)(2,1)S(1)} %get-tuple-element.66), channel_id=1, source_target_pairs={{1,3},{2,0},{5,7},{6,4},{9,11},{10,8},{13,15},{14,12},{17,19},{18,... | collective-permute-start | bytes 1179656 | tf_op jit(solution)/shard_map/ppermute | solution.py:250
  38.1 12.7 %collective-permute-start.6 = (bf16[384,512]{1,0:T(8,128)(2,1)S(1)}, bf16[384,512]{1,0:T(8,128)(2,1)S(1)}, u32[]{:S(2)}, u32[]{:S(2)}) collective-permute-start(bf16[384,512]{1,0:T(8,128)(2,1)S(1)} %get-tuple-element.65), channel_id=1, source_target_pairs={{1,2},{2,1},{5,6},{6,5},{9,10},{10,9},{13,14},{14,13},{17,18},{18,... | collective-permute-start | bytes 1179656 | tf_op jit(solution)/shard_map/ppermute | solution.py:252
  44.9 7.3 %collective-permute-start.9 = (bf16[384,512]{1,0:T(8,128)(2,1)S(1)}, bf16[384,512]{1,0:T(8,128)(2,1)S(1)}, u32[]{:S(2)}, u32[]{:S(2)}) collective-permute-start(bf16[384,512]{1,0:T(8,128)(2,1)S(1)} %gate.5), channel_id=1, source_target_pairs={{3,2},{0,1},{7,6},{4,5},{11,10},{8,9},{15,14},{12,13},{19,18},{16,... | collective-permute-start | bytes 1179656 | tf_op jit(solution)/shard_map/ppermute | solution.py:253
  52.2 0.8 copy-start.2
  54.0 7.6 %collective-permute-start.14 = (bf16[192,512]{1,0:T(8,128)(2,1)S(1)}, bf16[192,512]{1,0:T(8,128)(2,1)S(1)}, u32[]{:S(2)}, u32[]{:S(2)}) collective-permute-start(bf16[192,512]{1,0:T(8,128)(2,1)S(1)} %get-tuple-element.83), channel_id=1, source_target_pairs={{1,3},{2,0},{5,7},{6,4},{9,11},{10,8},{13,15},{14,12},{17,19},{18,... | collective-permute-start | bytes 589832 | tf_op jit(solution)/shard_map/ppermute | solution.py:250
  55.3 16.7 %collective-permute-start.12 = (bf16[384,512]{1,0:T(8,128)(2,1)S(1)}, bf16[384,512]{1,0:T(8,128)(2,1)S(1)}, u32[]{:S(2)}, u32[]{:S(2)}) collective-permute-start(bf16[384,512]{1,0:T(8,128)(2,1)S(1)} %get-tuple-element.74.refs_9_), channel_id=1, source_target_pairs={{0,1},{1,0},{2,3},{3,2},{4,5},{5,4},{6,7},{7,6},{8,9},{9,8},{10,11... | collective-permute-start | bytes 1179656 | tf_op jit(solution)/shard_map/ppermute | solution.py:251
  60.6 11.4 %collective-permute-start.13 = (bf16[192,512]{1,0:T(8,128)(2,1)S(1)}, bf16[192,512]{1,0:T(8,128)(2,1)S(1)}, u32[]{:S(2)}, u32[]{:S(2)}) collective-permute-start(bf16[192,512]{1,0:T(8,128)(2,1)S(1)} %gate.6), channel_id=1, source_target_pairs={{1,2},{2,1},{5,6},{6,5},{9,10},{10,9},{13,14},{14,13},{17,18},{18,... | collective-permute-start | bytes 589832 | tf_op jit(solution)/shard_map/ppermute | solution.py:252
  61.5 10.4 %collective-permute-start.15 = (bf16[192,512]{1,0:T(8,128)(2,1)S(1)}, bf16[192,512]{1,0:T(8,128)(2,1)S(1)}, u32[]{:S(2)}, u32[]{:S(2)}) collective-permute-start(bf16[192,512]{1,0:T(8,128)(2,1)S(1)} %gate.7), channel_id=1, source_target_pairs={{3,2},{0,1},{7,6},{4,5},{11,10},{8,9},{15,14},{12,13},{19,18},{16,... | collective-permute-start | bytes 589832 | tf_op jit(solution)/shard_map/ppermute | solution.py:253
  65.9 9.8 %collective-permute-start.20 = (bf16[96,512]{1,0:T(8,128)(2,1)S(1)}, bf16[96,512]{1,0:T(8,128)(2,1)S(1)}, u32[]{:S(2)}, u32[]{:S(2)}) collective-permute-start(bf16[96,512]{1,0:T(8,128)(2,1)S(1)} %gate.8), channel_id=1, source_target_pairs={{0,16},{4,20},{8,24},{12,28},{16,0},{20,4},{24,8},{28,12},{1,17},{... | collective-permute-start | bytes 294920 | tf_op jit(solution)/shard_map/ppermute | solution.py:209
  70.6 6.9 %collective-permute-start.21 = (bf16[96,512]{1,0:T(8,128)(2,1)S(1)}, bf16[96,512]{1,0:T(8,128)(2,1)S(1)}, u32[]{:S(2)}, u32[]{:S(2)}) collective-permute-start(bf16[96,512]{1,0:T(8,128)(2,1)S(1)} %gate.9), channel_id=1, source_target_pairs={{0,24},{4,28},{8,16},{12,20},{16,8},{20,12},{24,0},{28,4},{1,25},{... | collective-permute-start | bytes 294920 | tf_op jit(solution)/shard_map/ppermute | solution.py:209
  72.6 8.5 %collective-permute-start.16 = (bf16[96,512]{1,0:T(8,128)(2,1)S(1)}, bf16[96,512]{1,0:T(8,128)(2,1)S(1)}, u32[]{:S(2)}, u32[]{:S(2)}) collective-permute-start(bf16[96,512]{1,0:T(8,128)(2,1)S(1)} %get-tuple-element.87), channel_id=1, source_target_pairs={{0,8},{4,12},{8,0},{12,4},{16,24},{20,28},{24,16},{28,20},{1,9},{5... | collective-permute-start | bytes 294920 | tf_op jit(solution)/shard_map/ppermute | solution.py:450
  73.9 7.8 %collective-permute-start.17 = (bf16[96,512]{1,0:T(8,128)(2,1)S(1)}, bf16[96,512]{1,0:T(8,128)(2,1)S(1)}, u32[]{:S(2)}, u32[]{:S(2)}) collective-permute-start(bf16[96,512]{1,0:T(8,128)(2,1)S(1)} %get-tuple-element.88), channel_id=1, source_target_pairs={{0,12},{4,8},{8,4},{12,0},{16,28},{20,24},{24,20},{28,16},{1,13},{... | collective-permute-start | bytes 294920 | tf_op jit(solution)/shard_map/ppermute | solution.py:450
  73.9 7.8 %collective-permute-start.18 = (bf16[96,512]{1,0:T(8,128)(2,1)S(1)}, bf16[96,512]{1,0:T(8,128)(2,1)S(1)}, u32[]{:S(2)}, u32[]{:S(2)}) collective-permute-start(bf16[96,512]{1,0:T(8,128)(2,1)S(1)} %get-tuple-element.89), channel_id=1, source_target_pairs={{0,16},{4,20},{8,24},{12,28},{16,0},{20,4},{24,8},{28,12},{1,17},{... | collective-permute-start | bytes 294920 | tf_op jit(solution)/shard_map/ppermute | solution.py:209
  75.7 9.7 %collective-permute-start.19 = (bf16[96,512]{1,0:T(8,128)(2,1)S(1)}, bf16[96,512]{1,0:T(8,128)(2,1)S(1)}, u32[]{:S(2)}, u32[]{:S(2)}) collective-permute-start(bf16[96,512]{1,0:T(8,128)(2,1)S(1)} %get-tuple-element.90), channel_id=1, source_target_pairs={{0,24},{4,28},{8,16},{12,20},{16,8},{20,12},{24,0},{28,4},{1,25},{... | collective-permute-start | bytes 294920 | tf_op jit(solution)/shard_map/ppermute | solution.py:209
  85.3 1.7 %copy-start = (f32[48,6144]{1,0:T(8,128)S(1)}, f32[48,6144]{1,0:T(8,128)}, u32[]{:S(2)}) copy-start(f32[48,6144]{1,0:T(8,128)} %inn.1) | copy-start | bytes 3538948
  85.4 1.6 %collective-permute-start.22 = (bf16[6,48,512]{2,1,0:T(8,128)(2,1)S(1)}, bf16[6,48,512]{2,1,0:T(8,128)(2,1)S(1)}, u32[]{:S(2)}, u32[]{:S(2)}) collective-permute-start(bf16[6,48,512]{2,1,0:T(8,128)(2,1)S(1)} %peer_rows.1), channel_id=1, source_target_pairs={{0,4},{4,0},{8,12},{12,8},{16,20},{20,16},{24,28},{28,24},{1,5},{5... | collective-permute-start | bytes 884744 | tf_op jit(solution)/shard_map/ppermute | solution.py:197
